TPU v7x, 32 devices: a whole 2x2x4 slice. The times are simulated.
32 devices in a mesh: batch: 8 (over z, x), row: 4 (over y, core).
Axes of the slice: x: 2, y: 2, z: 4, core: 2. Of those that a mesh axis runs over, the one named last changes fastest.
Arguments:
- inputs: bfloat16 [576, 16, 16, 256], P('batch', 'row'), may hold values from -6 to 6
- partners: int32 [576], P('batch'), may hold values from 0 to 575, as said below
- boxes: int32 [576, 4], P('batch'), may hold values from 0 to 16, as said below
- drops: int32 [576, 2], P('batch'), may hold values 0 or 1
- norm1_gain: bfloat16 [256], replicated, may hold values from 0.5 to 1.5
- norm1_bias: bfloat16 [256], replicated, may hold values from -3 to 3
- qkv_weight: bfloat16 [256, 768], replicated, may hold values from -0.5 to 0.5
- lepe_weight: bfloat16 [3, 3, 256], replicated, may hold values from -1.5 to 1.5
- lepe_bias: bfloat16 [256], replicated, may hold values from -3 to 3
- proj_weight: bfloat16 [256, 256], replicated, may hold values from -0.5 to 0.5
- proj_bias: bfloat16 [256], replicated, may hold values from -3 to 3
- norm2_gain: bfloat16 [256], replicated, may hold values from 0.5 to 1.5
- norm2_bias: bfloat16 [256], replicated, may hold values from -3 to 3
- fc1_weight: bfloat16 [256, 1024], replicated, may hold values from -0.375 to 0.375
- fc1_bias: bfloat16 [1024], replicated, may hold values from -3 to 3
- fc2_weight: bfloat16 [1024, 256], replicated, may hold values from -0.1875 to 0.1875
- fc2_bias: bfloat16 [256], replicated, may hold values from -3 to 3
- cotangent: bfloat16 [576, 16, 16, 256], P('batch', 'row'), may hold values from -6 to 6
Outputs:
- block_out: bfloat16 [576, 16, 16, 256], P('batch', 'row')
- input_grad: bfloat16 [576, 16, 16, 256], P('batch', 'row')
- gain1_grad: float32 [256], replicated
- bias1_grad: float32 [256], replicated
- qkv_grad: float32 [256, 768], replicated
- conv_grad: float32 [3, 3, 256], replicated
- convbias_grad: float32 [256], replicated
- proj_grad: float32 [256, 256], replicated
- projbias_grad: float32 [256], replicated
- gain2_grad: float32 [256], replicated
- bias2_grad: float32 [256], replicated
- fc1_grad: float32 [256, 1024], replicated
- fc1bias_grad: float32 [1024], replicated
- fc2_grad: float32 [1024, 256], replicated
- fc2bias_grad: float32 [256], replicated
Inputs may be any that keep to these rules, and one draw needn't show every extreme that they name: Within each aligned block of 72 images the partners are a permutation of that block's image indices. `boxes`: each row holds first row < end row and first column < end column; every box covers grid row and column 8.
All inputs are finite; a program needn't handle non-finite values. No bound on the sum of `drops` on one device may be relied on, other than what follows from the above.
Results may differ from a plain program's by a relative error of at most 0.013.
Values may be sent and summed in bfloat16 or wider, within the bound.
A program may use at most 320 MiB of HBM per device.

v0:
```python
import jax
import jax.numpy as jnp
from jax import lax
from jax.sharding import PartitionSpec as P

HEADS = 8
STRIPE = 2


eps = 1e-05
mix_own = 0.7
mix_other = 0.3
keep_scale = 1.25


def extended(block, sides, width):
    for axis, dim in sides:
        count = lax.axis_size(axis)
        forward = [(i, i + 1) for i in range(count - 1)]
        backward = [(target, source) for source, target in forward]
        low = lax.ppermute(
            lax.slice_in_dim(block, block.shape[dim] - width, None, axis=dim), axis, forward
        )
        high = lax.ppermute(lax.slice_in_dim(block, 0, width, axis=dim), axis, backward)
        block = jnp.concatenate([low, block, high], axis=dim)
    return block


def layer_norm(value, gain, bias):
    center = value - jnp.mean(value, axis=-1, keepdims=True)
    spread = jnp.mean(center * center, axis=-1, keepdims=True)
    return center * lax.rsqrt(spread + eps) * gain + bias


def exact_gelu(value):
    return jax.nn.gelu(value, approximate=False)


def row_windows(value, head_count):
    count, height, breadth, channels = value.shape
    return value.reshape(
        count, height // STRIPE, STRIPE * breadth, head_count, channels // head_count
    )


def row_layout(value):
    count, stripes, length, head_count, head_size = value.shape
    return value.reshape(count, stripes * STRIPE, length // STRIPE, head_count * head_size)


def col_windows(value, head_count):
    count, height, breadth, channels = value.shape
    shaped = value.reshape(
        count, height, breadth // STRIPE, STRIPE, head_count, channels // head_count
    )
    return shaped.transpose(0, 2, 1, 3, 4, 5).reshape(
        count, breadth // STRIPE, height * STRIPE, head_count, channels // head_count
    )


def col_layout(value):
    count, stripes, length, head_count, head_size = value.shape
    shaped = value.reshape(count, stripes, length // STRIPE, STRIPE, head_count * head_size)
    return shaped.transpose(0, 2, 1, 3, 4).reshape(
        count, length // STRIPE, stripes * STRIPE, head_count * head_size
    )


def attend(queries, key_part, values):
    score_scale = queries.shape[-1] ** (-0.5)
    scores = (
        jnp.einsum("...qhe,...khe->...hqk", queries, key_part, preferred_element_type=jnp.float32)
        * score_scale
    )
    log_total = jax.nn.logsumexp(scores, axis=-1, keepdims=True)
    probs = jnp.exp(scores - log_total).astype(jnp.bfloat16)
    context = jnp.einsum("...hqk,...khe->...qhe", probs, values, preferred_element_type=jnp.float32)
    return (context, log_total)


def attend_back(queries, key_part, values, log_total, d_context):
    score_scale = queries.shape[-1] ** (-0.5)
    scores = (
        jnp.einsum("...qhe,...khe->...hqk", queries, key_part, preferred_element_type=jnp.float32)
        * score_scale
    )
    probs = jnp.exp(scores - log_total)
    low_probs = probs.astype(jnp.bfloat16)
    d_values = jnp.einsum(
        "...hqk,...qhe->...khe", low_probs, d_context, preferred_element_type=jnp.float32
    )
    d_probs = jnp.einsum(
        "...qhe,...khe->...hqk", d_context, values, preferred_element_type=jnp.float32
    )
    d_scores = (probs * (d_probs - jnp.sum(probs * d_probs, axis=-1, keepdims=True))).astype(
        jnp.bfloat16
    )
    d_queries = (
        jnp.einsum("...hqk,...khe->...qhe", d_scores, key_part, preferred_element_type=jnp.float32)
        * score_scale
    )
    d_keys = (
        jnp.einsum("...hqk,...qhe->...khe", d_scores, queries, preferred_element_type=jnp.float32)
        * score_scale
    )
    return (d_queries, d_keys, d_values)


def stripe_mask(row_ids, col_ids, down_step, side_step, by_rows):
    if by_rows:
        same = (row_ids + down_step) // STRIPE == row_ids // STRIPE
        return jnp.broadcast_to(same[:, None], (row_ids.shape[0], col_ids.shape[0]))
    same = (col_ids + side_step) // STRIPE == col_ids // STRIPE
    return jnp.broadcast_to(same[None, :], (row_ids.shape[0], col_ids.shape[0]))


def stencil(padded, taps, row_ids, col_ids, by_rows):
    height = row_ids.shape[0]
    breadth = col_ids.shape[0]
    total = jnp.zeros((padded.shape[0], height, breadth, padded.shape[3]), jnp.float32)
    for down_step in (-1, 0, 1):
        for side_step in (-1, 0, 1):
            window = padded[
                :,
                1 + down_step : 1 + down_step + height,
                1 + side_step : 1 + side_step + breadth,
                :,
            ].astype(jnp.float32)
            allowed = stripe_mask(row_ids, col_ids, down_step, side_step, by_rows)
            total = (
                total
                + jnp.where(allowed[None, :, :, None], window, 0.0)
                * taps[down_step + 1, side_step + 1]
            )
    return total


def stencil_back(padded_grad, taps, row_rim, col_rim, by_rows):
    height = row_rim.shape[0] - 2
    breadth = col_rim.shape[0] - 2
    grad_float = padded_grad.astype(jnp.float32)
    total = jnp.zeros((padded_grad.shape[0], height, breadth, padded_grad.shape[3]), jnp.float32)
    for down_step in (-1, 0, 1):
        for side_step in (-1, 0, 1):
            allowed = stripe_mask(row_rim, col_rim, down_step, side_step, by_rows)
            masked = jnp.where(allowed[None, :, :, None], grad_float, 0.0)
            total = (
                total
                + masked[
                    :,
                    1 - down_step : 1 - down_step + height,
                    1 - side_step : 1 - side_step + breadth,
                    :,
                ]
                * taps[down_step + 1, side_step + 1]
            )
    return total


def stencil_weight(padded, grad, row_ids, col_ids, by_rows):
    height = row_ids.shape[0]
    breadth = col_ids.shape[0]
    grad_float = grad.astype(jnp.float32)
    pieces = []
    for down_step in (-1, 0, 1):
        for side_step in (-1, 0, 1):
            window = padded[
                :,
                1 + down_step : 1 + down_step + height,
                1 + side_step : 1 + side_step + breadth,
                :,
            ].astype(jnp.float32)
            allowed = stripe_mask(row_ids, col_ids, down_step, side_step, by_rows)
            pieces.append(
                jnp.sum(
                    jnp.where(allowed[None, :, :, None], window, 0.0) * grad_float, axis=(0, 1, 2)
                )
            )
    return jnp.stack(pieces).reshape(3, 3, grad.shape[-1])


def pad_both(value):
    return jnp.pad(value, ((0, 0), (1, 1), (1, 1), (0, 0)))


def pad_cols(value):
    return jnp.pad(value, ((0, 0), (0, 0), (1, 1), (0, 0)))


def per_device(
    inputs,
    partners,
    boxes,
    drops,
    norm1_gain,
    norm1_bias,
    qkv_weight,
    lepe_weight,
    lepe_bias,
    proj_weight,
    proj_bias,
    norm2_gain,
    norm2_bias,
    fc1_weight,
    fc1_bias,
    fc2_weight,
    fc2_bias,
    cotangent,
):
    image_count, row_count, side_len, model_width = inputs.shape
    half_width = model_width // 2
    half_heads = HEADS // 2
    row_start = lax.axis_index("row") * row_count
    row_ids = row_start + jnp.arange(row_count)
    col_ids = jnp.arange(side_len)
    row_rim = row_start - 1 + jnp.arange(row_count + 2)
    col_rim = jnp.arange(side_len + 2) - 1
    local_partner = partners - lax.axis_index("batch") * image_count
    source = inputs.astype(jnp.float32)
    partner_rows = source[local_partner]
    inside = (
        (row_ids[None, :, None] >= boxes[:, 0, None, None])
        & (row_ids[None, :, None] < boxes[:, 1, None, None])
        & (col_ids[None, None, :] >= boxes[:, 2, None, None])
        & (col_ids[None, None, :] < boxes[:, 3, None, None])
    )[..., None]
    mixed = jnp.where(inside, partner_rows, mix_own * source + mix_other * partner_rows)
    keep_rates = drops.astype(jnp.float32) * keep_scale
    keep_first = keep_rates[:, 0, None, None, None]
    keep_second = keep_rates[:, 1, None, None, None]
    gain_one = norm1_gain.astype(jnp.float32)
    shift_one = norm1_bias.astype(jnp.float32)
    conv_taps = lepe_weight.astype(jnp.float32)
    conv_shift = lepe_bias.astype(jnp.float32)
    proj_shift = proj_bias.astype(jnp.float32)
    gain_two = norm2_gain.astype(jnp.float32)
    shift_two = norm2_bias.astype(jnp.float32)
    fc1_shift = fc1_bias.astype(jnp.float32)
    fc2_shift = fc2_bias.astype(jnp.float32)
    normed1, pull_one = jax.vjp(layer_norm, mixed, gain_one, shift_one)
    normed_first = normed1.astype(jnp.bfloat16)
    qkv = jnp.dot(normed_first, qkv_weight, preferred_element_type=jnp.float32).astype(jnp.bfloat16)
    flat_q = qkv[..., :half_width]
    flat_k = qkv[..., model_width : model_width + half_width]
    flat_v = qkv[..., 2 * model_width : 2 * model_width + half_width]
    tall_v = qkv[..., 2 * model_width + half_width :]
    vertical = jnp.concatenate(
        [
            qkv[..., half_width:model_width],
            qkv[..., model_width + half_width : 2 * model_width],
            tall_v,
        ],
        axis=-1,
    )
    flat_ctx, flat_lse = attend(
        row_windows(flat_q, half_heads),
        row_windows(flat_k, half_heads),
        row_windows(flat_v, half_heads),
    )
    flat_lepe = (
        stencil(pad_both(flat_v), conv_taps[..., :half_width], row_ids, col_ids, True)
        + conv_shift[:half_width]
    )
    flat_out = (row_layout(flat_ctx) + flat_lepe).astype(jnp.bfloat16)
    gathered = lax.all_to_all(vertical, "row", split_axis=2, concat_axis=1, tiled=True)
    queries = col_windows(gathered[..., :half_width], half_heads)
    key_part = col_windows(gathered[..., half_width : 2 * half_width], half_heads)
    values = col_windows(gathered[..., 2 * half_width :], half_heads)
    context, log_total = attend(queries, key_part, values)
    context = col_layout(context)
    tall_rows = lax.all_to_all(
        context.astype(jnp.bfloat16), "row", split_axis=1, concat_axis=2, tiled=True
    ).astype(context.dtype)
    rim_values = pad_cols(extended(tall_v, (("row", 1),), 1))
    tall_lepe = (
        stencil(rim_values, conv_taps[..., half_width:], row_ids, col_ids, False)
        + conv_shift[half_width:]
    )
    tall_out = (tall_rows + tall_lepe).astype(jnp.bfloat16)
    attended = jnp.concatenate([flat_out, tall_out], axis=-1)
    branch1 = jnp.dot(attended, proj_weight, preferred_element_type=jnp.float32) + proj_shift
    hidden1 = mixed + keep_first * branch1
    normed2, pull_two = jax.vjp(layer_norm, hidden1, gain_two, shift_two)
    normed_second = normed2.astype(jnp.bfloat16)
    pre = jnp.dot(normed_second, fc1_weight, preferred_element_type=jnp.float32) + fc1_shift
    act_float, gelu_pull = jax.vjp(exact_gelu, pre)
    act = act_float.astype(jnp.bfloat16)
    branch2 = jnp.dot(act, fc2_weight, preferred_element_type=jnp.float32) + fc2_shift
    block_out = (hidden1 + keep_second * branch2).astype(jnp.bfloat16)
    grad_out = cotangent.astype(jnp.float32)
    d_branch2 = (keep_second * grad_out).astype(jnp.bfloat16)
    fc2_grad = jnp.einsum("irsf,irsd->fd", act, d_branch2, preferred_element_type=jnp.float32)
    fc2bias_grad = jnp.sum(d_branch2.astype(jnp.float32), axis=(0, 1, 2))
    d_act = jnp.einsum("irsd,fd->irsf", d_branch2, fc2_weight, preferred_element_type=jnp.float32)
    d_pre = gelu_pull(d_act)[0].astype(jnp.bfloat16)
    fc1_grad = jnp.einsum("irsd,irsf->df", normed_second, d_pre, preferred_element_type=jnp.float32)
    fc1bias_grad = jnp.sum(d_pre.astype(jnp.float32), axis=(0, 1, 2))
    d_normed2 = jnp.einsum("irsf,df->irsd", d_pre, fc1_weight, preferred_element_type=jnp.float32)
    hidden_part, gain2_grad, bias2_grad = pull_two(d_normed2)
    d_hidden1 = grad_out + hidden_part
    d_branch1 = (keep_first * d_hidden1).astype(jnp.bfloat16)
    proj_grad = jnp.einsum("irsd,irse->de", attended, d_branch1, preferred_element_type=jnp.float32)
    projbias_grad = jnp.sum(d_branch1.astype(jnp.float32), axis=(0, 1, 2))
    d_attended = jnp.einsum(
        "irse,de->irsd", d_branch1, proj_weight, preferred_element_type=jnp.float32
    ).astype(jnp.bfloat16)
    flat_grad = d_attended[..., :half_width]
    tall_grad = d_attended[..., half_width:]
    flat_dq, flat_dk, flat_dv = attend_back(
        row_windows(flat_q, half_heads),
        row_windows(flat_k, half_heads),
        row_windows(flat_v, half_heads),
        flat_lse,
        row_windows(flat_grad, half_heads),
    )
    flat_dv = row_layout(flat_dv) + stencil_back(
        pad_both(flat_grad), conv_taps[..., :half_width], row_rim, col_rim, True
    )
    flat_taps = stencil_weight(pad_both(flat_v), flat_grad, row_ids, col_ids, True)
    flat_shift = jnp.sum(flat_grad.astype(jnp.float32), axis=(0, 1, 2))
    grad_cols = lax.all_to_all(tall_grad, "row", split_axis=2, concat_axis=1, tiled=True)
    tall_dq, tall_dk, tall_dv = attend_back(
        col_windows(gathered[..., :half_width], half_heads),
        col_windows(gathered[..., half_width : 2 * half_width], half_heads),
        col_windows(gathered[..., 2 * half_width :], half_heads),
        log_total,
        col_windows(grad_cols, half_heads),
    )
    tall_dq = col_layout(tall_dq)
    tall_dk = col_layout(tall_dk)
    tall_dv = col_layout(tall_dv)
    back_cols = jnp.concatenate([tall_dq, tall_dk, tall_dv], axis=-1)
    back_rows = lax.all_to_all(
        back_cols.astype(jnp.bfloat16), "row", split_axis=1, concat_axis=2, tiled=True
    ).astype(back_cols.dtype)
    rim_grad = pad_cols(extended(tall_grad, (("row", 1),), 1))
    lepe_part = stencil_back(rim_grad, conv_taps[..., half_width:], row_rim, col_rim, False)
    tall_back = jnp.concatenate(
        [back_rows[..., : 2 * half_width], back_rows[..., 2 * half_width :] + lepe_part], axis=-1
    ).astype(jnp.bfloat16)
    tall_taps = stencil_weight(rim_values, tall_grad, row_ids, col_ids, False)
    tall_shift = jnp.sum(tall_grad.astype(jnp.float32), axis=(0, 1, 2))
    conv_grad = jnp.concatenate([flat_taps, tall_taps], axis=-1)
    convbias_grad = jnp.concatenate([flat_shift, tall_shift], axis=-1)
    d_qkv = jnp.concatenate(
        [
            row_layout(flat_dq).astype(jnp.bfloat16),
            tall_back[..., :half_width],
            row_layout(flat_dk).astype(jnp.bfloat16),
            tall_back[..., half_width : 2 * half_width],
            flat_dv.astype(jnp.bfloat16),
            tall_back[..., 2 * half_width :],
        ],
        axis=-1,
    )
    qkv_grad = jnp.einsum("irsd,irsc->dc", normed_first, d_qkv, preferred_element_type=jnp.float32)
    d_normed1 = jnp.einsum("irsc,dc->irsd", d_qkv, qkv_weight, preferred_element_type=jnp.float32)
    mixed_part, gain1_grad, bias1_grad = pull_one(d_normed1)
    d_mixed = d_hidden1 + mixed_part
    (
        gain1_grad,
        bias1_grad,
        qkv_grad,
        conv_grad,
        convbias_grad,
        proj_grad,
        projbias_grad,
        gain2_grad,
        bias2_grad,
        fc1_grad,
        fc1bias_grad,
        fc2_grad,
        fc2bias_grad,
    ) = lax.psum(
        (
            gain1_grad,
            bias1_grad,
            qkv_grad,
            conv_grad,
            convbias_grad,
            proj_grad,
            projbias_grad,
            gain2_grad,
            bias2_grad,
            fc1_grad,
            fc1bias_grad,
            fc2_grad,
            fc2bias_grad,
        ),
        ("batch", "row"),
    )
    own_part = mix_own * jnp.where(inside, 0.0, d_mixed)
    toward = jnp.where(inside, d_mixed, mix_other * d_mixed)
    image_ids = jnp.arange(image_count)
    hits = local_partner[:, None] == image_ids[None, :]
    inverse = jnp.sum(jnp.where(hits, image_ids[:, None], 0), axis=0)
    input_grad = (own_part + toward[inverse]).astype(jnp.bfloat16)
    return (
        block_out,
        input_grad,
        gain1_grad,
        bias1_grad,
        qkv_grad,
        conv_grad,
        convbias_grad,
        proj_grad,
        projbias_grad,
        gain2_grad,
        bias2_grad,
        fc1_grad,
        fc1bias_grad,
        fc2_grad,
        fc2bias_grad,
    )


def solution(mesh):
    placed = (
        P("batch", "row", None, None),
        P("batch"),
        P("batch", None),
        P("batch", None),
        P(),
        P(),
        P(),
        P(),
        P(),
        P(),
        P(),
        P(),
        P(),
        P(),
        P(),
        P(),
        P(),
        P("batch", "row", None, None),
    )
    return jax.shard_map(
        per_device,
        mesh=mesh,
        in_specs=placed,
        out_specs=(
            P("batch", "row", None, None),
            P("batch", "row", None, None),
            P(),
            P(),
            P(),
            P(),
            P(),
            P(),
            P(),
            P(),
            P(),
            P(),
            P(),
            P(),
            P(),
        ),
        check_vma=False,
    )
```

profile of v0, /device:TPU:0, one launch (start us, length us, event | category | flops | bytes accessed | tf_op | source)
XLA Modules:
  0.0 820.7 jit_solution(756323321251286888)
XLA Ops:
  14.2 5.5 gather_fusion
  54.4 10.3 %copy.352 = bf16[72,2,32,4,32]{2,4,3,1,0:T(8,128)(2,1)} copy(bf16[72,2,32,4,32]{0,4,3,2,1:T(8,128)(2,1)} %bitcast.247) | data formatting | bytes 2359296 | tf_op jit(solution)/shard_map/reshape | solution.py:41
  67.2 10.2 %copy.378 = bf16[72,2,32,4,32]{2,4,3,1,0:T(8,128)(2,1)} copy(bf16[72,2,32,4,32]{0,4,3,2,1:T(8,128)(2,1)} %bitcast.248) | data formatting | bytes 2359296 | tf_op jit(solution)/shard_map/reshape | solution.py:41
  77.5 9.7 %multiply_reduce_fusion.3 = (f32[72,2,4,32]{3,2,1,0:T(4,128)S(1)}, f32[72,2,4,32,32]{3,4,2,1,0:T(8,128)}) fusion(bf16[72,2,32,4,32]{2,4,3,1,0:T(8,128)(2,1)} %copy.378, bf16[72,2,32,4,32]{2,4,3,1,0:T(8,128)(2,1)} %copy.352), kind=kOutput, calls=%fused_computation.37 | convolution fusion | flops 38909952 | bytes 4792320 | tf_op jit(solution)/shard_map/...qhe,...khe->...hqk/dot_general | solution.py:72
  89.9 9.4 %copy.351 = bf16[72,2,32,4,32]{4,2,3,1,0:T(8,128)(2,1)} copy(bf16[72,2,32,4,32]{0,4,3,2,1:T(8,128)(2,1)} %bitcast.260) | data formatting | bytes 2359296 | tf_op jit(solution)/shard_map/reshape | solution.py:41
  99.2 6.6 exponential_reduce_fusion.1
  106.0 7.3 convolution_bitcast_fusion.1
  113.3 10.7 %copy.331 = f32[72,2,32,4,32]{0,4,3,2,1:T(8,128)} copy(f32[72,2,32,4,32]{2,4,3,1,0:T(8,128)} %convolution_bitcast_fusion.1) | data formatting | bytes 4718592 | tf_op jit(solution)/shard_map/...hqk,...khe->...qhe/transpose | solution.py:77
  129.9 6.4 fusion.26
  144.1 8.4 %copy.339 = bf16[72,2,16,2,4,32]{5,3,2,4,1,0:T(2,128)(2,1)} copy(bf16[72,2,16,2,4,32]{0,5,4,3,1,2:T(8,128)(2,1)S(1)} %bitcast.249) | data formatting | bytes 2359296 | tf_op jit(solution)/shard_map/transpose | solution.py:56
  155.4 8.3 %copy.341 = bf16[72,2,16,2,4,32]{5,3,2,4,1,0:T(2,128)(2,1)} copy(bf16[72,2,16,2,4,32]{0,5,4,3,1,2:T(8,128)(2,1)S(1)} %bitcast.250) | data formatting | bytes 2359296 | tf_op jit(solution)/shard_map/transpose | solution.py:56
  163.7 6.5 multiply_reduce_fusion.2
  178.5 9.5 %copy.360 = bf16[72,2,32,4,32]{4,2,3,1,0:T(8,128)(2,1)} copy(bf16[72,2,32,4,32]{0,4,3,2,1:T(8,128)(2,1)} %bitcast.252) | data formatting | bytes 2359296 | tf_op jit(solution)/shard_map/reshape | solution.py:56
  188.1 9.7 %convert_bitcast_fusion.1 = bf16[72,2,32,4,32]{2,4,3,1,0:T(8,128)(2,1)} fusion(bf16[72,2,32,4,32]{4,2,3,1,0:T(8,128)(2,1)} %copy.360, f32[72,2,4,32,32]{3,4,2,1,0:T(8,128)} %copy-done.2, f32[72,2,4,32]{3,2,1,0:T(4,128)S(1)} %log_add_fusion), kind=kOutput, calls=%fused_computation.96 | convolution fusion | flops 40108032 | bytes 4792320 | tf_op jit(solution)/shard_map/...hqk,...khe->...qhe/dot_general | solution.py:77
  197.8 8.9 %copy.344 = bf16[72,2,32,4,32]{0,4,3,2,1:T(8,128)(2,1)S(1)} copy(bf16[72,2,32,4,32]{2,4,3,1,0:T(8,128)(2,1)} %convert_bitcast_fusion.1) | data formatting | bytes 2359296 | tf_op jit(solution)/shard_map/convert_element_type | solution.py:272
  220.5 13.0 %all-to-all-done.1 = bf16[72,16,4,128]{3,2,0,1:T(4,128)(2,1)} async-done(((bf16[72,16,4,128]{3,2,0,1:T(4,128)(2,1)}), bf16[72,16,4,128]{3,2,0,1:T(4,128)(2,1)}, u32[]{:S(2)}, u32[]{:S(2)}) %all-to-all-start.1) | async-done | bytes 1179680 | tf_op jit(solution)/shard_map/all_to_all | solution.py:271
  244.1 9.3 %fusion.15 = (u8[72,16,1024]{2,1,0:T(8,128)(4,1)}, u8[72,16,1024]{2,1,0:T(8,128)(4,1)}, f32[72,4,16,1024]{3,2,1,0:T(8,128)S(1)}) fusion(f32[1024]{0:T(1024)S(1)} %convert_element_type.291, bf16[256,1024]{1,0:T(8,128)(2,1)S(1)} %copy-done, f32[72,4,16,256]{3,2,1,0:T(8,128)S(1)} %get-tuple-element.134, f32[256]{0:T(256)S(1)} %convert_element_type.289, ...), kind=kOutput, calls=%fused_computation.101 | convolution fusion | flops 2485518336 | bytes 26519552 | tf_op jit(solution)/shard_map/dot_general | solution.py:285
  253.4 47.1 %multiply_convert_fusion = (bf16[72,4,16,1024]{3,2,1,0:T(8,128)(2,1)}, f32[72,4,16,1024]{3,2,1,0:T(8,128)}) fusion(f32[72,4,16,1024]{3,2,1,0:T(8,128)S(1)} %get-tuple-element.135, f32[1024]{0:T(1024)S(1)} %convert_element_type.291, u8[72,16,1024]{2,1,0:T(8,128)(4,1)} %get-tuple-element.16, u8[72,16,1024]{2,1,0:T(8,128)(4,1)} %get-tuple-element.15), kind=kLoop, calls=%fused_computation.11 | loop fusion | flops 335020032 | bytes 49549312 | tf_op jit(solution)/shard_map/convert_element_type | solution.py:287
  300.6 20.7 %convert_reduce_fusion = (f32[1024]{0:T(1024)}, bf16[72,4,16,1024]{3,2,1,0:T(8,128)(2,1)}) fusion(f32[72,4,16,1024]{3,2,1,0:T(8,128)} %get-tuple-element.76, bf16[1024,256]{1,0:T(8,128)(2,1)S(1)} %copy-done.106, bf16[72,4,16,256]{3,2,1,0:T(8,128)(2,1)} %param.35, f32[72]{0:T(128)S(1)} %get-tuple-element.125, f32[72,4,16,1024]{3,2,1,0:T(8,128)} %copy-done.17, ...), kind=kOutput, calls=%fused_computation.9 | convolution fusion | flops 2499673088 | bytes 50077984 | tf_op jit(solution)/shard_map/irsd,fd->irsf/dot_general | solution.py:294
  321.3 10.0 %convolution_bitcast_fusion.3 = f32[256,1024]{1,0:T(8,128)} fusion(bf16[72,4,16,1024]{3,2,1,0:T(8,128)(2,1)} %get-tuple-element.143, f32[72,4,16,256]{3,2,1,0:T(8,128)} %copy-done.9, f32[256]{0:T(256)S(1)} %convert_element_type.289, f32[256]{0:T(256)S(1)} %convert_element_type.288, f32[72,4,16]{2,1,0:T(4,128)S(1)} %fusion.97, ...), kind=kOutput, calls=%fused_computation.216 | convolution fusion | flops 2421817344 | bytes 15243264 | tf_op jit(solution)/shard_map/irsd,irsf->df/dot_general | solution.py:296
  348.1 10.3 %copy.382 = bf16[72,2,32,4,32]{2,4,3,1,0:T(8,128)(2,1)} copy(bf16[72,2,32,4,32]{0,4,3,2,1:T(8,128)(2,1)} %bitcast.261) | data formatting | bytes 2359296 | tf_op jit(solution)/shard_map/reshape | solution.py:41
  358.4 13.0 %multiply_reduce_fusion.1 = (f32[72,2,4,32]{3,2,1,0:T(4,128)S(1)}, f32[72,2,4,32,32]{3,4,2,1,0:T(8,128)}) fusion(f32[72,2,4,32,32]{3,4,2,1,0:T(8,128)} %get-tuple-element.132, f32[72,2,4,32]{3,2,1,0:T(4,128)S(1)} %log_add_fusion.1, bf16[72,2,32,4,32]{4,2,3,1,0:T(8,128)(2,1)} %copy.351, bf16[72,2,32,4,32]{2,4,3,1,0:T(8,128)(2,1)} %copy.382), kind=kOutput, calls=%fused_computation.31 | convolution fusion | flops 40089600 | bytes 7225344 | tf_op jit(solution)/shard_map/...qhe,...khe->...hqk/dot_general | solution.py:92
  371.4 8.1 multiply_convert_fusion.6
  379.6 8.7 %fusion.10 = bf16[72,2,32,4,32]{4,2,3,1,0:T(8,128)(2,1)} fusion(bf16[72,2,32,4,32]{2,4,3,1,0:T(8,128)(2,1)} %copy.352, bf16[72,2,4,32,32]{3,4,2,1,0:T(8,128)(2,1)} %multiply_convert_fusion.6), kind=kOutput, calls=%fused_computation.78 | convolution fusion | flops 38928384 | bytes 3538944 | tf_op jit(solution)/shard_map/...hqk,...khe->...qhe/dot_general | solution.py:99
  388.3 7.2 fusion.13
  408.8 8.4 %copy.355 = bf16[72,2,32,4,32]{0,4,3,2,1:T(8,128)(2,1)} copy(bf16[72,2,32,4,32]{4,2,3,1,0:T(8,128)(2,1)} %fusion.10) | data formatting | bytes 2359296 | tf_op jit(solution)/shard_map/convert_element_type | solution.py:347
  421.4 8.3 %convolution_bitcast_fusion.2 = f32[1024,256]{1,0:T(8,128)} fusion(bf16[72,4,16,1024]{3,2,1,0:T(8,128)(2,1)} %get-tuple-element.75, bf16[72,4,16,256]{3,2,1,0:T(8,128)(2,1)} %param.35, f32[72]{0:T(128)S(1)} %get-tuple-element.125), kind=kOutput, calls=%fused_computation.215 | convolution fusion | flops 2419458048 | bytes 12845344 | tf_op jit(solution)/shard_map/irsf,irsd->fd/dot_general | solution.py:292
  429.7 9.2 %add_convert_fusion.2 = bf16[72,4,16,256]{3,2,1,0:T(8,128)(2,1)} fusion(f32[72,4,16,256]{3,2,1,0:T(8,128)} %copy-done.9, f32[256]{0:T(256)S(1)} %copy-done.114, f32[72]{0:T(128)S(1)} %get-tuple-element.125, bf16[72,4,16,1024]{3,2,1,0:T(8,128)(2,1)} %get-tuple-element.75, bf16[1024,256]{1,0:T(8,128)(2,1)S(1)} %copy-done.107), kind=kOutput, calls=%fused_computation.92 | convolution fusion | flops 2420637696 | bytes 17040672 | tf_op jit(solution)/shard_map/dot_general | solution.py:288
  450.5 11.3 %convolution_bitcast_fusion = f32[72,2,32,4,32]{2,4,3,1,0:T(8,128)} fusion(bf16[72,2,32,4,32]{2,4,3,1,0:T(8,128)(2,1)} %copy.382, f32[72,2,4,32,32]{3,4,2,1,0:T(8,128)} %get-tuple-element.132, f32[72,2,4,32]{3,2,1,0:T(4,128)S(1)} %log_add_fusion.1), kind=kOutput, calls=%fused_computation.104 | convolution fusion | flops 39518208 | bytes 5971968 | tf_op jit(solution)/shard_map/...hqk,...qhe->...khe/dot_general | solution.py:89
  467.1 8.5 %copy.359 = bf16[72,2,16,2,4,32]{5,3,2,4,1,0:T(2,128)(2,1)} copy(bf16[72,2,16,2,4,32]{0,5,4,3,1,2:T(8,128)(2,1)S(1)} %bitcast.255) | data formatting | bytes 2359296 | tf_op jit(solution)/shard_map/transpose | solution.py:56
  475.7 13.0 %multiply_reduce_fusion = (f32[72,2,4,32]{3,2,1,0:T(4,128)S(1)}, f32[72,2,4,32,32]{3,4,2,1,0:T(8,128)}) fusion(f32[72,2,4,32,32]{3,4,2,1,0:T(8,128)} %copy-done.2, f32[72,2,4,32]{3,2,1,0:T(4,128)S(1)} %copy-done.33, bf16[72,2,32,4,32]{4,2,3,1,0:T(8,128)(2,1)} %bitcast.233, bf16[72,2,32,4,32]{4,2,3,1,0:T(8,128)(2,1)} %copy.360), kind=kOutput, calls=%fused_computation.28 | convolution fusion | flops 40089600 | bytes 7225344 | tf_op jit(solution)/shard_map/...qhe,...khe->...hqk/dot_general | solution.py:92
  488.7 8.0 multiply_convert_fusion.4
  501.8 5.9 fusion.12
  507.7 10.0 %convert_bitcast_fusion = bf16[72,2,32,4,32]{2,4,3,1,0:T(8,128)(2,1)} fusion(bf16[72,2,32,4,32]{4,2,3,1,0:T(8,128)(2,1)} %bitcast.234, f32[72,2,4,32,32]{3,4,2,1,0:T(8,128)} %copy-done.2, f32[72,2,4,32]{3,2,1,0:T(4,128)S(1)} %copy-done.33), kind=kOutput, calls=%fused_computation.89 | convolution fusion | flops 40108032 | bytes 4792320 | tf_op jit(solution)/shard_map/...hqk,...qhe->...khe/dot_general | solution.py:89
  517.7 7.5 copy.364
  527.6 7.5 copy.369
  537.5 9.1 %copy.373 = bf16[72,2,32,4,32]{0,4,3,2,1:T(8,128)(2,1)S(1)} copy(bf16[72,2,32,4,32]{2,4,3,1,0:T(8,128)(2,1)} %convert_bitcast_fusion) | data formatting | bytes 2359296 | tf_op jit(solution)/shard_map/...hqk,...qhe->...khe/transpose | solution.py:89
  562.5 10.7 %copy.384 = f32[72,2,32,4,32]{0,4,3,2,1:T(8,128)} copy(f32[72,2,32,4,32]{2,4,3,1,0:T(8,128)} %convolution_bitcast_fusion) | data formatting | bytes 4718592 | tf_op jit(solution)/shard_map/...hqk,...qhe->...khe/transpose | solution.py:89
  578.0 8.5 %copy.381 = bf16[72,2,32,4,32]{0,4,3,2,1:T(8,128)(2,1)} copy(bf16[72,2,32,4,32]{4,2,3,1,0:T(8,128)(2,1)} %fusion.13) | data formatting | bytes 2359296 | tf_op jit(solution)/shard_map/convert_element_type | solution.py:349
  597.8 5.6 broadcast_select_fusion.1
  609.7 6.7 convert_element_type.307
  624.8 13.2 %fusion.77 = bf16[72,4,16,768]{3,2,1,0:T(8,128)(2,1)} fusion(bf16[72,4,16,768]{3,2,1,0:T(8,128)(2,1)} %slice_dynamic-update-slice_fusion, f32[72,4,16,128]{3,2,1,0:T(8,128)S(1)} %copy-done.28, f32[72,6,18,128]{3,2,1,0:T(8,128)} %get-tuple-element.102, f32[72,6,18,128]{3,2,1,0:T(8,128)} %pad_convert_fusion, f32[72,6,18,128]{3,2,1,0:T(8,128)} %get-tuple-element.101, ...), kind=kLoop, calls=%fused_computation.218 | loop fusion | flops 11206656 | bytes 24777216
  644.3 7.0 convolution_bitcast_fusion.4
  651.3 6.7 fusion.118
  658.2 6.1 multiply_reduce_fusion.5
  664.4 10.1 %multiply_select_fusion = (f32[72,4,16,256]{3,2,1,0:T(8,128)}, f32[72,4,16,256]{3,2,1,0:T(8,128)}, f32[256]{0:T(256)S(1)}) fusion(pred[72,4,16]{2,1,0:T(4,128)(4,1)S(1)} %copy-done.47, f32[72,4,16]{2,1,0:T(4,128)S(1)} %negate_multiply_fusion.1, f32[72,4,16]{2,1,0:T(4,128)S(1)} %multiply_multiply_fusion.5, f32[72,4,16,256]{3,2,1,0:T(8,128)} %copy-done.3, ...), kind=kLoop, calls=%fused_computation.60 | loop fusion | flops 20053760 | bytes 26051360 | tf_op jit(solution)/shard_map/jit(_where)/select_n | solution.py:393
  680.1 43.0 %all-reduce.4 = (f32[256]{0:T(256)}, f32[256]{0:T(256)}, f32[3,3,256]{2,1,0:T(4,128)}, f32[256]{0:T(256)}, f32[256]{0:T(256)}, /*index=5*/f32[256]{0:T(256)}, f32[256]{0:T(256)}, f32[1024]{0:T(1024)}, f32[256]{0:T(256)}) all-reduce(f32[256]{0:T(256)S(1)} %get-tuple-element.17, ...), channel_id=1, replica_groups=mesh['batch'=8,'row'=4] {'batch','row'}, use_global_device_ids=true, to_apply=%region_16.17 | all-reduce | flops 5120 | bytes 40960 | tf_op jit(solution)/shard_map/psum | solution.py:374
  728.4 77.9 %all-reduce.8.cloned.1.call-done = (f32[256,768]{1,0:T(8,128)}, f32[256,256]{1,0:T(8,128)}, f32[256,1024]{1,0:T(8,128)}, f32[1024,256]{1,0:T(8,128)}) async-done(((f32[256,768]{1,0:T(8,128)}, f32[256,256]{1,0:T(8,128)}, f32[256,1024]{1,0:T(8,128)}, f32[1024,256]{1,0:T(8,128)}), (f32[256,768]{1,0:T(8,128)}, f32[256,256]{1,0:T(8,128)}, f32[256,1024]{1,0:T(8,128)}, ...) | async-done | bytes 3145744 | tf_op jit(solution)/shard_map/psum | solution.py:374
  (392 shorter events, 227.3 us)
Async XLA Ops:
  7.2 237.0 %copy-start = (bf16[256,1024]{1,0:T(8,128)(2,1)S(1)}, bf16[256,1024]{1,0:T(8,128)(2,1)}, u32[]{:S(2)}) copy-start(bf16[256,1024]{1,0:T(8,128)(2,1)} %param.31) | copy-start | bytes 1572868
  34.2 95.7 %copy-start.18 = (bf16[72,4,16,128]{3,2,1,0:T(8,128)(2,1)}, bf16[72,4,16,128]{3,2,1,0:T(8,128)(2,1)S(1)}, u32[]{:S(2)}) copy-start(bf16[72,4,16,128]{3,2,1,0:T(8,128)(2,1)S(1)} %get-tuple-element.86) | copy-start | bytes 3538948
  38.9 97.4 %all-to-all-start = ((bf16[72,4,16,384]{3,1,0,2:T(4,128)(2,1)}), bf16[72,4,16,384]{3,1,0,2:T(4,128)(2,1)}, u32[]{:S(2)}, u32[]{:S(2)}) async-start(bf16[72,4,16,384]{3,1,0,2:T(4,128)(2,1)} %copy.333), calls=%async_computation | async-start | bytes 7077888 | tf_op jit(solution)/shard_map/all_to_all | solution.py:265
  45.7 172.2 %collective-permute-start = (bf16[72,1,16,128]{3,2,1,0:T(8,128)(2,1)}, bf16[72,1,16,128]{3,2,1,0:T(8,128)(2,1)}, u32[]{:S(2)}, u32[]{:S(2)}) collective-permute-start(bf16[72,1,16,128]{3,2,1,0:T(8,128)(2,1)} %get-tuple-element.87), channel_id=1, source_target_pairs={{0,1},{1,2},{2,3},{4,5},{5,6},{6,7},{8,9},{9,10},{10,11},{12,13},{... | collective-permute-start | bytes 884744 | tf_op jit(solution)/shard_map/ppermute | solution.py:21
  48.7 169.1 %collective-permute-start.1 = (bf16[72,1,16,128]{3,2,1,0:T(8,128)(2,1)}, bf16[72,1,16,128]{3,2,1,0:T(8,128)(2,1)}, u32[]{:S(2)}, u32[]{:S(2)}) collective-permute-start(bf16[72,1,16,128]{3,2,1,0:T(8,128)(2,1)} %get-tuple-element.88), channel_id=1, source_target_pairs={{1,0},{2,1},{3,2},{5,4},{6,5},{7,6},{9,8},{10,9},{11,10},{13,12},{... | collective-permute-start | bytes 884744 | tf_op jit(solution)/shard_map/ppermute | solution.py:24
  129.8 106.0 %copy-start.55 = (f32[128]{0:T(128)}, f32[128]{0:T(128)S(1)}, u32[]{:S(2)}) copy-start(f32[128]{0:T(128)S(1)} %get-tuple-element.104) | copy-start | bytes 1540
  129.8 106.0 %copy-start.57 = (f32[128]{0:T(128)}, f32[128]{0:T(128)S(1)}, u32[]{:S(2)}) copy-start(f32[128]{0:T(128)S(1)} %get-tuple-element.105) | copy-start | bytes 1540
  129.8 106.0 %copy-start.59 = (f32[128]{0:T(128)}, f32[128]{0:T(128)S(1)}, u32[]{:S(2)}) copy-start(f32[128]{0:T(128)S(1)} %get-tuple-element.106) | copy-start | bytes 1540
  129.9 106.0 %copy-start.61 = (f32[128]{0:T(128)}, f32[128]{0:T(128)S(1)}, u32[]{:S(2)}) copy-start(f32[128]{0:T(128)S(1)} %get-tuple-element.107) | copy-start | bytes 1540
  129.9 106.0 %copy-start.63 = (f32[128]{0:T(128)}, f32[128]{0:T(128)S(1)}, u32[]{:S(2)}) copy-start(f32[128]{0:T(128)S(1)} %get-tuple-element.108) | copy-start | bytes 1540
  129.9 106.0 %copy-start.65 = (f32[128]{0:T(128)}, f32[128]{0:T(128)S(1)}, u32[]{:S(2)}) copy-start(f32[128]{0:T(128)S(1)} %get-tuple-element.109) | copy-start | bytes 1540
  129.9 106.0 %copy-start.67 = (f32[128]{0:T(128)}, f32[128]{0:T(128)S(1)}, u32[]{:S(2)}) copy-start(f32[128]{0:T(128)S(1)} %get-tuple-element.110) | copy-start | bytes 1540
  129.9 106.0 %copy-start.69 = (f32[128]{0:T(128)}, f32[128]{0:T(128)S(1)}, u32[]{:S(2)}) copy-start(f32[128]{0:T(128)S(1)} %get-tuple-element.111) | copy-start | bytes 1540
  129.9 106.0 %copy-start.71 = (f32[128]{0:T(128)}, f32[128]{0:T(128)S(1)}, u32[]{:S(2)}) copy-start(f32[128]{0:T(128)S(1)} %get-tuple-element.112) | copy-start | bytes 1540
  173.9 14.2 %copy-start.32 = (f32[72,2,4,32]{3,2,1,0:T(4,128)}, f32[72,2,4,32]{3,2,1,0:T(4,128)S(1)}, u32[]{:S(2)}) copy-start(f32[72,2,4,32]{3,2,1,0:T(4,128)S(1)} %log_add_fusion) | copy-start | bytes 221188
  211.8 21.7 %all-to-all-start.1 = ((bf16[72,16,4,128]{3,2,0,1:T(4,128)(2,1)}), bf16[72,16,4,128]{3,2,0,1:T(4,128)(2,1)}, u32[]{:S(2)}, u32[]{:S(2)}) async-start(bf16[72,16,4,128]{3,2,0,1:T(4,128)(2,1)} %copy.346), calls=%async_computation.1 | async-start | bytes 2359296 | tf_op jit(solution)/shard_map/all_to_all | solution.py:271
  220.5 15.4 %copy-start.4 = (bf16[72,6,18,128]{3,2,1,0:T(8,128)(2,1)}, bf16[72,6,18,128]{3,2,1,0:T(8,128)(2,1)S(1)}, u32[]{:S(2)}) copy-start(bf16[72,6,18,128]{3,2,1,0:T(8,128)(2,1)S(1)} %select_maximum_fusion.2) | copy-start | bytes 5971972
  242.3 11.1 %copy-start.9 = (f32[72,4,16,256]{3,2,1,0:T(8,128)}, f32[72,4,16,256]{3,2,1,0:T(8,128)S(1)}, u32[]{:S(2)}) copy-start(f32[72,4,16,256]{3,2,1,0:T(8,128)S(1)} %get-tuple-element.134) | copy-start | bytes 14155780
  253.4 47.2 %copy-start.17 = (f32[72,4,16,1024]{3,2,1,0:T(8,128)}, f32[72,4,16,1024]{3,2,1,0:T(8,128)S(1)}, u32[]{:S(2)}) copy-start(f32[72,4,16,1024]{3,2,1,0:T(8,128)S(1)} %get-tuple-element.135) | copy-start | bytes 56623108
  253.4 47.2 %copy-start.106 = (bf16[1024,256]{1,0:T(8,128)(2,1)S(1)}, bf16[1024,256]{1,0:T(8,128)(2,1)}, u32[]{:S(2)}) copy-start(bf16[1024,256]{1,0:T(8,128)(2,1)} %param.33) | copy-start | bytes 1572868
  348.1 23.3 %slice-start = ((s8[9437184]{0:T(1024)(128)(4,1)}), s8[1048576]{0:T(1024)(128)(4,1)S(1)}, s32[]{:S(2)}) async-start(s8[9437184]{0:T(1024)(128)(4,1)} %bitcast.223), calls=%async_computation.5 | async-start | bytes 2097152
  358.4 13.0 %slice-start.1 = ((s8[9437184]{0:T(1024)(128)(4,1)}), s8[4194304]{0:T(1024)(128)(4,1)S(1)}, s32[]{:S(2)}) async-start(s8[9437184]{0:T(1024)(128)(4,1)} %bitcast.223), calls=%async_computation.6 | async-start | bytes 8388608
  358.4 13.0 %slice-start.2 = ((s8[9437184]{0:T(1024)(128)(4,1)}), s8[4194304]{0:T(1024)(128)(4,1)S(1)}, s32[]{:S(2)}) async-start(s8[9437184]{0:T(1024)(128)(4,1)} %bitcast.223), calls=%async_computation.7 | async-start | bytes 8388608
  400.1 193.7 %collective-permute-start.2 = (bf16[72,1,16,128]{3,2,1,0:T(8,128)(2,1)}, bf16[72,1,16,128]{3,2,1,0:T(8,128)(2,1)S(1)}, u32[]{:S(2)}, u32[]{:S(2)}) collective-permute-start(bf16[72,1,16,128]{3,2,1,0:T(8,128)(2,1)} %get-tuple-element.95), channel_id=1, source_target_pairs={{0,1},{1,2},{2,3},{4,5},{5,6},{6,7},{8,9},{9,10},{10,11},{12,13},{... | collective-permute-start | bytes 884744 | tf_op jit(solution)/shard_map/ppermute | solution.py:21
  401.4 192.4 %collective-permute-start.3 = (bf16[72,1,16,128]{3,2,1,0:T(8,128)(2,1)}, bf16[72,1,16,128]{3,2,1,0:T(8,128)(2,1)}, u32[]{:S(2)}, u32[]{:S(2)}) collective-permute-start(bf16[72,1,16,128]{3,2,1,0:T(8,128)(2,1)} %get-tuple-element.96), channel_id=1, source_target_pairs={{1,0},{2,1},{3,2},{5,4},{6,5},{7,6},{9,8},{10,9},{11,10},{13,12},{... | collective-permute-start | bytes 884744 | tf_op jit(solution)/shard_map/ppermute | solution.py:24
  404.2 57.7 %all-to-all-start.2 = ((bf16[72,4,16,128]{3,1,0,2:T(4,128)(2,1)}), bf16[72,4,16,128]{3,1,0,2:T(4,128)(2,1)}, u32[]{:S(2)}, u32[]{:S(2)}) async-start(bf16[72,4,16,128]{3,1,0,2:T(4,128)(2,1)} %copy.356), calls=%async_computation.2 | async-start | bytes 2359296 | tf_op jit(solution)/shard_map/all_to_all | solution.py:321
  464.2 11.4 %copy-start.33 = (f32[72,2,4,32]{3,2,1,0:T(4,128)S(1)}, f32[72,2,4,32]{3,2,1,0:T(4,128)}, u32[]{:S(2)}) copy-start(f32[72,2,4,32]{3,2,1,0:T(4,128)} %copy-done.32) | copy-start | bytes 221188
  554.4 49.1 %all-to-all-start.3 = ((bf16[72,16,4,384]{3,2,0,1:T(4,128)(2,1)}), bf16[72,16,4,384]{3,2,0,1:T(4,128)(2,1)}, u32[]{:S(2)}, u32[]{:S(2)}) async-start(bf16[72,16,4,384]{3,2,0,1:T(4,128)(2,1)} %copy.375), calls=%async_computation.3 | async-start | bytes 7077888 | tf_op jit(solution)/shard_map/all_to_all | solution.py:333
  559.2 247.1 %all-reduce.8.cloned.1.call-start = ((), (), s32[]{:S(2)}) async-start(), calls=%async_computation.4 | async-start | bytes 6291456 | tf_op jit(solution)/shard_map/psum | solution.py:374
  578.0 12.7 %copy-start.22 = (bf16[72,4,16,128]{3,2,1,0:T(8,128)(2,1)S(1)}, bf16[72,4,16,128]{3,2,1,0:T(8,128)(2,1)}, u32[]{:S(2)}) copy-start(bf16[72,4,16,128]{3,2,1,0:T(8,128)(2,1)} %copy-done.20) | copy-start | bytes 3538948
  616.5 27.8 %slice-start.5 = ((s8[4718592]{0:T(1024)(128)(4,1)}), s8[4194304]{0:T(1024)(128)(4,1)S(1)}, s32[]{:S(2)}) async-start(s8[4718592]{0:T(1024)(128)(4,1)} %bitcast.227), calls=%async_computation.10 | async-start | bytes 8388608
  624.5 13.4 %slice-start.7 = ((s8[5308416]{0:T(1024)(128)(4,1)}), s8[4194304]{0:T(1024)(128)(4,1)S(1)}, s32[]{:S(2)}) async-start(s8[5308416]{0:T(1024)(128)(4,1)} %bitcast.235), calls=%async_computation.12 | async-start | bytes 8388608
  624.5 13.4 %slice-start.9 = ((s8[5308416]{0:T(1024)(128)(4,1)}), s8[4194304]{0:T(1024)(128)(4,1)S(1)}, s32[]{:S(2)}) async-start(s8[5308416]{0:T(1024)(128)(4,1)} %bitcast.237), calls=%async_computation.14 | async-start | bytes 8388608
  624.5 13.4 %slice-start.11 = ((s8[5308416]{0:T(1024)(128)(4,1)}), s8[4194304]{0:T(1024)(128)(4,1)S(1)}, s32[]{:S(2)}) async-start(s8[5308416]{0:T(1024)(128)(4,1)} %bitcast.239), calls=%async_computation.16 | async-start | bytes 8388608
  624.6 13.3 %slice-start.8 = ((s8[5308416]{0:T(1024)(128)(4,1)}), s8[1114112]{0:T(1024)(128)(4,1)S(1)}, s32[]{:S(2)}) async-start(s8[5308416]{0:T(1024)(128)(4,1)} %bitcast.235), calls=%async_computation.13 | async-start | bytes 2228224
  624.6 13.8 %slice-start.10 = ((s8[5308416]{0:T(1024)(128)(4,1)}), s8[1114112]{0:T(1024)(128)(4,1)S(1)}, s32[]{:S(2)}) async-start(s8[5308416]{0:T(1024)(128)(4,1)} %bitcast.237), calls=%async_computation.15 | async-start | bytes 2228224
  624.6 14.1 %slice-start.12 = ((s8[5308416]{0:T(1024)(128)(4,1)}), s8[1114112]{0:T(1024)(128)(4,1)S(1)}, s32[]{:S(2)}) async-start(s8[5308416]{0:T(1024)(128)(4,1)} %bitcast.239), calls=%async_computation.17 | async-start | bytes 2228224
  624.7 14.1 %copy-start.56 = (f32[128]{0:T(128)S(1)}, f32[128]{0:T(128)}, u32[]{:S(2)}) copy-start(f32[128]{0:T(128)} %copy-done.55) | copy-start | bytes 1540
  624.7 14.1 %copy-start.58 = (f32[128]{0:T(128)S(1)}, f32[128]{0:T(128)}, u32[]{:S(2)}) copy-start(f32[128]{0:T(128)} %copy-done.57) | copy-start | bytes 1540
  624.7 14.1 %copy-start.60 = (f32[128]{0:T(128)S(1)}, f32[128]{0:T(128)}, u32[]{:S(2)}) copy-start(f32[128]{0:T(128)} %copy-done.59) | copy-start | bytes 1540
  624.7 14.1 %copy-start.62 = (f32[128]{0:T(128)S(1)}, f32[128]{0:T(128)}, u32[]{:S(2)}) copy-start(f32[128]{0:T(128)} %copy-done.61) | copy-start | bytes 1540
  624.7 14.1 %copy-start.64 = (f32[128]{0:T(128)S(1)}, f32[128]{0:T(128)}, u32[]{:S(2)}) copy-start(f32[128]{0:T(128)} %copy-done.63) | copy-start | bytes 1540
  624.7 14.1 %copy-start.66 = (f32[128]{0:T(128)S(1)}, f32[128]{0:T(128)}, u32[]{:S(2)}) copy-start(f32[128]{0:T(128)} %copy-done.65) | copy-start | bytes 1540
  624.7 14.1 %copy-start.68 = (f32[128]{0:T(128)S(1)}, f32[128]{0:T(128)}, u32[]{:S(2)}) copy-start(f32[128]{0:T(128)} %copy-done.67) | copy-start | bytes 1540
  624.7 14.1 %copy-start.70 = (f32[128]{0:T(128)S(1)}, f32[128]{0:T(128)}, u32[]{:S(2)}) copy-start(f32[128]{0:T(128)} %copy-done.69) | copy-start | bytes 1540
  624.7 14.1 %copy-start.72 = (f32[128]{0:T(128)S(1)}, f32[128]{0:T(128)}, u32[]{:S(2)}) copy-start(f32[128]{0:T(128)} %copy-done.71) | copy-start | bytes 1540
  624.7 19.5 %slice-start.6 = ((s8[4718592]{0:T(1024)(128)(4,1)}), s8[524288]{0:T(1024)(128)(4,1)S(1)}, s32[]{:S(2)}) async-start(s8[4718592]{0:T(1024)(128)(4,1)} %bitcast.227), calls=%async_computation.11 | async-start | bytes 1048576
  723.1 90.3 %copy-start.1 = (bf16[256,1024]{1,0:T(8,128)(2,1)S(1)}, bf16[256,1024]{1,0:T(8,128)(2,1)}, u32[]{:S(2)}) copy-start(bf16[256,1024]{1,0:T(8,128)(2,1)} %param.31) | copy-start | bytes 1572868
  (90 other events, 513.3 us)
Sparse Core Ops, SparseCore 0:
  664.5 141.7 all-reduce.7
where the time goes:
time: 830 us; the launch traced here: 821 us
  local copies, waits for them, and re-layouts  273 us (33%)
  matrix products  192 us (23%)
  other arithmetic  179 us (22%)
  waiting for transfers between devices  90.9 us (11%)
  blocking collectives  43 us (5%)
  starting transfers between devices  26.9 us (3%)
  between operations  16.4 us (2%)
    psum x1, waiting for transfers between devices, per_device(): lax.psum((gain1_grad, bias1_grad, qkv_grad, conv_grad, convbias_grad, pro...  77.9 us
    convert_element_type x1, other arithmetic, per_device(): act = act_float.astype(jnp.bfloat16)  47.1 us
    psum x1, blocking collectives, per_device(): lax.psum((gain1_grad, bias1_grad, qkv_grad, conv_grad, convbias_grad, pro...  43 us
    reshape x4, local copies, waits for them, and re-layouts, row_windows(): value.reshape(count, height // STRIPE, STRIPE * breadth, head_count, chan...  40.2 us
    transpose x4, local copies, waits for them, and re-layouts, col_windows(): shaped.transpose(0, 2, 1, 3, 4, 5)  27 us
    dot_general x2, matrix products, attend_back(): jnp.einsum('...qhe,...khe->...hqk', d_context, values, preferred_element_...  26 us
    dot_general x2, matrix products, attend_back(): jnp.einsum('...hqk,...qhe->...khe', low_probs, d_context, preferred_eleme...  21.4 us
    unnamed x266, local copies, waits for them, and re-layouts  21.1 us
  transfers between devices with their start and end apart: 9, of which 2 were waited for; matrix products, arithmetic and copies ran while one was open for 46% of the time, Pallas kernels for 0%

commit v1 on v0

v1 whole, which is shorter than its diff:
```python
import functools, math

import jax
import jax.numpy as jnp
from jax import lax
from jax.experimental import pallas as pl
from jax.experimental.pallas import tpu as pltpu
from jax.sharding import PartitionSpec as P
from types import SimpleNamespace as NS

F32 = jnp.float32
BF = jnp.bfloat16
EPS = 1e-5
SCALE = 32 ** -0.5
LOG2E = math.log2(math.e)
ERF_P = 0.3275911 / math.sqrt(2.0)
ERF_C = [0.5 * c for c in (0.254829592, -0.284496736, 1.421413741, -1.453152027, 1.061405429)]


def dot(a, b, ca=1, cb=0):
    return lax.dot_general(a, b, (((ca,), (cb,)), ((), ())), preferred_element_type=F32)


def gelu_parts(v):
    t = 1.0 / (1.0 + ERF_P * jnp.abs(v))
    e = jnp.exp2(v * v * (-0.5 * LOG2E))
    poly = ERF_C[4]
    for c in ERF_C[3::-1]:
        poly = poly * t + c
    h = poly * t * e
    cdf = jnp.where(v >= 0.0, 1.0 - h, h)
    act = v * cdf
    slope = cdf + v * (e * (1.0 / math.sqrt(2.0 * math.pi)))
    return act, slope


def normalise(x):
    mean = jnp.mean(x, axis=-1, keepdims=True)
    center = x - mean
    var = jnp.mean(center * center, axis=-1, keepdims=True)
    rstd = lax.rsqrt(var + EPS)
    return center * rstd, rstd


def normalise_back(d, u, rstd, gain):
    e = d * gain
    m1 = jnp.mean(e, axis=-1, keepdims=True)
    m2 = jnp.mean(e * u, axis=-1, keepdims=True)
    return (e - m1 - u * m2) * rstd


def rowsum(x):
    return jnp.sum(x, axis=0, keepdims=True)


def expand(w, hm):
    return jnp.concatenate([w, w, w, w], axis=0) * hm


def diagonal(r, lane):
    o = r[0:32]
    for h in (1, 2, 3):
        o = jnp.where(lane >= 32 * h, r[32 * h : 32 * h + 32], o)
    return o


def shifts(a, pos):
    n = a.shape[0]
    before = jnp.where(pos == 0, 0.0, pltpu.roll(a, 1, 0))
    after = jnp.where(pos == 15, 0.0, pltpu.roll(a, n - 1, 0))
    return before, a, after


def swap_rows(a):
    n, c = a.shape
    a4 = a.reshape(n // 32, 2, 16, c)
    return a4[:, 0], a4[:, 1]


def join_rows(a0, a1):
    n = a0.shape[0]
    return jnp.stack([a0, a1], axis=1).reshape(n * 32, a0.shape[-1])


def psum8(x):
    n, c = x.shape
    return jnp.sum(x.reshape(n // 8, 8, c), axis=0)


G1, B1, G2, B2, PB, FB2, CB, CONV = 0, 1, 2, 3, 4, 5, 6, 7


class Params:
    def __init__(self, refs):
        (
            self.perm,
            self.hm,
            self.vec,
            self.taps,
            self.wf,
            self.wt,
            self.wq,
            self.wp,
            self.w1,
            self.bf1,
            self.w2,
        ) = refs


def permute(perm, x):
    n = x.shape[0] // 256
    return jnp.concatenate(
        [dot(perm, x[256 * i : 256 * i + 256]).astype(BF) for i in range(n)], axis=0
    )


def phase_one(c, p, s, a, keep1, keep2):
    tokens = s.x.shape[1]
    windows = tokens // 32
    perm = p.perm[...]
    hm = p.hm[...]
    vec = lambda i: p.vec[i : i + 1]
    x = s.x[c].astype(F32)
    u1, _ = normalise(x)
    n1 = (u1 * vec(G1) + vec(B1)).astype(BF)
    s.n1[c] = n1
    n1p = permute(perm, n1)
    qkv_f = dot(n1, p.wf[...]).astype(BF)
    qkv_t = dot(n1p, p.wt[...]).astype(BF)
    s.q[c] = jnp.concatenate([qkv_f[:, 0:128], qkv_t[:, 0:128]], axis=1)
    s.k[c] = jnp.concatenate([qkv_f[:, 128:256], qkv_t[:, 128:256]], axis=1)
    s.v[c] = jnp.concatenate([qkv_f[:, 256:384], qkv_t[:, 256:384]], axis=1)
    lane = lax.broadcasted_iota(jnp.int32, (32, 128), 1)
    pos = lax.broadcasted_iota(jnp.int32, (tokens, 256), 0) % 16
    out = []
    for w in range(windows):
        halves = []
        rows = slice(32 * w, 32 * w + 32)
        for half in range(2):
            cols = slice(128 * half, 128 * half + 128)
            qx = expand(s.q[c, rows, cols], hm)
            st = dot(s.k[c, rows, cols], qx, 1, 1)
            top = jnp.max(st, axis=0, keepdims=True)
            e = jnp.exp2((st - top) * (SCALE * LOG2E))
            pr = (e * (1.0 / jnp.sum(e, axis=0, keepdims=True))).astype(BF)
            s.p[c, rows, cols] = pr
            halves.append(diagonal(dot(pr, s.v[c, rows, cols], 0, 0), lane))
        out.append(jnp.concatenate(halves, axis=1))
    ctx = jnp.concatenate(out, axis=0)
    tap = lambda i, j: p.taps[3 * (i + 1) + j + 1 : 3 * (i + 1) + j + 2]
    vs = shifts(s.v[c].astype(F32), pos)
    line = lambda i, pick: sum(pick(vs[j + 1]) * tap(i, j) for j in (-1, 0, 1))
    first = lambda z: swap_rows(z)[0].reshape(tokens // 2, 256)
    second = lambda z: swap_rows(z)[1].reshape(tokens // 2, 256)
    o0 = line(0, first) + line(1, second)
    o1 = line(0, second) + line(-1, first)
    o0 = o0.reshape(windows, 16, 256)
    o1 = o1.reshape(windows, 16, 256)
    lepe = join_rows(o0, o1) + vec(CB)
    att = (ctx + lepe).astype(BF)
    att = jnp.concatenate([att[:, :128], permute(perm, att[:, 128:])], axis=1)
    branch1 = dot(att, p.wp[...]) + vec(PB)
    h1 = x + keep1 * branch1
    u2, rstd2 = normalise(h1)
    n2 = (u2 * vec(G2) + vec(B2)).astype(BF)
    cot = s.cot[c].astype(F32)
    db2f = keep2 * cot
    db2 = db2f.astype(BF)
    a.small[FB2] += psum8(db2.astype(F32))
    ones = jnp.ones((16, tokens), BF)
    n2t = jnp.concatenate([n2.T, ones], axis=0)
    db2t = db2.T
    branch2 = jnp.zeros((tokens, 256), F32)
    dn2 = jnp.zeros((tokens, 256), F32)
    for f in range(4):
        fs = slice(256 * f, 256 * f + 256)
        pre = dot(n2, p.w1[:, fs]) + p.bf1[:, fs]
        act, slope = gelu_parts(pre)
        act = act.astype(BF)
        dpre = (slope * dot(db2, p.w2[fs, :], 1, 1)).astype(BF)
        branch2 = branch2 + dot(act, p.w2[fs, :])
        dn2 = dn2 + dot(dpre, p.w1[:, fs], 1, 1)
        a.w1[:, fs] += dot(n2t, dpre)
        a.w2t[:, fs] += dot(db2t, act)
    s.out[c] = (h1 + keep2 * (branch2 + vec(FB2))).astype(BF)
    a.small[G2] += psum8(dn2 * u2)
    a.small[B2] += psum8(dn2)
    dh1 = cot + normalise_back(dn2, u2, rstd2, vec(G2))
    s.dh1[c] = dh1
    db1 = (keep1 * dh1).astype(BF)
    a.small[PB] += psum8(db1.astype(F32))
    a.wp[...] += dot(att, db1, 0, 0)
    datt = dot(db1, p.wp[...], 1, 1).astype(BF)
    s.da[c] = jnp.concatenate([datt[:, :128], permute(perm, datt[:, 128:])], axis=1)


def phase_two(c, p, s, a):
    tokens = s.x.shape[1]
    windows = tokens // 32
    perm = p.perm[...]
    hm = p.hm[...]
    vec = lambda i: p.vec[i : i + 1]
    lane = lax.broadcasted_iota(jnp.int32, (32, 128), 1)
    pos = lax.broadcasted_iota(jnp.int32, (tokens, 256), 0) % 16
    dq, dk, dv = [], [], []
    for w in range(windows):
        hq, hk, hv = [], [], []
        rows = slice(32 * w, 32 * w + 32)
        for half in range(2):
            cols = slice(128 * half, 128 * half + 128)
            dax = expand(s.da[c, rows, cols], hm)
            qx = expand(s.q[c, rows, cols], hm)
            dp = dot(s.v[c, rows, cols], dax, 1, 1)
            pb = s.p[c, rows, cols]
            pr = pb.astype(F32)
            t = pr * dp
            ds = (t - pr * jnp.sum(t, axis=0, keepdims=True)).astype(BF)
            hv.append(dot(pb, dax))
            hk.append(dot(ds, qx))
            hq.append(diagonal(dot(ds, s.k[c, rows, cols], 0, 0), lane))
        dq.append(jnp.concatenate(hq, axis=1))
        dk.append(jnp.concatenate(hk, axis=1))
        dv.append(jnp.concatenate(hv, axis=1))
    dq = (jnp.concatenate(dq, axis=0) * SCALE).astype(BF)
    dk = (jnp.concatenate(dk, axis=0) * SCALE).astype(BF)
    dv = jnp.concatenate(dv, axis=0)
    tap = lambda i, j: p.taps[3 * (i + 1) + j + 1 : 3 * (i + 1) + j + 2]
    da = s.da[c].astype(F32)
    a.small[CB] += psum8(da)
    before, here, after = shifts(da, pos)
    moved = {-1: after, 0: here, 1: before}
    first = lambda z: swap_rows(z)[0].reshape(tokens // 2, 256)
    second = lambda z: swap_rows(z)[1].reshape(tokens // 2, 256)
    v = s.v[c].astype(F32)
    v0, v1 = first(v), second(v)
    line = lambda i, pick: sum(pick(moved[j]) * tap(i, j) for j in (-1, 0, 1))
    o0 = line(0, first) + line(-1, second)
    o1 = line(1, first) + line(0, second)
    dv = dv + join_rows(o0.reshape(windows, 16, 256), o1.reshape(windows, 16, 256))
    for j in (-1, 0, 1):
        m0, m1 = first(moved[j]), second(moved[j])
        a.small[CONV + 3 + j + 1] += psum8(m0 * v0) + psum8(m1 * v1)
        a.small[CONV + 6 + j + 1] += psum8(m0 * v1)
        a.small[CONV + 0 + j + 1] += psum8(m1 * v0)
    dv = dv.astype(BF)
    tall = permute(perm, jnp.concatenate([dq[:, 128:], dk[:, 128:], dv[:, 128:]], axis=1))
    dqkv = jnp.concatenate(
        [dq[:, :128], tall[:, :128], dk[:, :128], tall[:, 128:256], dv[:, :128], tall[:, 256:]],
        axis=1,
    )
    n1t = s.n1[c].T
    for f in range(3):
        fs = slice(256 * f, 256 * f + 256)
        a.wq[:, fs] += dot(n1t, dqkv[:, fs])
    dn1 = dot(dqkv, p.wq[...], 1, 1)
    u1, rstd1 = normalise(s.x[c].astype(F32))
    a.small[G1] += psum8(dn1 * u1)
    a.small[B1] += psum8(dn1)
    dx = s.dh1[c] + normalise_back(dn1, u1, rstd1, vec(G1))
    s.dx[c] = dx.astype(BF)
def prep(inputs_dict):
    d = inputs_dict
    g = lambda n: d[n].astype(F32)
    t = jnp.arange(256)
    perm = (((t % 16) * 16 + t // 16)[:, None] == t[None, :]).astype(BF)
    r = jnp.arange(128)
    hm = (r[:, None] // 32 == r[None, :] // 32).astype(BF)
    vec = jnp.stack([g("norm1_gain"), g("norm1_bias"), g("norm2_gain"), g("norm2_bias"), g("proj_bias"), g("fc2_bias"), g("lepe_bias"), jnp.zeros((256,), F32)])
    lw = g("lepe_weight")
    taps = jnp.concatenate([lw[..., :128], lw.transpose(1, 0, 2)[..., 128:]], axis=-1).reshape(9, 256)
    wq = d["qkv_weight"]
    wf = jnp.concatenate([wq[:, 0:128], wq[:, 256:384], wq[:, 512:640]], axis=1)
    wt = jnp.concatenate([wq[:, 128:256], wq[:, 384:512], wq[:, 640:768]], axis=1)
    return [perm, hm, vec, taps, wf, wt, wq, d["proj_weight"], d["fc1_weight"], g("fc1_bias")[None], d["fc2_weight"]]

def kernel(nimg, x_ref, cot_ref, drops_ref, *refs):
    p = Params(refs[:11])
    out, dx, w1, w2t, wq, wp, small = refs[11:18]
    q, k, v, pr, n1, dh1, da = refs[18:]
    s = NS(x=x_ref, cot=cot_ref, out=out, dx=dx, q=q, k=k, v=v, p=pr, n1=n1, dh1=dh1, da=da)
    a = NS(w1=w1, w2t=w2t, wq=wq, wp=wp, small=small)
    for r in (w1, w2t, wq, wp, small):
        r[...] = jnp.zeros_like(r)
    chunks = x_ref.shape[0]
    def keep(c, j):
        return jnp.concatenate([jnp.full((256, 1), drops_ref[c * nimg + i, j].astype(F32) * 1.25) for i in range(nimg)], axis=0)
    def one(c, _):
        phase_one(c, p, s, a, keep(c, 0), keep(c, 1))
        return 0
    def two(c, _):
        phase_two(c, p, s, a)
        return 0
    lax.fori_loop(0, chunks, one, 0)
    lax.fori_loop(0, chunks, two, 0)

def run(x, cot, drops, ws, nimg=2):
    chunks = x.size // (65536 * nimg)
    x = x.reshape(chunks, 256 * nimg, 256); cot = cot.reshape(x.shape)
    V = pl.BlockSpec(memory_space=pltpu.VMEM)
    sds = jax.ShapeDtypeStruct
    T = 256 * nimg
    vm = lambda dt: pltpu.VMEM((chunks, T, 256), dt)
    return pl.pallas_call(functools.partial(kernel, nimg),
        in_specs=[V, V, pl.BlockSpec(memory_space=pltpu.SMEM)] + [V] * 11,
        out_specs=[V] * 7,
        out_shape=[sds(x.shape, BF), sds(x.shape, BF), sds((272, 1024), F32), sds((256, 1024), F32), sds((256, 768), F32), sds((256, 256), F32), sds((16, 8, 256), F32)],
        scratch_shapes=[vm(BF), vm(BF), vm(BF), vm(BF), vm(BF), vm(F32), vm(BF)],
        compiler_params=pltpu.CompilerParams(vmem_limit_bytes=60 * 2**20),
    )(x, cot, drops, *ws)


def per_device(inputs, partners, boxes, drops, norm1_gain, norm1_bias, qkv_weight, lepe_weight, lepe_bias, proj_weight, proj_bias, norm2_gain, norm2_bias, fc1_weight, fc1_bias, fc2_weight, fc2_bias, cotangent):
    image_count, row_count, side, width = inputs.shape
    shares = lax.axis_size("row")
    mine = image_count // shares
    row = lax.axis_index("row")
    local_partner = partners - lax.axis_index("batch") * image_count
    row_ids = row * row_count + jnp.arange(row_count)
    col_ids = jnp.arange(side)
    source = inputs.astype(F32)
    partner_rows = inputs[local_partner].astype(F32)
    inside = (
        (row_ids[None, :, None] >= boxes[:, 0, None, None])
        & (row_ids[None, :, None] < boxes[:, 1, None, None])
        & (col_ids[None, None, :] >= boxes[:, 2, None, None])
        & (col_ids[None, None, :] < boxes[:, 3, None, None])
    )[..., None]
    mixed = jnp.where(inside, partner_rows, 0.7 * source + 0.3 * partner_rows).astype(BF)
    x = lax.all_to_all(mixed, "row", split_axis=0, concat_axis=1, tiled=True)
    cot = lax.all_to_all(cotangent, "row", split_axis=0, concat_axis=1, tiled=True)
    my_drops = lax.dynamic_slice_in_dim(drops, row * mine, mine, 0)
    names = dict(norm1_gain=norm1_gain, norm1_bias=norm1_bias, qkv_weight=qkv_weight, lepe_weight=lepe_weight, lepe_bias=lepe_bias, proj_weight=proj_weight, proj_bias=proj_bias, norm2_gain=norm2_gain, norm2_bias=norm2_bias, fc1_weight=fc1_weight, fc1_bias=fc1_bias, fc2_weight=fc2_weight, fc2_bias=fc2_bias)
    out, dx, w1, w2t, wq, wp, small = run(x, cot, my_drops, prep(names), 2)
    shape = (mine, side, side, width)
    out = lax.all_to_all(out.reshape(shape), "row", split_axis=1, concat_axis=0, tiled=True)
    dx = lax.all_to_all(dx.reshape(shape), "row", split_axis=1, concat_axis=0, tiled=True).astype(F32)
    small = jnp.sum(small, axis=1)
    w1, w2t, wq, wp, small = lax.psum((w1, w2t, wq, wp, small), ("batch", "row"))
    own_part = 0.7 * jnp.where(inside, 0.0, dx)
    toward = jnp.where(inside, dx, 0.3 * dx)
    image_ids = jnp.arange(image_count)
    hits = local_partner[:, None] == image_ids[None, :]
    inverse = jnp.sum(jnp.where(hits, image_ids[:, None], 0), axis=0)
    input_grad = (own_part + toward[inverse]).astype(BF)
    conv = small[CONV : CONV + 9].reshape(3, 3, 256)
    conv = jnp.concatenate([conv[..., :128], conv.transpose(1, 0, 2)[..., 128:]], axis=-1)
    return (
        out,
        input_grad,
        small[G1],
        small[B1],
        wq,
        conv,
        small[CB],
        wp,
        small[PB],
        small[G2],
        small[B2],
        w1[:256],
        w1[256],
        w2t.T,
        small[FB2],
    )


def solution(mesh):
    tokens = P("batch", "row", None, None)
    return jax.shard_map(
        per_device,
        mesh=mesh,
        in_specs=(tokens, P("batch"), P("batch", None), P("batch", None)) + (P(),) * 13 + (tokens,),
        out_specs=(tokens, tokens) + (P(),) * 13,
        check_vma=False,
    )
```

time: 830 us -> 474 us (0.57); the launches traced: 821 us -> 474 us
  local copies, waits for them, and re-layouts: 273 us -> 37.1 us
  matrix products: 192 us -> 0 us
  Pallas kernels: 0 us -> 174 us
  other arithmetic: 179 us -> 16.1 us
  waiting for transfers between devices: 90.9 us -> 147 us
  blocking collectives: 43 us -> 69.6 us
  starting transfers between devices: 26.9 us -> 15.6 us
    dot_general x24 -> x0, matrix products: 192 us -> none  [the longest x2 26 us: attend_back(): jnp.einsum('...qhe,...khe->...hqk', d_context, values, preferred_element_...]
    pallas_call x0 -> x1, Pallas kernels: none -> 174 us  [run(): pl.pallas_call(functools.partial(kernel, nimg), in_specs=[V, V, pl.BlockS...]
    convert_element_type x18 -> x4, other arithmetic: 92.3 us -> 11.3 us  [the longest x1 5.36 us: per_device(): input_grad = (own_part + toward[inverse]).astype(BF)]
    transpose x10 -> x0, local copies, waits for them, and re-layouts: 64.7 us -> none  [the longest x4 27 us: col_windows(): shaped.transpose(0, 2, 1, 3, 4, 5)]
    all_to_all x4, waiting for transfers between devices: 13 us -> 66.9 us  [the longest x1 25.1 us: per_device(): lax.all_to_all(out.reshape(shape), 'row', split_axis=1, concat_axis=0, ti...]
    reshape x9 -> x4, local copies, waits for them, and re-layouts: 59.5 us -> 7.3 us  [the longest x1 3.36 us: per_device(): dx.reshape(shape)]
    convert_element_type x10 -> x1, local copies, waits for them, and re-layouts: 50.4 us -> 0.66 us  [per_device(): lax.all_to_all(dx.reshape(shape), 'row', split_axis=1, concat_axis=0, til...]
    reduce_sum x10 -> x1, other arithmetic: 38.5 us -> 0.04 us  [per_device(): small = jnp.sum(small, axis=1)]
  transfers between devices with their start and end apart: 9 -> 5, of which waited for: 2 -> 4; matrix products, arithmetic and copies ran while one was open for 46% -> 6% of each run, Pallas kernels for 0% -> 0%
where the time goes in v1:
time: 474 us
  Pallas kernels  174 us (37%)
  waiting for transfers between devices  147 us (31%)
  blocking collectives  69.6 us (15%)
  local copies, waits for them, and re-layouts  37.1 us (8%)
  other arithmetic  16.1 us (3%)
  starting transfers between devices  15.6 us (3%)
  between operations  14.5 us (3%)
    pallas_call x1, Pallas kernels, run(): pl.pallas_call(functools.partial(kernel, nimg), in_specs=[V, V, pl.BlockS...  174 us
    psum x1, waiting for transfers between devices, per_device(): lax.psum((w1, w2t, wq, wp, small), ('batch', 'row'))  79.6 us
    psum x1, blocking collectives, per_device(): lax.psum((w1, w2t, wq, wp, small), ('batch', 'row'))  69.6 us
    all_to_all x1, waiting for transfers between devices, per_device(): lax.all_to_all(out.reshape(shape), 'row', split_axis=1, concat_axis=0, ti...  25.1 us
    all_to_all x1, waiting for transfers between devices, per_device(): lax.all_to_all(cotangent, 'row', split_axis=0, concat_axis=1, tiled=True)  21.8 us
    all_to_all x1, waiting for transfers between devices, per_device(): x = lax.all_to_all(mixed, 'row', split_axis=0, concat_axis=1, tiled=True)  20 us
  transfers between devices with their start and end apart: 5, of which 4 were waited for; matrix products, arithmetic and copies ran while one was open for 6% of the time, Pallas kernels for 0%

profile of v1, /device:TPU:0, one launch (start us, length us, event | category | flops | bytes accessed | tf_op | source)
XLA Modules:
  0.0 473.6 jit_solution(3226718012419707400)
XLA Ops:
  7.2 0.0 copy-start
  7.2 4.7 all-to-all-start.1
  11.9 0.1 compare_and_fusion
  12.0 0.1 copy.76
  12.2 2.3 gather_fusion
  14.5 0.1 iota_compare_fusion.2
  14.6 0.1 and_and_fusion
  14.7 4.5 fusion.1
  19.3 21.8 %all-to-all-done.1 = bf16[72,4,16,256]{3,2,1,0:T(8,128)(2,1)} async-done(((bf16[72,4,16,256]{3,2,1,0:T(8,128)(2,1)}), bf16[72,4,16,256]{3,2,1,0:T(8,128)(2,1)}, u32[]{:S(2)}, u32[]{:S(2)}) %all-to-all-start.1) | async-done | bytes 2359328 | tf_op jit(solution)/shard_map/all_to_all | solution.py:330
  41.1 3.6 all-to-all-start
  44.9 0.6 broadcast_in_dim.61
  45.5 0.1 constant_dynamic-slice_fusion
  45.6 0.7 copy.89.drops_ref
  46.3 0.6 reshape.288.refs_3_
  46.9 0.6 stack.59.refs_2_
  47.5 0.1 fusion.11
  47.6 0.8 pad_maximum_fusion
  48.4 0.7 compare_convert_fusion.refs_1_
  49.1 0.8 fusion.5.refs_0_
  49.9 3.4 copy.78
  53.2 20.0 %all-to-all-done = bf16[72,4,16,256]{3,2,1,0:T(8,128)(2,1)S(1)} async-done(((bf16[72,4,16,256]{3,2,1,0:T(8,128)(2,1)}), bf16[72,4,16,256]{3,2,1,0:T(8,128)(2,1)S(1)}, u32[]{:S(2)}, u32[]{:S(2)}) %all-to-all-start) | async-done | bytes 2359328 | tf_op jit(solution)/shard_map/all_to_all | solution.py:329
  73.2 1.6 copy.77
  74.8 173.5 %shard_map.289 = (bf16[9,512,256]{2,1,0:T(8,128)(2,1)}, bf16[9,512,256]{2,1,0:T(8,128)(2,1)}, f32[272,1024]{1,0:T(8,128)}, f32[256,1024]{1,0:T(8,128)}, f32[256,...) custom-call(bf16[9,512,256]{2,1,0:T(8,128)(2,1)} %bitcast.63, bf16[9,512,256]{2,1,0:T(8,128)(2,1)} %bitcast.62, ...), custom_call_target="tpu_custom_call" | custom-call | tf_op jit(solution)/shard_map/pallas_call | solution.py:303
  248.3 3.3 copy.82
  251.6 3.6 all-to-all-start.2
  255.3 3.4 copy.84
  258.6 25.1 %all-to-all-done.2 = bf16[18,16,16,256]{3,2,0,1:T(8,128)(2,1)S(1)} async-done(((bf16[18,16,16,256]{3,2,0,1:T(8,128)(2,1)}), bf16[18,16,16,256]{3,2,0,1:T(8,128)(2,1)S(1)}, u32[]{:S(2)}, u32[]{:S(2)}) %all-to-all-start.2) | async-done | bytes 2359328 | tf_op jit(solution)/shard_map/all_to_all | solution.py:335
  283.7 1.4 copy-done.3
  285.2 3.6 all-to-all-start.3
  288.8 0.0 all-reduce.3.cloned.1.call-start
  288.9 0.7 all-reduce.3.cloned.1.call-update
  289.5 0.1 select_reduce_fusion
  289.7 0.0 copy-done.8
  289.7 69.6 %psum.35 = f32[16,256]{1,0:T(8,128)S(1)} all-reduce(f32[16,256]{1,0:T(8,128)S(1)} %reduce_sum.22), channel_id=1, replica_groups=mesh['batch'=8,'row'=4] {'batch','row'}, use_global_device_ids=true, to_apply=%region_2.3 | all-reduce | flops 4096 | bytes 32768 | tf_op jit(solution)/shard_map/psum | solution.py:338
  359.4 0.6 copy.87
  360.0 0.6 fusion.12
  360.6 79.6 %all-reduce.3.cloned.1.call-done = (f32[256,768]{1,0:T(8,128)}, f32[256,256]{1,0:T(8,128)}, f32[272,1024]{1,0:T(8,128)}, f32[1024,256]{0,1:T(8,128)}) async-done(((f32[256,768]{1,0:T(8,128)}, f32[256,256]{1,0:T(8,128)}, f32[272,1024]{1,0:T(8,128)}, f32[1024,256]{0,1:T(8,128)}), (f32[256,768]{1,0:T(8,128)}, f32[256,256]{1,0:T(8,128)}, f32[272,1024]{1,0:T(8,128)}, ...) | async-done | bytes 3211280 | tf_op jit(solution)/shard_map/psum | solution.py:338
  440.1 1.4 slice.118
  441.6 2.3 slice.117
  443.9 1.3 copy.88
  445.2 3.4 copy.83
  448.6 0.7 copy.85
  449.3 2.1 copy-done.1
  451.4 3.0 multiply_select_fusion
  454.4 5.4 %gather_fusion.1 = f32[72,4,16,256]{3,2,1,0:T(8,128)} fusion(f32[72,4,16,256]{3,2,1,0:T(8,128)} %multiply_select_fusion, s32[1024]{0:T(1024)S(1)} %pad_clamp_fusion), kind=kCustom, calls=%fused_computation.1 | custom fusion | bytes 9437472 | tf_op jit(solution)/shard_map/gather | solution.py:344
  459.8 5.4 %fusion.4 = bf16[72,4,16,256]{3,2,1,0:T(8,128)(2,1)} fusion(f32[72,4,16,256]{3,2,1,0:T(8,128)} %gather_fusion.1, f32[18,4,4,16,256]{4,3,2,0,1:T(8,128)} %copy-done.1, pred[72,4,16]{2,1,0:T(4,128)(4,1)S(1)} %and_and_fusion), kind=kLoop, calls=%fused_computation.10 | loop fusion | flops 4718592 | bytes 11801088 | tf_op jit(solution)/shard_map/convert_element_type | solution.py:344
  465.1 0.9 copy.96
  466.0 0.7 copy.97
  (66 shorter events, 0.3 us)
Async XLA Ops:
  7.2 38.3 %copy-start = (s32[72,2]{0,1:T(2,128)S(1)}, s32[72,2]{0,1:T(2,128)}, u32[]{:S(2)}) copy-start(s32[72,2]{0,1:T(2,128)} %param.21) | copy-start | bytes 1732
  7.2 4.7 copy-start.11
  7.2 4.9 %copy-start.12 = (s32[72]{0:T(128)S(1)}, s32[72]{0:T(128)}, u32[]{:S(2)}) copy-start(s32[72]{0:T(128)} %param.19) | copy-start | bytes 868
  7.2 5.0 %copy-start.2 = (bf16[72,4,16,256]{3,2,1,0:T(8,128)(2,1)S(1)}, bf16[72,4,16,256]{3,2,1,0:T(8,128)(2,1)}, u32[]{:S(2)}) copy-start(bf16[72,4,16,256]{3,2,1,0:T(8,128)(2,1)} %param.18) | copy-start | bytes 7077892
  7.2 33.9 %all-to-all-start.1 = ((bf16[72,4,16,256]{3,2,1,0:T(8,128)(2,1)}), bf16[72,4,16,256]{3,2,1,0:T(8,128)(2,1)}, u32[]{:S(2)}, u32[]{:S(2)}) async-start(bf16[72,4,16,256]{3,2,1,0:T(8,128)(2,1)} %param.35), calls=%async_computation.1 | async-start | bytes 4718592 | tf_op jit(solution)/shard_map/all_to_all | solution.py:330
  19.2 25.5 %copy-start.13 = (bf16[256]{0:T(256)(128)(2,1)S(1)}, bf16[256]{0:T(256)(128)(2,1)}, u32[]{:S(2)}) copy-start(bf16[256]{0:T(256)(128)(2,1)} %param.22) | copy-start | bytes 1540
  19.2 25.6 %copy-start.14 = (bf16[256]{0:T(256)(128)(2,1)S(1)}, bf16[256]{0:T(256)(128)(2,1)}, u32[]{:S(2)}) copy-start(bf16[256]{0:T(256)(128)(2,1)} %param.23) | copy-start | bytes 1540
  19.2 25.6 %copy-start.15 = (bf16[256]{0:T(256)(128)(2,1)S(1)}, bf16[256]{0:T(256)(128)(2,1)}, u32[]{:S(2)}) copy-start(bf16[256]{0:T(256)(128)(2,1)} %param.26) | copy-start | bytes 1540
  19.2 25.6 %copy-start.16 = (bf16[256]{0:T(256)(128)(2,1)S(1)}, bf16[256]{0:T(256)(128)(2,1)}, u32[]{:S(2)}) copy-start(bf16[256]{0:T(256)(128)(2,1)} %param.28) | copy-start | bytes 1540
  19.2 25.6 %copy-start.17 = (bf16[256]{0:T(256)(128)(2,1)S(1)}, bf16[256]{0:T(256)(128)(2,1)}, u32[]{:S(2)}) copy-start(bf16[256]{0:T(256)(128)(2,1)} %param.29) | copy-start | bytes 1540
  19.2 25.6 %copy-start.18 = (bf16[256]{0:T(256)(128)(2,1)S(1)}, bf16[256]{0:T(256)(128)(2,1)}, u32[]{:S(2)}) copy-start(bf16[256]{0:T(256)(128)(2,1)} %param.30) | copy-start | bytes 1540
  19.2 25.6 %copy-start.19 = (bf16[256]{0:T(256)(128)(2,1)S(1)}, bf16[256]{0:T(256)(128)(2,1)}, u32[]{:S(2)}) copy-start(bf16[256]{0:T(256)(128)(2,1)} %param.34) | copy-start | bytes 1540
  19.2 25.6 %copy-start.10 = (bf16[1024]{0:T(1024)(128)(2,1)S(1)}, bf16[1024]{0:T(1024)(128)(2,1)}, u32[]{:S(2)}) copy-start(bf16[1024]{0:T(1024)(128)(2,1)} %param.32) | copy-start | bytes 6148
  19.3 26.2 %copy-start.9 = (bf16[3,3,256]{2,1,0:T(4,128)(2,1)S(1)}, bf16[3,3,256]{2,1,0:T(4,128)(2,1)}, u32[]{:S(2)}) copy-start(bf16[3,3,256]{2,1,0:T(4,128)(2,1)} %param.25) | copy-start | bytes 13828
  19.3 28.3 %copy-start.4 = (bf16[256,768]{1,0:T(8,128)(2,1)S(1)}, bf16[256,768]{1,0:T(8,128)(2,1)}, u32[]{:S(2)}) copy-start(bf16[256,768]{1,0:T(8,128)(2,1)} %refs_6_.1) | copy-start | bytes 1179652
  41.1 32.1 %all-to-all-start = ((bf16[72,4,16,256]{3,2,1,0:T(8,128)(2,1)}), bf16[72,4,16,256]{3,2,1,0:T(8,128)(2,1)S(1)}, u32[]{:S(2)}, u32[]{:S(2)}) async-start(bf16[72,4,16,256]{3,2,1,0:T(8,128)(2,1)} %fusion.1), calls=%async_computation | async-start | bytes 4718592 | tf_op jit(solution)/shard_map/all_to_all | solution.py:329
  251.6 32.1 %all-to-all-start.2 = ((bf16[18,16,16,256]{3,2,0,1:T(8,128)(2,1)}), bf16[18,16,16,256]{3,2,0,1:T(8,128)(2,1)S(1)}, u32[]{:S(2)}, u32[]{:S(2)}) async-start(bf16[18,16,16,256]{3,2,0,1:T(8,128)(2,1)} %copy.82), calls=%async_computation.2 | async-start | bytes 4718592 | tf_op jit(solution)/shard_map/all_to_all | solution.py:335
  283.7 1.4 copy-start.3
  285.2 163.5 %all-to-all-start.3 = ((bf16[18,16,16,256]{3,2,0,1:T(8,128)(2,1)}), bf16[18,16,16,256]{3,2,0,1:T(8,128)(2,1)S(1)}, u32[]{:S(2)}, u32[]{:S(2)}) async-start(bf16[18,16,16,256]{3,2,0,1:T(8,128)(2,1)} %copy.84), calls=%async_computation.3 | async-start | bytes 4718592 | tf_op jit(solution)/shard_map/all_to_all | solution.py:336
  288.8 0.9 copy-start.8
  288.8 151.3 %all-reduce.3.cloned.1.call-start = ((), (), s32[]{:S(2)}) async-start(), calls=%async_computation.4 | async-start | bytes 6422528 | tf_op jit(solution)/shard_map/psum | solution.py:338
  440.1 3.8 copy-start.5
  449.3 2.2 copy-start.1
  459.8 5.4 %copy-start.6 = (f32[256,768]{1,0:T(8,128)S(1)}, f32[256,768]{1,0:T(8,128)}, u32[]{:S(2)}) copy-start(f32[256,768]{1,0:T(8,128)} %get-tuple-element.135) | copy-start | bytes 2359300
  459.8 6.2 %copy-start.7 = (f32[256,256]{1,0:T(8,128)S(1)}, f32[256,256]{1,0:T(8,128)}, u32[]{:S(2)}) copy-start(f32[256,256]{1,0:T(8,128)} %get-tuple-element.138) | copy-start | bytes 786436
Sparse Core Ops, SparseCore 0:
  296.9 143.1 all-reduce.2

commit v2 on v1

v2 whole, which is shorter than its diff:
```python
import functools
import math

import jax
import jax.numpy as jnp
from jax import lax
from jax.experimental import pallas as pl
from jax.experimental.pallas import tpu as pltpu
from jax.sharding import PartitionSpec as P

F32 = jnp.float32
BF = jnp.bfloat16
EPS = 1e-5
SCALE = 32**-0.5
LOG2E = math.log2(math.e)
ERF_P = 0.3275911 / math.sqrt(2.0)
ERF_C = [0.5 * c for c in (0.254829592, -0.284496736, 1.421413741, -1.453152027, 1.061405429)]
G1, B1, G2, B2, PB, FB2, CB, CONV, FB1 = 0, 1, 2, 3, 4, 5, 6, 7, 16
N1, AT, DA, DN = 0, 1, 2, 3


def dot(a, b, ca=1, cb=0):
    return lax.dot_general(a, b, (((ca,), (cb,)), ((), ())), preferred_element_type=F32)


def gelu_parts(v):
    t = 1.0 / (1.0 + ERF_P * jnp.abs(v))
    e = jnp.exp2(v * v * (-0.5 * LOG2E))
    poly = ERF_C[4]
    for c in ERF_C[3::-1]:
        poly = poly * t + c
    h = poly * t * e
    cdf = jnp.where(v >= 0.0, 1.0 - h, h)
    return v * cdf, cdf + v * (e * (1.0 / math.sqrt(2.0 * math.pi)))


def normalise(x):
    center = x - jnp.mean(x, axis=-1, keepdims=True)
    rstd = lax.rsqrt(jnp.mean(center * center, axis=-1, keepdims=True) + EPS)
    return center * rstd, rstd


def normalise_back(d, u, rstd, gain):
    e = d * gain
    m1 = jnp.mean(e, axis=-1, keepdims=True)
    m2 = jnp.mean(e * u, axis=-1, keepdims=True)
    return (e - m1 - u * m2) * rstd


def sum8(x):
    n, c = x.shape
    return jnp.sum(x.reshape(n // 8, 8, c), axis=0)


def split_heads(w, lm):
    return [w * lm[h : h + 1] for h in range(4)]


def skewed(parts, w):
    return jnp.concatenate([parts[j ^ w] for j in range(4)], axis=0)


def stacked(parts, j):
    return jnp.concatenate([parts[w][j ^ w] for w in range(4)], axis=0)


def unskew(o, w, lane):
    r = o[w]
    for h in (1, 2, 3):
        r = jnp.where(lane >= 32 * h, o[h ^ w], r)
    return r


def four(x):
    return [x[32 * w : 32 * w + 32] for w in range(4)]


def attend_group(q, k, v, lm, lane):
    ps = []
    for w, (qw, kw) in enumerate(zip(four(q), four(k))):
        st = dot(kw, skewed(split_heads(qw, lm), w), 1, 1)
        top = jnp.max(st, axis=0, keepdims=True)
        e = jnp.exp2((st - top) * (SCALE * LOG2E))
        ps.append((e * (1.0 / jnp.sum(e, axis=0, keepdims=True))).astype(BF))
    p = jnp.concatenate(ps, axis=0)
    pt = four(p.T)
    vh = [split_heads(vw, lm) for vw in four(v)]
    o = [dot(pt[j], stacked(vh, j)) for j in range(4)]
    return p, jnp.concatenate([unskew(o, w, lane) for w in range(4)], axis=0)


def attend_group_back(q, k, v, p, da, lm, lane):
    dss, dks, dvs = [], [], []
    for w, (qw, vw, pw, dw) in enumerate(zip(four(q), four(v), four(p), four(da))):
        dx = skewed(split_heads(dw, lm), w)
        dp = dot(vw, dx, 1, 1)
        pr = pw.astype(F32)
        t = pr * dp
        ds = (t - pr * jnp.sum(t, axis=0, keepdims=True)).astype(BF)
        dss.append(ds)
        dvs.append(dot(pw, dx))
        dks.append(dot(ds, skewed(split_heads(qw, lm), w)))
    dst = four(jnp.concatenate(dss, axis=0).T)
    kh = [split_heads(kw, lm) for kw in four(k)]
    o = [dot(dst[j], stacked(kh, j)) for j in range(4)]
    dq = jnp.concatenate([unskew(o, w, lane) for w in range(4)], axis=0)
    return dq, jnp.concatenate(dks, axis=0), jnp.concatenate(dvs, axis=0)


def shifts(a):
    n = a.shape[0]
    pos = lax.broadcasted_iota(jnp.int32, a.shape, 0) % 16
    return {
        -1: jnp.where(pos == 0, 0.0, pltpu.roll(a, 1, 0)),
        0: a,
        1: jnp.where(pos == 15, 0.0, pltpu.roll(a, n - 1, 0)),
    }


def lines(a):
    n, c = a.shape
    b = a.reshape(n // 32, 2, 16, c)
    return b[:, 0].reshape(n // 2, c), b[:, 1].reshape(n // 2, c)


def woven(a0, a1):
    n, c = a0.shape
    return jnp.stack([a0.reshape(n // 16, 16, c), a1.reshape(n // 16, 16, c)], axis=1).reshape(2 * n, c)


def attend_half(s, lm, taps, shift):
    tokens = s["q"].shape[0]
    lane = lax.broadcasted_iota(jnp.int32, (32, 128), 1)
    out = []
    for g in range(tokens // 128):
        rows = slice(128 * g, 128 * g + 128)
        p, o = attend_group(s["q"][rows], s["k"][rows], s["v"][rows], lm, lane)
        s["p"][rows] = p
        out.append(o)
    tap = lambda i, j: taps[3 * (i + 1) + j + 1][None]
    near = {j: lines(z) for j, z in shifts(s["v"][...].astype(F32)).items()}
    line = lambda i, n: sum(near[j][n] * tap(i, j) for j in (-1, 0, 1))
    lepe = woven(line(0, 0) + line(1, 1), line(0, 1) + line(-1, 0))
    return (jnp.concatenate(out, axis=0) + (lepe + shift)).astype(BF)


def attend_half_back(s, lm, taps, small, cols):
    tokens = s["q"].shape[0]
    lane = lax.broadcasted_iota(jnp.int32, (32, 128), 1)
    parts = []
    for g in range(tokens // 128):
        rows = slice(128 * g, 128 * g + 128)
        parts.append(attend_group_back(s["q"][rows], s["k"][rows], s["v"][rows], s["p"][rows], s["da"][rows], lm, lane))
    dq, dk, dv = (jnp.concatenate(z, axis=0) for z in zip(*parts))
    tap = lambda i, j: taps[3 * (i + 1) + j + 1][None]
    da = s["da"][...].astype(F32)
    small[CB, :, cols] += sum8(da)
    moved = {-j: lines(z) for j, z in shifts(da).items()}
    v0, v1 = lines(s["v"][...].astype(F32))
    line = lambda i, n: sum(moved[j][n] * tap(i, j) for j in (-1, 0, 1))
    dv = dv + woven(line(0, 0) + line(-1, 1), line(1, 0) + line(0, 1))
    for j in (-1, 0, 1):
        m0, m1 = moved[j]
        small[CONV + 3 + j + 1, :, cols] += sum8(m0 * v0 + m1 * v1)
        small[CONV + 6 + j + 1, :, cols] += sum8(m0 * v1)
        small[CONV + 0 + j + 1, :, cols] += sum8(m1 * v0)
    return jnp.concatenate([(dq * SCALE).astype(BF), (dk * SCALE).astype(BF), dv.astype(BF)], axis=1)


class Exchange:
    def __init__(self, me, shares, send_sem, recv_sem):
        self.me, self.shares, self.send_sem, self.recv_sem = me, shares, send_sem, recv_sem

    def copy(self, kind, c, d, src, dst, arriving):
        to = lax.rem(self.me + d, self.shares)
        far = lax.rem(self.me + self.shares - d, self.shares) if arriving else self.me
        if kind in (N1, DA):
            source, target = src.at[c, to], dst.at[c, :, far]
        else:
            source, target = src.at[c, :, to], dst.at[c, far]
        return pltpu.make_async_remote_copy(
            src_ref=source,
            dst_ref=target,
            send_sem=self.send_sem.at[kind, c, d - 1],
            recv_sem=self.recv_sem.at[kind, c, d - 1],
            device_id={"row": to},
            device_id_type=pl.DeviceIdType.MESH,
        )

    def send(self, kind, c, src, dst):
        me = self.me
        if kind in (N1, DA):
            dst[c, :, me] = src[c, me]
        else:
            dst[c, me] = src[c, :, me]
        for d in range(1, self.shares):
            self.copy(kind, c, d, src, dst, False).start()

    def receive(self, kind, c, src, dst):
        for d in range(1, self.shares):
            self.copy(kind, c, d, src, dst, True).wait_recv()

    def sent(self, kind, c, src, dst):
        for d in range(1, self.shares):
            self.copy(kind, c, d, src, dst, False).wait_send()


def block_kernel(
    shares,
    ahead,
    boxes,
    drops,
    partners,
    inverse,
    x_ref,
    cot_ref,
    vec,
    wq,
    wp,
    w1,
    w2,
    out,
    ig,
    gw1,
    gw2t,
    gqf,
    gqt,
    gp,
    small,
    perm_ref,
    wf_ref,
    wt_ref,
    mixed,
    n1h,
    n1t,
    n1p,
    qf,
    kf,
    vf,
    pf,
    qt,
    kt,
    vt,
    pt,
    att_f,
    att_ts,
    att_th,
    dh1,
    da_f,
    da_ts,
    da_tt,
    dn_ts,
    dn_th,
    send_sem,
    recv_sem,
):
    chunks, _, pair, strip = n1h.shape[:4]
    images = x_ref.shape[0]
    mine = images // shares
    tokens = shares * pair * strip
    me = lax.axis_index("row")
    ex = Exchange(me, shares, send_sem, recv_sem)

    barrier = pltpu.get_barrier_semaphore()
    for d in range(1, shares):
        pl.semaphore_signal(
            barrier, inc=1, device_id={"row": lax.rem(me + d, shares)}, device_id_type=pl.DeviceIdType.MESH
        )
    pl.semaphore_wait(barrier, shares - 1)

    v = lambda i: vec[i : i + 1]
    lm = (
        lax.broadcasted_iota(jnp.int32, (8, 128), 0) == lax.broadcasted_iota(jnp.int32, (8, 128), 1) // 32
    ).astype(F32).astype(BF)
    to_row = lax.broadcasted_iota(jnp.int32, (256, 256), 0)
    to_col = lax.broadcasted_iota(jnp.int32, (256, 256), 1)
    perm_ref[...] = jnp.where((to_row % 16) * 16 + to_row // 16 == to_col, 1.0, 0.0).astype(BF)
    for ref in (gw1, gw2t, gqf, gqt, gp, small):
        ref[...] = jnp.zeros_like(ref)
    for part in range(3):
        cols = slice(128 * part, 128 * part + 128)
        wf_ref[:, cols] = wq[:, 256 * part : 256 * part + 128]
        wt_ref[:, cols] = wq[:, 256 * part + 128 : 256 * part + 256]
    taps = [vec[CONV + i] for i in range(9)]
    taps_f = [z[:128] for z in taps]
    taps_t = [z[128:] for z in taps]

    spot = lax.broadcasted_iota(jnp.int32, (strip, 1), 0)
    grid_row = me * (strip // 16) + spot // 16
    grid_col = spot % 16

    def shares_of(image):
        inside = (
            (grid_row >= boxes[image, 0])
            & (grid_row < boxes[image, 1])
            & (grid_col >= boxes[image, 2])
            & (grid_col < boxes[image, 3])
        )
        return jnp.where(inside, 0.0, 0.7), jnp.where(inside, 1.0, 0.3)

    def home(c):
        return [(q, i, mine * q + pair * c + i) for q in range(shares) for i in range(pair)]

    def permute(value):
        whole = perm_ref[...]
        return jnp.concatenate(
            [dot(whole, value[256 * i : 256 * i + 256]).astype(BF) for i in range(pair)], axis=0
        )

    def keep(c, j):
        return jnp.concatenate(
            [jnp.full((strip, 1), drops[image, j].astype(F32) * 1.25) for _, _, image in home(c)], axis=0
        )

    def half(c, tall):
        refs = (qt, kt, vt, pt) if tall else (qf, kf, vf, pf)
        return dict(zip("qkvp", [r.at[c] for r in refs]))

    def mix(c, _):
        for q, i, image in home(c):
            own, other = shares_of(image)
            m = own * x_ref[image].astype(F32) + other * x_ref[partners[image]].astype(F32)
            mixed[image] = m
            u, _ = normalise(m)
            n1h[c, q, i] = (u * v(G1) + v(B1)).astype(BF)
        ex.send(N1, c, n1h, n1t)
        return 0

    def flat(c, _):
        qkv = dot(n1h[c].reshape(tokens, 256), wf_ref[...]).astype(BF)
        qf[c], kf[c], vf[c] = qkv[:, :128], qkv[:, 128:256], qkv[:, 256:]
        att_f[c] = attend_half(half(c, False), lm, taps_f, vec[CB : CB + 1, :128])
        return 0

    def tall(c, _):
        ex.receive(N1, c, n1h, n1t)
        n1 = permute(n1t[c].reshape(tokens, 256))
        n1p[c] = n1
        qkv = dot(n1, wt_ref[...]).astype(BF)
        qt[c], kt[c], vt[c] = qkv[:, :128], qkv[:, 128:256], qkv[:, 256:]
        att = attend_half(half(c, True), lm, taps_t, vec[CB : CB + 1, 128:])
        att_ts[c] = permute(att).reshape(att_ts.shape[1:])
        ex.send(AT, c, att_ts, att_th)
        return 0

    def mlp(c, _):
        ex.receive(AT, c, att_ts, att_th)
        keep1, keep2 = keep(c, 0), keep(c, 1)
        att = jnp.concatenate([att_f[c], att_th[c].reshape(tokens, 128)], axis=1)
        m = jnp.concatenate([mixed[image] for _, _, image in home(c)], axis=0)
        h1 = m + keep1 * (dot(att, wp[...]) + v(PB))
        u2, rstd2 = normalise(h1)
        n2 = (u2 * v(G2) + v(B2)).astype(BF)
        cot = jnp.concatenate([cot_ref[image] for _, _, image in home(c)], axis=0).astype(F32)
        db2 = (keep2 * cot).astype(BF)
        small[FB2] += sum8(db2.astype(F32))
        n2t = jnp.concatenate([n2.T, jnp.ones((16, tokens), BF)], axis=0)
        db2t = db2.T
        branch2 = jnp.zeros((tokens, 256), F32)
        dn2 = jnp.zeros((tokens, 256), F32)
        for f in range(w1.shape[1] // 256):
            fs = slice(256 * f, 256 * f + 256)
            act, slope = gelu_parts(dot(n2, w1[:, fs]) + v(FB1 + f))
            act = act.astype(BF)
            dpre = (slope * dot(db2, w2[fs, :], 1, 1)).astype(BF)
            branch2 = branch2 + dot(act, w2[fs, :])
            dn2 = dn2 + dot(dpre, w1[:, fs], 1, 1)
            gw1[:, fs] += dot(n2t, dpre)
            gw2t[:, fs] += dot(db2t, act)
        done = (h1 + keep2 * (branch2 + v(FB2))).astype(BF)
        for n, (_, _, image) in enumerate(home(c)):
            out[image] = done[strip * n : strip * n + strip]
        small[G2] += sum8(dn2 * u2)
        small[B2] += sum8(dn2)
        d = cot + normalise_back(dn2, u2, rstd2, v(G2))
        dh1[c] = d
        db1 = (keep1 * d).astype(BF)
        small[PB] += sum8(db1.astype(F32))
        gp[...] += dot(att, db1, 0, 0)
        datt = dot(db1, wp[...], 1, 1).astype(BF)
        da_f[c] = datt[:, :128]
        da_ts[c] = datt[:, 128:].reshape(da_ts.shape[1:])
        ex.send(DA, c, da_ts, da_tt)
        return 0

    def tall_back(c, _):
        ex.receive(DA, c, da_ts, da_tt)
        da = permute(da_tt[c].reshape(tokens, 128))
        s = dict(half(c, True), da=da)
        dqkv = attend_half_back(s, lm, taps_t, small, slice(128, 256))
        gqt[...] += dot(n1p[c], dqkv, 0, 0)
        dn_ts[c] = permute(dot(dqkv, wt_ref[...], 1, 1).astype(BF)).reshape(dn_ts.shape[1:])
        ex.send(DN, c, dn_ts, dn_th)
        return 0

    def flat_back(c, _):
        s = dict(half(c, False), da=da_f.at[c])
        dqkv = attend_half_back(s, lm, taps_f, small, slice(0, 128))
        gqf[...] += dot(n1h[c].reshape(tokens, 256), dqkv, 0, 0)
        dn1 = dot(dqkv, wf_ref[...], 1, 1)
        ex.receive(DN, c, dn_ts, dn_th)
        dn1 = dn1 + dn_th[c].reshape(tokens, 256).astype(F32)
        m = jnp.concatenate([mixed[image] for _, _, image in home(c)], axis=0)
        u1, rstd1 = normalise(m)
        small[G1] += sum8(dn1 * u1)
        small[B1] += sum8(dn1)
        d = dh1[c] + normalise_back(dn1, u1, rstd1, v(G1))
        for n, (_, _, image) in enumerate(home(c)):
            mixed[image] = d[strip * n : strip * n + strip]
        return 0

    def unmix(image, _):
        other = inverse[image]
        ig[image] = (shares_of(image)[0] * mixed[image] + shares_of(other)[1] * mixed[other]).astype(BF)
        return 0

    def both(first, second, lead):
        lax.fori_loop(0, lead, first, 0)

        def step(c, _):
            first(c + lead, 0)
            second(c, 0)
            return 0

        lax.fori_loop(0, chunks - lead, step, 0)
        lax.fori_loop(chunks - lead, chunks, second, 0)

    lax.fori_loop(0, chunks, mix, 0)
    lax.fori_loop(0, chunks, flat, 0)
    both(tall, mlp, ahead)
    both(tall_back, flat_back, ahead)
    lax.fori_loop(0, images, unmix, 0)

    def drain(c, _):
        for kind, src, dst in ((N1, n1h, n1t), (AT, att_ts, att_th), (DA, da_ts, da_tt), (DN, dn_ts, dn_th)):
            ex.sent(kind, c, src, dst)
        return 0

    lax.fori_loop(0, chunks, drain, 0)


def block(inputs, cotangent, boxes, drops, partners, inverse, vec, wq, wp, w1, w2, pair=2, ahead=2):
    images, grid_rows, side, width = inputs.shape
    shares = lax.axis_size("row")
    strip = grid_rows * side
    chunks = images // shares // pair
    tokens = shares * pair * strip
    hidden = w1.shape[1]
    sds = jax.ShapeDtypeStruct
    vmem = pl.BlockSpec(memory_space=pltpu.VMEM)
    smem = pl.BlockSpec(memory_space=pltpu.SMEM)
    x = inputs.reshape(images, strip, width)
    cot = cotangent.reshape(images, strip, width)
    rows = lambda ch, dt=BF: pltpu.VMEM((chunks, tokens, ch), dt)
    at_home = lambda ch: pltpu.VMEM((chunks, shares, pair, strip, ch), BF)
    at_tall = lambda ch: pltpu.VMEM((chunks, pair, shares, strip, ch), BF)
    return pl.pallas_call(
        functools.partial(block_kernel, shares, ahead),
        in_specs=[smem] * 4 + [vmem] * 7,
        out_specs=[vmem] * 8,
        out_shape=[
            sds(x.shape, BF),
            sds(x.shape, BF),
            sds((width + 16, hidden), F32),
            sds((width, hidden), F32),
            sds((width, 384), F32),
            sds((width, 384), F32),
            sds((width, width), F32),
            sds((16, 8, width), F32),
        ],
        scratch_shapes=[
            pltpu.VMEM((256, 256), BF),
            pltpu.VMEM((width, 384), BF),
            pltpu.VMEM((width, 384), BF),
            pltpu.VMEM(x.shape, F32),
            at_home(width),
            at_tall(width),
            rows(width),
        ]
        + [rows(128)] * 9
        + [at_tall(128), at_home(128), rows(width, F32), rows(128), at_home(128), at_tall(128), at_tall(width), at_home(width)]
        + [pltpu.SemaphoreType.DMA((4, chunks, shares - 1))] * 2,
        compiler_params=pltpu.CompilerParams(
            collective_id=0, has_side_effects=True, vmem_limit_bytes=62 * 2**20
        ),
    )(boxes, drops, partners, inverse, x, cot, vec, wq, wp, w1, w2)


def per_device(
    inputs,
    partners,
    boxes,
    drops,
    norm1_gain,
    norm1_bias,
    qkv_weight,
    lepe_weight,
    lepe_bias,
    proj_weight,
    proj_bias,
    norm2_gain,
    norm2_bias,
    fc1_weight,
    fc1_bias,
    fc2_weight,
    fc2_bias,
    cotangent,
):
    images = inputs.shape[0]
    ids = lax.axis_index("batch") * images + jnp.arange(images)
    inverse = jnp.sum(jnp.where(partners[:, None] == ids[None, :], jnp.arange(images)[:, None], 0), axis=0)
    wide = lambda z: z.astype(F32).reshape(-1, 256)
    taps = jnp.concatenate([lepe_weight[..., :128], lepe_weight.transpose(1, 0, 2)[..., 128:]], axis=-1)
    vec = jnp.concatenate(
        [wide(z) for z in (norm1_gain, norm1_bias, norm2_gain, norm2_bias, proj_bias, fc2_bias, lepe_bias, taps, fc1_bias)]
    )
    vec = jnp.pad(vec, ((0, -vec.shape[0] % 8), (0, 0)))
    out, ig, gw1, gw2t, gqf, gqt, gp, small = block(
        inputs, cotangent, boxes, drops, partners - lax.axis_index("batch") * images, inverse, vec, qkv_weight, proj_weight, fc1_weight, fc2_weight
    )
    small = jnp.sum(small, axis=1)
    gw1, gw2t, gqf, gqt, gp, small = lax.psum((gw1, gw2t, gqf, gqt, gp, small), ("batch", "row"))
    conv = small[CONV : CONV + 9].reshape(3, 3, 256)
    conv = jnp.concatenate([conv[..., :128], conv.transpose(1, 0, 2)[..., 128:]], axis=-1)
    gq = jnp.stack([gqf.reshape(256, 3, 128), gqt.reshape(256, 3, 128)], axis=2).reshape(256, 768)
    return (
        out.reshape(inputs.shape),
        ig.reshape(inputs.shape),
        small[G1],
        small[B1],
        gq,
        conv,
        small[CB],
        gp,
        small[PB],
        small[G2],
        small[B2],
        gw1[:256],
        gw1[256],
        gw2t.T,
        small[FB2],
    )


def solution(mesh):
    tokens = P("batch", "row", None, None)
    return jax.shard_map(
        per_device,
        mesh=mesh,
        in_specs=(tokens, P("batch"), P("batch", None), P("batch", None)) + (P(),) * 13 + (tokens,),
        out_specs=(tokens, tokens) + (P(),) * 13,
        check_vma=False,
    )
```

time: 474 us -> 314 us (0.66)
  waiting for transfers between devices: 147 us -> 100 us
  Pallas kernels: 174 us -> 128 us
  blocking collectives: 69.6 us -> 41.3 us
  starting transfers between devices: 15.6 us -> 0.04 us
  other arithmetic: 16.1 us -> 3.15 us
  local copies, waits for them, and re-layouts: 37.1 us -> 26.8 us
    all_to_all x4 -> x0, waiting for transfers between devices: 66.9 us -> none  [the longest x1 25.1 us: per_device(): lax.all_to_all(out.reshape(shape), 'row', split_axis=1, concat_axis=0, ti...]
    pallas_call x1, Pallas kernels: 174 us -> 128 us  [block(): pl.pallas_call(functools.partial(block_kernel, shares, ahead), in_specs=[...]
    psum x1, blocking collectives: 69.6 us -> 41.3 us  [per_device(): lax.psum((gw1, gw2t, gqf, gqt, gp, small), ('batch', 'row'))]
    psum x1, waiting for transfers between devices: 79.6 us -> 100 us  [per_device(): lax.psum((gw1, gw2t, gqf, gqt, gp, small), ('batch', 'row'))]
    all_to_all x4 -> x0, starting transfers between devices: 15.6 us -> none  [the longest x1 4.67 us: per_device(): lax.all_to_all(cotangent, 'row', split_axis=0, concat_axis=1, tiled=True)]
    convert_element_type x4 -> x0, other arithmetic: 11.3 us -> none  [the longest x1 5.36 us: per_device(): input_grad = (own_part + toward[inverse]).astype(BF)]
    all_to_all x3 -> x0, local copies, waits for them, and re-layouts: 8.36 us -> none  [the longest x1 3.43 us: per_device(): lax.all_to_all(out.reshape(shape), 'row', split_axis=1, concat_axis=0, ti...]
    gather x2 -> x0, local copies, waits for them, and re-layouts: 7.68 us -> none  [the longest x1 5.37 us: per_device(): input_grad = (own_part + toward[inverse]).astype(BF)]
  transfers between devices with their start and end apart: 5 -> 1, of which waited for: 4 -> 1; matrix products, arithmetic and copies ran while one was open for 6% -> 0% of each run, Pallas kernels for 0% -> 0%
where the time goes in v2:
time: 314 us
  Pallas kernels  128 us (41%)
  waiting for transfers between devices  100 us (32%)
  blocking collectives  41.3 us (13%)
  local copies, waits for them, and re-layouts  26.8 us (9%)
  between operations  14.1 us (4%)
  other arithmetic  3.15 us (1%)
    pallas_call x1, Pallas kernels, block(): pl.pallas_call(functools.partial(block_kernel, shares, ahead), in_specs=[...  128 us
    psum x1, waiting for transfers between devices, per_device(): lax.psum((gw1, gw2t, gqf, gqt, gp, small), ('batch', 'row'))  100 us
    psum x1, blocking collectives, per_device(): lax.psum((gw1, gw2t, gqf, gqt, gp, small), ('batch', 'row'))  41.3 us
    unnamed x21, local copies, waits for them, and re-layouts  11.7 us
  transfers between devices with their start and end apart: 1, of which 1 were waited for; matrix products, arithmetic and copies ran while one was open for 0% of the time, Pallas kernels for 0%

profile of v2, /device:TPU:0, one launch (start us, length us, event | category | flops | bytes accessed | tf_op | source)
XLA Modules:
  0.0 313.9 jit_solution(5062405563702271566)
XLA Ops:
  7.2 0.0 all-reduce.4.cloned.1.call-start
  7.2 1.2 iota_add_fusion
  8.4 1.3 select_reduce_fusion.inverse
  9.7 0.7 reshape.90
  10.3 0.7 reshape.91
  11.0 0.7 reshape.96
  11.6 0.7 reshape.94
  12.3 0.7 reshape.92
  12.9 0.7 reshape.93
  13.6 0.7 reshape.95
  14.3 0.7 reshape.97
  15.0 0.7 slice.42
  15.6 0.7 slice.56
  16.4 0.2 concatenate.18
  16.6 0.6 pad_convert_fusion.vec
  17.2 1.4 copy.58.boxes
  18.6 1.4 copy.59.drops
  20.0 128.2 %shard_map.289 = (bf16[72,64,256]{2,1,0:T(8,128)(2,1)}, bf16[72,64,256]{2,1,0:T(8,128)(2,1)}, f32[272,1024]{1,0:T(8,128)}, f32[256,1024]{1,0:T(8,128)}, f32[256,...) custom-call(s32[72,4]{1,0:T(8,128)} %copy.58.boxes, s32[72,2]{1,0:T(8,128)} %copy.59.drops, ...), custom_call_target="tpu_custom_call" | custom-call | tf_op jit(solution)/shard_map/pallas_call | solution.py:457
  148.2 0.0 copy-start.5
  148.2 1.9 copy.60
  150.2 1.9 copy.61
  152.1 0.0 all-reduce.4.cloned.1.call-update
  152.1 0.0 copy-done.5
  152.2 41.3 %psum.42 = f32[16,256]{1,0:T(8,128)S(1)} all-reduce(f32[16,256]{1,0:T(8,128)S(1)} %reduce_sum.19), channel_id=1, replica_groups=mesh['batch'=8,'row'=4] {'batch','row'}, use_global_device_ids=true, to_apply=%region_2.3 | all-reduce | flops 4096 | bytes 32768 | tf_op jit(solution)/shard_map/psum | solution.py:522
  193.6 0.6 copy.65
  194.2 0.6 fusion
  194.8 100.2 %all-reduce.4.cloned.1.call-done = (f32[256,3,1,128]{0,3,1,2:T(8,128)}, f32[256,3,1,128]{0,3,1,2:T(8,128)}, f32[256,256]{1,0:T(8,128)}, f32[272,1024]{1,0:T(8,128)}, f32[1024,256]{0,1:T(8,128)}) async-done(((f32[256,3,1,128]{0,3,1,2:T(8,128)}, f32[256,3,1,128]{0,3,1,2:T(8,128)}, f32[256,256]{1,0:T(8,128)}, f32[272,1024]{1,0:T(8,128)}, f32[1024,256]{0,1:T(8,128)}), (f32[256,3,1,128]{0,3,1,2:T(8,128)}, ...) | async-done | bytes 3211280 | tf_op jit(solution)/shard_map/psum | solution.py:522
  294.9 0.0 copy-start.2
  294.9 0.0 copy-start.3
  294.9 1.4 slice.67
  296.3 2.3 slice.66
  298.6 0.0 copy-done.2
  298.7 0.0 copy-done.3
  298.7 0.1 pad_maximum_fusion
  298.7 0.0 copy-start.1
  298.7 0.1 copy.62
  298.8 1.1 copy.64
  299.9 2.5 copy.66
  302.5 0.0 copy-done.1
  302.5 0.0 copy-start
  302.5 1.4 copy.76
  303.9 1.1 copy-done
  305.0 0.0 copy-start.4
  305.0 1.4 copy.77
  306.4 0.0 copy-done.4
  306.4 0.7 copy.78
  (11 shorter events, 0.1 us)
Async XLA Ops:
  7.2 287.7 %all-reduce.4.cloned.1.call-start = ((), (), s32[]{:S(2)}) async-start(), calls=%async_computation | async-start | bytes 6422528 | tf_op jit(solution)/shard_map/psum | solution.py:522
  148.2 3.9 %copy-start.5 = (f32[16,8,256]{2,1,0:T(8,128)S(1)}, f32[16,8,256]{2,1,0:T(8,128)}, u32[]{:S(2)}) copy-start(f32[16,8,256]{2,1,0:T(8,128)} %get-tuple-element.25) | copy-start | bytes 393220
  294.9 3.7 %copy-start.2 = (f32[256,3,1,128]{0,3,1,2:T(8,128)S(1)}, f32[256,3,1,128]{0,3,1,2:T(8,128)}, u32[]{:S(2)}) copy-start(f32[256,3,1,128]{0,3,1,2:T(8,128)} %get-tuple-element.91) | copy-start | bytes 1179652
  294.9 3.7 %copy-start.3 = (f32[256,3,1,128]{0,3,1,2:T(8,128)S(1)}, f32[256,3,1,128]{0,3,1,2:T(8,128)}, u32[]{:S(2)}) copy-start(f32[256,3,1,128]{0,3,1,2:T(8,128)} %get-tuple-element.92) | copy-start | bytes 1179652
  298.7 3.8 %copy-start.1 = (bf16[72,64,256]{2,1,0:T(8,128)(2,1)S(1)}, bf16[72,64,256]{2,1,0:T(8,128)(2,1)}, u32[]{:S(2)}) copy-start(bf16[72,64,256]{2,1,0:T(8,128)(2,1)} %get-tuple-element.23) | copy-start | bytes 7077892
  302.5 2.5 copy-start
  305.0 1.4 copy-start.4
Sparse Core Ops, SparseCore 0:
  152.2 142.6 all-reduce.3

commit v3 on v2

--- a/solution.py
+++ b/solution.py
@@ -205,26 +205,122 @@
             self.copy(kind, c, d, src, dst, False).wait_send()
 
 
+class Reduce:
+    def __init__(self, group, me, mb, shares, stage, whole, r1, r2, r3, z, send_sem, recv_sem):
+        self.whole = whole
+        self.group, self.me, self.mb, self.shares = group, me, mb, shares
+        self.stage, self.r1, self.r2, self.r3, self.z = stage, r1, r2, r3, z
+        self.send_sem, self.recv_sem = send_sem, recv_sem
+        self.core = lax.rem(me, 2)
+        self.batch = stage.shape[1]
+
+    def copy(self, slot, src, dst, device):
+        return pltpu.make_async_remote_copy(
+            src_ref=src,
+            dst_ref=dst,
+            send_sem=self.send_sem.at[self.group, slot],
+            recv_sem=self.recv_sem.at[self.group, slot],
+            device_id=device,
+            device_id_type=pl.DeviceIdType.MESH,
+        )
+
+    def near(self):
+        mate = {"row": self.me + 1 - 2 * self.core}
+        return self.copy(0, self.stage.at[1 - self.core], self.r1, mate)
+
+    def across(self):
+        return self.copy(1, self.z, self.r3, {"row": lax.rem(self.me + 2, self.shares)})
+
+    def back(self, arriving):
+        mate = {"row": self.me + 1 - 2 * self.core}
+        half = 1 - self.core if arriving else self.core
+        return self.copy(2, self.whole.at[self.core], self.whole.at[half], mate)
+
+    def peers(self, body):
+        def one(d, _):
+            body(d, lax.rem(self.mb + d, self.batch), lax.rem(self.mb + self.batch - d, self.batch))
+            return 0
+
+        lax.fori_loop(1, self.batch, one, 0)
+
+    def scatter(self, d, to, far):
+        return self.copy(2 + d, self.stage.at[self.core, to], self.r2.at[far], {"batch": to})
+
+    def gather(self, d, to, far):
+        return self.copy(1 + self.batch + d, self.whole.at[self.core, self.mb], self.whole.at[self.core, far], {"batch": to})
+
+    def step(self, n):
+        core, mb = self.core, self.mb
+        if n == 0:
+            self.near().start()
+        if n == 1:
+            self.near().wait_recv()
+
+            def add(b, _):
+                self.stage[core, b] = (self.stage[core, b].astype(F32) + self.r1[b].astype(F32)).astype(BF)
+                return 0
+
+            lax.fori_loop(0, self.batch, add, 0)
+            self.peers(lambda d, to, far: self.scatter(d, to, mb).start())
+        if n == 2:
+            self.peers(lambda d, to, far: self.scatter(d, to, far).wait_recv())
+
+            def more(d, total):
+                return total + self.r2[lax.rem(mb + d, self.batch)].astype(F32)
+
+            self.z[...] = lax.fori_loop(1, self.batch, more, self.stage[core, mb].astype(F32)).astype(BF)
+            self.across().start()
+        if n == 3:
+            self.across().wait_recv()
+            self.whole[core, mb] = (self.z[...].astype(F32) + self.r3[...].astype(F32)).astype(BF)
+            self.peers(lambda d, to, far: self.gather(d, to, mb).start())
+        if n == 4:
+            self.peers(lambda d, to, far: self.gather(d, to, far).wait_recv())
+            self.back(False).start()
+        if n == 5:
+            self.back(True).wait_recv()
+            self.near().wait_send()
+            self.across().wait_send()
+            self.back(False).wait_send()
+            self.peers(lambda d, to, far: self.scatter(d, to, mb).wait_send())
+            self.peers(lambda d, to, far: self.gather(d, to, mb).wait_send())
+
+
 def block_kernel(
     shares,
     ahead,
-    boxes,
-    drops,
-    partners,
-    inverse,
+    boxes_ref,
+    drops_ref,
+    index_ref,
     x_ref,
     cot_ref,
-    vec,
+    norm1_gain,
+    norm1_bias,
+    norm2_gain,
+    norm2_bias,
+    proj_bias,
+    fc2_bias,
+    lepe_bias,
+    lepe_weight,
+    fc1_bias,
     wq,
     wp,
     w1,
     w2,
     out,
     ig,
+    whole1,
+    whole2,
+    stage1,
+    stage2,
+    boxes,
+    drops,
+    index,
+    vec,
     gw1,
+    gb1,
     gw2t,
-    gqf,
-    gqt,
+    gq,
     gp,
     small,
     perm_ref,
@@ -251,8 +347,20 @@
     da_tt,
     dn_ts,
     dn_th,
+    r11,
+    r12,
+    r13,
+    z1,
+    r21,
+    r22,
+    r23,
+    z2,
     send_sem,
     recv_sem,
+    sum_send,
+    sum_recv,
+    load_sem,
+    store_sem,
 ):
     chunks, _, pair, strip = n1h.shape[:4]
     images = x_ref.shape[0]
@@ -261,13 +369,44 @@
     me = lax.axis_index("row")
     ex = Exchange(me, shares, send_sem, recv_sem)
 
+    mb = lax.axis_index("batch")
+    batch = stage1.shape[1]
+    red1 = Reduce(0, me, mb, shares, stage1, whole1, r11, r12, r13, z1, sum_send, sum_recv)
+    red2 = Reduce(1, me, mb, shares, stage2, whole2, r21, r22, r23, z2, sum_send, sum_recv)
+
+    loads = [
+        pltpu.make_async_copy(src, dst, load_sem.at[n])
+        for n, (src, dst) in enumerate(((boxes_ref, boxes), (drops_ref, drops), (index_ref, index)))
+    ]
+    for load in loads:
+        load.start()
     barrier = pltpu.get_barrier_semaphore()
     for d in range(1, shares):
         pl.semaphore_signal(
             barrier, inc=1, device_id={"row": lax.rem(me + d, shares)}, device_id_type=pl.DeviceIdType.MESH
         )
-    pl.semaphore_wait(barrier, shares - 1)
-
+
+    def greet(d, _):
+        pl.semaphore_signal(
+            barrier, inc=1, device_id={"batch": lax.rem(mb + d, batch)}, device_id_type=pl.DeviceIdType.MESH
+        )
+        return 0
+
+    lax.fori_loop(1, batch, greet, 0)
+    pl.semaphore_wait(barrier, shares + batch - 2)
+    for load in loads:
+        load.wait()
+
+    params = (norm1_gain, norm1_bias, norm2_gain, norm2_bias, proj_bias, fc2_bias, lepe_bias)
+    for n, ref in enumerate(params):
+        vec[n : n + 1] = ref[...].astype(F32).reshape(1, 256)
+    for i in range(3):
+        for j in range(3):
+            n = CONV + 3 * i + j
+            vec[n : n + 1, :128] = lepe_weight[i, j : j + 1, :128].astype(F32)
+            vec[n : n + 1, 128:] = lepe_weight[j, i : i + 1, 128:].astype(F32)
+    for n in range(4):
+        vec[FB1 + n : FB1 + n + 1] = fc1_bias[256 * n : 256 * n + 256].astype(F32).reshape(1, 256)
     v = lambda i: vec[i : i + 1]
     lm = (
         lax.broadcasted_iota(jnp.int32, (8, 128), 0) == lax.broadcasted_iota(jnp.int32, (8, 128), 1) // 32
@@ -275,7 +414,7 @@
     to_row = lax.broadcasted_iota(jnp.int32, (256, 256), 0)
     to_col = lax.broadcasted_iota(jnp.int32, (256, 256), 1)
     perm_ref[...] = jnp.where((to_row % 16) * 16 + to_row // 16 == to_col, 1.0, 0.0).astype(BF)
-    for ref in (gw1, gw2t, gqf, gqt, gp, small):
+    for ref in (gw1, gb1, gw2t, gq, gp, small):
         ref[...] = jnp.zeros_like(ref)
     for part in range(3):
         cols = slice(128 * part, 128 * part + 128)
@@ -319,7 +458,7 @@
     def mix(c, _):
         for q, i, image in home(c):
             own, other = shares_of(image)
-            m = own * x_ref[image].astype(F32) + other * x_ref[partners[image]].astype(F32)
+            m = own * x_ref[image].astype(F32) + other * x_ref[index[0, image]].astype(F32)
             mixed[image] = m
             u, _ = normalise(m)
             n1h[c, q, i] = (u * v(G1) + v(B1)).astype(BF)
@@ -365,7 +504,9 @@
             dpre = (slope * dot(db2, w2[fs, :], 1, 1)).astype(BF)
             branch2 = branch2 + dot(act, w2[fs, :])
             dn2 = dn2 + dot(dpre, w1[:, fs], 1, 1)
-            gw1[:, fs] += dot(n2t, dpre)
+            grad = dot(n2t, dpre)
+            gw1[:, fs] += grad[:256]
+            gb1[:, fs] += grad[256:]
             gw2t[:, fs] += dot(db2t, act)
         done = (h1 + keep2 * (branch2 + v(FB2))).astype(BF)
         for n, (_, _, image) in enumerate(home(c)):
@@ -383,12 +524,51 @@
         ex.send(DA, c, da_ts, da_tt)
         return 0
 
+    def add_qkv(grad, start):
+        for part in range(3):
+            cols = slice(256 * part + start, 256 * part + start + 128)
+            gq[:, cols] += grad[:, 128 * part : 128 * part + 128]
+
+    def put(stage, blocks):
+        rows = stage.shape[2]
+        spot = 0
+        for value in blocks:
+            done = 0
+            while done < value.shape[0]:
+                piece, at = divmod(spot, rows)
+                n = min(rows - at, value.shape[0] - done)
+                stage[piece // batch, piece % batch, at : at + n] = value[done : done + n]
+                done += n
+                spot += n
+        while spot < 2 * batch * rows:
+            piece, at = divmod(spot, rows)
+            stage[piece // batch, piece % batch, at:] = jnp.zeros((rows - at, 256), BF)
+            spot += rows - at
+
+    def pack1():
+        quarters = [slice(256 * f, 256 * f + 256) for f in range(w1.shape[1] // 256)]
+        blocks = [gw1[:, fs].astype(BF) for fs in quarters]
+        blocks += [gw2t[:, fs].astype(BF).T for fs in quarters]
+        put(stage1, blocks + [gp[...].astype(BF)])
+
+    def pack2():
+        blocks = [gq[:, 256 * n : 256 * n + 256].astype(BF) for n in range(3)]
+        row = lambda i: jnp.sum(small[i], axis=0, keepdims=True)
+        rows = [row(i) for i in range(CONV)]
+        conv = [row(CONV + i) for i in range(9)]
+        for i in range(3):
+            for j in range(3):
+                rows.append(jnp.concatenate([conv[3 * i + j][:, :128], conv[3 * j + i][:, 128:]], axis=1))
+        rows += [gb1[0:1, 256 * f : 256 * f + 256] for f in range(w1.shape[1] // 256)]
+        rows.append(jnp.zeros((32 - len(rows), 256), F32))
+        put(stage2, blocks + [jnp.concatenate(rows, axis=0).astype(BF)])
+
     def tall_back(c, _):
         ex.receive(DA, c, da_ts, da_tt)
         da = permute(da_tt[c].reshape(tokens, 128))
         s = dict(half(c, True), da=da)
         dqkv = attend_half_back(s, lm, taps_t, small, slice(128, 256))
-        gqt[...] += dot(n1p[c], dqkv, 0, 0)
+        add_qkv(dot(n1p[c], dqkv, 0, 0), 128)
         dn_ts[c] = permute(dot(dqkv, wt_ref[...], 1, 1).astype(BF)).reshape(dn_ts.shape[1:])
         ex.send(DN, c, dn_ts, dn_th)
         return 0
@@ -396,7 +576,7 @@
     def flat_back(c, _):
         s = dict(half(c, False), da=da_f.at[c])
         dqkv = attend_half_back(s, lm, taps_f, small, slice(0, 128))
-        gqf[...] += dot(n1h[c].reshape(tokens, 256), dqkv, 0, 0)
+        add_qkv(dot(n1h[c].reshape(tokens, 256), dqkv, 0, 0), 0)
         dn1 = dot(dqkv, wf_ref[...], 1, 1)
         ex.receive(DN, c, dn_ts, dn_th)
         dn1 = dn1 + dn_th[c].reshape(tokens, 256).astype(F32)
@@ -409,66 +589,120 @@
             mixed[image] = d[strip * n : strip * n + strip]
         return 0
 
-    def unmix(image, _):
-        other = inverse[image]
-        ig[image] = (shares_of(image)[0] * mixed[image] + shares_of(other)[1] * mixed[other]).astype(BF)
-        return 0
-
-    def both(first, second, lead):
-        lax.fori_loop(0, lead, first, 0)
-
-        def step(c, _):
-            first(c + lead, 0)
-            second(c, 0)
-            return 0
-
-        lax.fori_loop(0, chunks - lead, step, 0)
-        lax.fori_loop(chunks - lead, chunks, second, 0)
+    def stores(c):
+        return [
+            pltpu.make_async_copy(n1h.at[c, q], ig.at[pl.ds(mine * q + pair * c, pair)], store_sem.at[c, q])
+            for q in range(shares)
+        ]
+
+    def unmix(c, _):
+        ex.sent(N1, c, n1h, n1t)
+        for q, i, image in home(c):
+            other = index[1, image]
+            n1h[c, q, i] = (shares_of(image)[0] * mixed[image] + shares_of(other)[1] * mixed[other]).astype(BF)
+        for store in stores(c):
+            store.start()
+        return 0
 
     lax.fori_loop(0, chunks, mix, 0)
     lax.fori_loop(0, chunks, flat, 0)
-    both(tall, mlp, ahead)
-    both(tall_back, flat_back, ahead)
-    lax.fori_loop(0, images, unmix, 0)
+    lax.fori_loop(0, ahead, tall, 0)
+
+    def forward(c, _):
+        @pl.when(c < chunks - ahead)
+        def _():
+            tall(c + ahead, 0)
+
+        mlp(c, 0)
+        return 0
+
+    lax.fori_loop(0, chunks, forward, 0)
+    pack1()
+    red1.step(0)
+    lax.fori_loop(0, ahead, tall_back, 0)
+    red1.step(1)
+
+    def backward(c, _):
+        @pl.when(c < chunks - ahead)
+        def _():
+            tall_back(c + ahead, 0)
+
+        flat_back(c, 0)
+        for n, at in ((2, chunks // 2), (3, chunks // 2 + 1)):
+
+            @pl.when(c == at)
+            def _():
+                red1.step(n)
+
+        return 0
+
+    lax.fori_loop(0, chunks, backward, 0)
+    pack2()
+    red2.step(0)
+    red1.step(4)
+    red2.step(1)
+    lax.fori_loop(0, chunks, unmix, 0)
+    red2.step(2)
+    red1.step(5)
+    red2.step(3)
+    red2.step(4)
+    red2.step(5)
 
     def drain(c, _):
-        for kind, src, dst in ((N1, n1h, n1t), (AT, att_ts, att_th), (DA, da_ts, da_tt), (DN, dn_ts, dn_th)):
+        for kind, src, dst in ((AT, att_ts, att_th), (DA, da_ts, da_tt), (DN, dn_ts, dn_th)):
             ex.sent(kind, c, src, dst)
+        for store in stores(c):
+            store.wait()
         return 0
 
     lax.fori_loop(0, chunks, drain, 0)
 
 
-def block(inputs, cotangent, boxes, drops, partners, inverse, vec, wq, wp, w1, w2, pair=2, ahead=2):
+def share_rows(rows, batch):
+    return -(-rows // (2 * batch * 16)) * 16
+
+
+def block(inputs, cotangent, boxes, drops, index, vectors, weights, pair=2, ahead=2):
     images, grid_rows, side, width = inputs.shape
-    shares = lax.axis_size("row")
+    shares, batch = lax.axis_size("row"), lax.axis_size("batch")
     strip = grid_rows * side
     chunks = images // shares // pair
     tokens = shares * pair * strip
-    hidden = w1.shape[1]
+    hidden = weights[2].shape[1]
     sds = jax.ShapeDtypeStruct
     vmem = pl.BlockSpec(memory_space=pltpu.VMEM)
-    smem = pl.BlockSpec(memory_space=pltpu.SMEM)
+    hbm = pl.BlockSpec(memory_space=pl.ANY)
     x = inputs.reshape(images, strip, width)
     cot = cotangent.reshape(images, strip, width)
+    n1 = share_rows(2 * hidden + width, batch)
+    n2 = share_rows(3 * width + 32, batch)
     rows = lambda ch, dt=BF: pltpu.VMEM((chunks, tokens, ch), dt)
     at_home = lambda ch: pltpu.VMEM((chunks, shares, pair, strip, ch), BF)
     at_tall = lambda ch: pltpu.VMEM((chunks, pair, shares, strip, ch), BF)
+    part = lambda n, *lead: pltpu.VMEM((*lead, n, width), BF)
     return pl.pallas_call(
         functools.partial(block_kernel, shares, ahead),
-        in_specs=[smem] * 4 + [vmem] * 7,
-        out_specs=[vmem] * 8,
+        in_specs=[hbm] * 3 + [vmem] * (2 + len(vectors) + len(weights)),
+        out_specs=[vmem, hbm, vmem, vmem],
         out_shape=[
             sds(x.shape, BF),
             sds(x.shape, BF),
-            sds((width + 16, hidden), F32),
-            sds((width, hidden), F32),
-            sds((width, 384), F32),
-            sds((width, 384), F32),
-            sds((width, width), F32),
-            sds((16, 8, width), F32),
+            sds((2, batch, n1, width), BF),
+            sds((2, batch, n2, width), BF),
         ],
         scratch_shapes=[
+            pltpu.VMEM((2, batch, n1, width), BF),
+            pltpu.VMEM((2, batch, n2, width), BF),
+            pltpu.SMEM(boxes.shape, jnp.int32),
+            pltpu.SMEM(drops.shape, jnp.int32),
+            pltpu.SMEM(index.shape, jnp.int32),
+            pltpu.VMEM((24, width), F32),
+            pltpu.VMEM((width, hidden), F32),
+            pltpu.VMEM((16, hidden), F32),
+            pltpu.VMEM((width, hidden), F32),
+            pltpu.VMEM((width, 3 * width), F32),
+            pltpu.VMEM((width, width), F32),
+            pltpu.VMEM((16, 8, width), F32),
             pltpu.VMEM((256, 256), BF),
             pltpu.VMEM((width, 384), BF),
             pltpu.VMEM((width, 384), BF),
@@ -479,11 +713,72 @@
         ]
         + [rows(128)] * 9
         + [at_tall(128), at_home(128), rows(width, F32), rows(128), at_home(128), at_tall(128), at_tall(width), at_home(width)]
-        + [pltpu.SemaphoreType.DMA((4, chunks, shares - 1))] * 2,
+        + [part(n1, batch), part(n1, batch), part(n1), part(n1)]
+        + [part(n2, batch), part(n2, batch), part(n2), part(n2)]
+        + [pltpu.SemaphoreType.DMA((4, chunks, shares - 1))] * 2
+        + [pltpu.SemaphoreType.DMA((2, 2 * batch + 1))] * 2
+        + [pltpu.SemaphoreType.DMA((3,)), pltpu.SemaphoreType.DMA((chunks, shares))],
         compiler_params=pltpu.CompilerParams(
-            collective_id=0, has_side_effects=True, vmem_limit_bytes=62 * 2**20
+            collective_id=0, has_side_effects=True, vmem_limit_bytes=63 * 2**20
         ),
-    )(boxes, drops, partners, inverse, x, cot, vec, wq, wp, w1, w2)
+    )(boxes, drops, index, x, cot, *vectors, *weights)
+
+
+def finish_kernel(
+    out_ref, ig_ref, sum1, sum2, out, ig, g1, b1, gq, conv, cb, gp, pb, g2, b2, gw1, fb1, gw2, fb2, sems
+):
+    copies = [pltpu.make_async_copy(out_ref, out, sems.at[0]), pltpu.make_async_copy(ig_ref, ig, sems.at[1])]
+    for copy in copies:
+        copy.start()
+    hidden = gw1.shape[1]
+    for f in range(hidden // 256):
+        gw1[:, 256 * f : 256 * f + 256] = sum1[256 * f : 256 * f + 256].astype(F32)
+    gw2[...] = sum1[hidden : 2 * hidden].astype(F32)
+    gp[...] = sum1[2 * hidden : 2 * hidden + 256].astype(F32)
+    for f in range(3):
+        gq[:, 256 * f : 256 * f + 256] = sum2[256 * f : 256 * f + 256].astype(F32)
+    rows = sum2[768:800].astype(F32)
+    for n, ref in ((G1, g1), (B1, b1), (G2, g2), (B2, b2), (PB, pb), (FB2, fb2), (CB, cb)):
+        ref[...] = rows[n]
+    for i in range(3):
+        for j in range(3):
+            conv[i, j] = rows[CONV + 3 * i + j]
+    for f in range(hidden // 256):
+        fb1[256 * f : 256 * f + 256] = rows[FB1 + f]
+    for copy in copies:
+        copy.wait()
+
+
+def finish(out, ig, sum1, sum2, hidden):
+    width = out.shape[-1]
+    sds = jax.ShapeDtypeStruct
+    vmem = pl.BlockSpec(memory_space=pltpu.VMEM)
+    hbm = pl.BlockSpec(memory_space=pl.ANY)
+    flat = lambda n: sds((n,), F32)
+    square = lambda *n: sds(n, F32)
+    shapes = [
+        flat(width),
+        flat(width),
+        square(width, 3 * width),
+        square(3, 3, width),
+        flat(width),
+        square(width, width),
+        flat(width),
+        flat(width),
+        flat(width),
+        square(width, hidden),
+        flat(hidden),
+        square(hidden, width),
+        flat(width),
+    ]
+    return pl.pallas_call(
+        finish_kernel,
+        in_specs=[hbm, hbm, vmem, vmem],
+        out_specs=[hbm, hbm] + [vmem] * len(shapes),
+        out_shape=[sds(out.shape, BF), sds(ig.shape, BF)] + shapes,
+        scratch_shapes=[pltpu.SemaphoreType.DMA((2,))],
+        compiler_params=pltpu.CompilerParams(vmem_limit_bytes=32 * 2**20),
+    )(out, ig, sum1.reshape(-1, width), sum2.reshape(-1, width))
 
 
 def per_device(
@@ -507,39 +802,15 @@
     cotangent,
 ):
     images = inputs.shape[0]
-    ids = lax.axis_index("batch") * images + jnp.arange(images)
-    inverse = jnp.sum(jnp.where(partners[:, None] == ids[None, :], jnp.arange(images)[:, None], 0), axis=0)
-    wide = lambda z: z.astype(F32).reshape(-1, 256)
-    taps = jnp.concatenate([lepe_weight[..., :128], lepe_weight.transpose(1, 0, 2)[..., 128:]], axis=-1)
-    vec = jnp.concatenate(
-        [wide(z) for z in (norm1_gain, norm1_bias, norm2_gain, norm2_bias, proj_bias, fc2_bias, lepe_bias, taps, fc1_bias)]
-    )
-    vec = jnp.pad(vec, ((0, -vec.shape[0] % 8), (0, 0)))
-    out, ig, gw1, gw2t, gqf, gqt, gp, small = block(
-        inputs, cotangent, boxes, drops, partners - lax.axis_index("batch") * images, inverse, vec, qkv_weight, proj_weight, fc1_weight, fc2_weight
-    )
-    small = jnp.sum(small, axis=1)
-    gw1, gw2t, gqf, gqt, gp, small = lax.psum((gw1, gw2t, gqf, gqt, gp, small), ("batch", "row"))
-    conv = small[CONV : CONV + 9].reshape(3, 3, 256)
-    conv = jnp.concatenate([conv[..., :128], conv.transpose(1, 0, 2)[..., 128:]], axis=-1)
-    gq = jnp.stack([gqf.reshape(256, 3, 128), gqt.reshape(256, 3, 128)], axis=2).reshape(256, 768)
-    return (
-        out.reshape(inputs.shape),
-        ig.reshape(inputs.shape),
-        small[G1],
-        small[B1],
-        gq,
-        conv,
-        small[CB],
-        gp,
-        small[PB],
-        small[G2],
-        small[B2],
-        gw1[:256],
-        gw1[256],
-        gw2t.T,
-        small[FB2],
-    )
+    ids = jnp.arange(images)
+    local = partners - lax.axis_index("batch") * images
+    inverse = jnp.sum(jnp.where(local[:, None] == ids[None, :], ids[:, None], 0), axis=0)
+    index = jnp.stack([local, inverse])
+    vectors = (norm1_gain, norm1_bias, norm2_gain, norm2_bias, proj_bias, fc2_bias, lepe_bias, lepe_weight, fc1_bias)
+    weights = (qkv_weight, proj_weight, fc1_weight, fc2_weight)
+    out, ig, sum1, sum2 = block(inputs, cotangent, boxes, drops, index, vectors, weights)
+    out, ig, *grads = finish(out, ig, sum1, sum2, fc1_weight.shape[1])
+    return (out.reshape(inputs.shape), ig.reshape(inputs.shape), *grads)
 
 
 def solution(mesh):

time: 314 us -> 170 us (0.54)
  waiting for transfers between devices: 100 us -> 0 us
  blocking collectives: 41.3 us -> 0 us
  Pallas kernels: 128 us -> 158 us
  local copies, waits for them, and re-layouts: 26.8 us -> 8.41 us
  between operations: 14.1 us -> 0.83 us
    psum x1 -> x0, waiting for transfers between devices: 100 us -> none  [per_device(): lax.psum((gw1, gw2t, gqf, gqt, gp, small), ('batch', 'row'))]
    psum x1 -> x0, blocking collectives: 41.3 us -> none  [per_device(): lax.psum((gw1, gw2t, gqf, gqt, gp, small), ('batch', 'row'))]
    pallas_call x1, Pallas kernels: 128 us -> 154 us  [block(): pl.pallas_call(functools.partial(block_kernel, shares, ahead), in_specs=[...]
    slice x9 -> x0, local copies, waits for them, and re-layouts: 5.72 us -> none  [the longest x1 2.31 us: per_device(): gw1[:256]]
    reshape x9 -> x0, local copies, waits for them, and re-layouts: 5.31 us -> none  [the longest x8 5.3 us: per_device(): wide = lambda z: z.astype(F32).reshape(-1, 256)]
    pallas_call x0 -> x1, Pallas kernels: none -> 3.88 us  [finish(): pl.pallas_call(finish_kernel, in_specs=[hbm, hbm, vmem, vmem], out_specs=...]
    pallas_call x2 -> x0, local copies, waits for them, and re-layouts: 3.85 us -> none  [block(): pl.pallas_call(functools.partial(block_kernel, shares, ahead), in_specs=[...]
    unnamed x21 -> x10, local copies, waits for them, and re-layouts: 11.7 us -> 8.41 us
  transfers between devices with their start and end apart: 1 -> 0, of which waited for: 1 -> 0; matrix products, arithmetic and copies ran while one was open for 0% -> 0% of each run, Pallas kernels for 0% -> 0%
where the time goes in v3:
time: 170 us; the launch traced here: 169 us
  Pallas kernels  158 us (93%)
  local copies, waits for them, and re-layouts  8.41 us (5%)
  other arithmetic  1.99 us (1%)
    pallas_call x1, Pallas kernels, block(): pl.pallas_call(functools.partial(block_kernel, shares, ahead), in_specs=[...  154 us
    unnamed x10, local copies, waits for them, and re-layouts  8.41 us
    pallas_call x1, Pallas kernels, finish(): pl.pallas_call(finish_kernel, in_specs=[hbm, hbm, vmem, vmem], out_specs=...  3.88 us

profile of v3, /device:TPU:0, one launch (start us, length us, event | category | flops | bytes accessed | tf_op | source)
XLA Modules:
  0.0 168.9 jit_solution(8794865342948823034)
XLA Ops:
  0.6 0.7 fusion
  1.3 0.7 broadcast_subtract_fusion
  2.0 0.1 select_reduce_fusion
  2.1 0.6 pad_add_fusion.index_ref
  2.6 1.4 copy.35.boxes_ref
  4.0 1.4 copy.36.drops_ref
  5.4 153.8 %shard_map.289 = (bf16[72,64,256]{2,1,0:T(8,128)(2,1)}, bf16[72,64,256]{2,1,0:T(8,128)(2,1)}, bf16[2,8,144,256]{3,2,1,0:T(8,128)(2,1)}, bf16[2,8,64,256]{3,2,1,0:T(8,128)(2,1)}) custom-call(s32[72,4]{1,0:T(8,128)} %copy.35.boxes_ref, s32[72,2]{1,0:T(8,128)} %copy.36.drops_ref, s32[2,72]{1,0:T(2,128)} %pad_add_fusion.index_ref, ...), custom_call_target="tpu_custom_call" | custom-call | tf_op jit(solution)/shard_map/pallas_call | solution.py:683
  159.2 0.0 copy-start
  159.2 1.7 copy-done
  160.9 0.0 copy-start.1
  160.9 1.7 copy-done.1
  162.6 0.0 copy-start.2
  162.6 1.3 copy-done.2
  163.8 0.0 copy-start.3
  163.8 1.0 copy-done.3
  164.9 3.9 %shard_map.290 = (bf16[72,64,256]{2,1,0:T(8,128)(2,1)}, bf16[72,64,256]{2,1,0:T(8,128)(2,1)}, f32[256]{0:T(256)}, f32[256]{0:T(256)}, f32[256,768]{1,0:T(8,128)}...) custom-call(bf16[72,64,256]{2,1,0:T(8,128)(2,1)S(1)} %copy-done, ...), custom_call_target="tpu_custom_call" | custom-call | tf_op jit(solution)/shard_map/pallas_call | solution.py:774
Async XLA Ops:
  159.2 1.7 copy-start
  160.9 1.7 copy-start.1
  162.6 1.3 copy-start.2
  163.8 1.0 copy-start.3

commit v4 on v3

--- a/solution.py
+++ b/solution.py
@@ -13,8 +13,8 @@
 EPS = 1e-5
 SCALE = 32**-0.5
 LOG2E = math.log2(math.e)
-ERF_P = 0.3275911 / math.sqrt(2.0)
-ERF_C = [0.5 * c for c in (0.254829592, -0.284496736, 1.421413741, -1.453152027, 1.061405429)]
+SLOPE = 2.0 / math.sqrt(math.pi)
+ROOT_HALF = math.sqrt(0.5)
 G1, B1, G2, B2, PB, FB2, CB, CONV, FB1 = 0, 1, 2, 3, 4, 5, 6, 7, 16
 N1, AT, DA, DN = 0, 1, 2, 3
 
@@ -23,15 +23,10 @@
     return lax.dot_general(a, b, (((ca,), (cb,)), ((), ())), preferred_element_type=F32)
 
 
-def gelu_parts(v):
-    t = 1.0 / (1.0 + ERF_P * jnp.abs(v))
-    e = jnp.exp2(v * v * (-0.5 * LOG2E))
-    poly = ERF_C[4]
-    for c in ERF_C[3::-1]:
-        poly = poly * t + c
-    h = poly * t * e
-    cdf = jnp.where(v >= 0.0, 1.0 - h, h)
-    return v * cdf, cdf + v * (e * (1.0 / math.sqrt(2.0 * math.pi)))
+def gelu_twice(v):
+    w = v * ROOT_HALF
+    up = 1.0 + lax.erf(w)
+    return v * up, up + (w * jnp.exp2(w * w * -LOG2E)) * SLOPE
 
 
 def normalise(x):
@@ -52,59 +47,91 @@
     return jnp.sum(x.reshape(n // 8, 8, c), axis=0)
 
 
-def split_heads(w, lm):
-    return [w * lm[h : h + 1] for h in range(4)]
-
-
-def skewed(parts, w):
-    return jnp.concatenate([parts[j ^ w] for j in range(4)], axis=0)
-
-
-def stacked(parts, j):
-    return jnp.concatenate([parts[w][j ^ w] for w in range(4)], axis=0)
-
-
-def unskew(o, w, lane):
-    r = o[w]
-    for h in (1, 2, 3):
-        r = jnp.where(lane >= 32 * h, o[h ^ w], r)
-    return r
-
-
 def four(x):
     return [x[32 * w : 32 * w + 32] for w in range(4)]
 
 
-def attend_group(q, k, v, lm, lane):
-    ps = []
-    for w, (qw, kw) in enumerate(zip(four(q), four(k))):
-        st = dot(kw, skewed(split_heads(qw, lm), w), 1, 1)
-        top = jnp.max(st, axis=0, keepdims=True)
-        e = jnp.exp2((st - top) * (SCALE * LOG2E))
-        ps.append((e * (1.0 / jnp.sum(e, axis=0, keepdims=True))).astype(BF))
-    p = jnp.concatenate(ps, axis=0)
-    pt = four(p.T)
-    vh = [split_heads(vw, lm) for vw in four(v)]
-    o = [dot(pt[j], stacked(vh, j)) for j in range(4)]
-    return p, jnp.concatenate([unskew(o, w, lane) for w in range(4)], axis=0)
-
-
-def attend_group_back(q, k, v, p, da, lm, lane):
-    dss, dks, dvs = [], [], []
-    for w, (qw, vw, pw, dw) in enumerate(zip(four(q), four(v), four(p), four(da))):
-        dx = skewed(split_heads(dw, lm), w)
-        dp = dot(vw, dx, 1, 1)
-        pr = pw.astype(F32)
-        t = pr * dp
-        ds = (t - pr * jnp.sum(t, axis=0, keepdims=True)).astype(BF)
-        dss.append(ds)
-        dvs.append(dot(pw, dx))
-        dks.append(dot(ds, skewed(split_heads(qw, lm), w)))
-    dst = four(jnp.concatenate(dss, axis=0).T)
-    kh = [split_heads(kw, lm) for kw in four(k)]
-    o = [dot(dst[j], stacked(kh, j)) for j in range(4)]
-    dq = jnp.concatenate([unskew(o, w, lane) for w in range(4)], axis=0)
-    return dq, jnp.concatenate(dks, axis=0), jnp.concatenate(dvs, axis=0)
+def masked(x, j, lm):
+    return jnp.concatenate([r * lm[b ^ j : (b ^ j) + 1] for b, r in enumerate(four(x))], axis=0)
+
+
+def spread(x, w, lm):
+    return jnp.concatenate([x * lm[j ^ w : (j ^ w) + 1] for j in range(4)], axis=0)
+
+
+def weave(parts, j, lane):
+    r = parts[j]
+    for h in (1, 2, 3):
+        r = jnp.where(lane >= 32 * h, parts[h ^ j], r)
+    return r
+
+
+def two_dots(a, b):
+    r = dot(jnp.concatenate(a, axis=0), jnp.concatenate(b, axis=1))
+    n, m = a[0].shape[0], b[0].shape[1]
+    return r[:n, :m], r[n:, m:]
+
+
+def attend_groups(q, k, v, lm, lane):
+    n = range(len(q))
+    pairs = range(0, len(q), 2)
+    qt = [x.T for x in q]
+    k4, v4 = [four(x) for x in k], [four(x) for x in v]
+    st = [[None] * 4 for _ in n]
+    for j in range(4):
+        for g in pairs:
+            st[g][j], st[g + 1][j] = two_dots(
+                [weave(x, j, lane) for x in k4[g : g + 2]], [masked(x, j, lm) for x in qt[g : g + 2]]
+            )
+    p = [[] for _ in n]
+    for g in n:
+        for s in st[g]:
+            top = jnp.max(s, axis=0, keepdims=True)
+            e = jnp.exp2((s - top) * (SCALE * LOG2E))
+            p[g].append((e * (1.0 / jnp.sum(e, axis=0, keepdims=True))).astype(BF))
+    p = [jnp.concatenate(x, axis=0) for x in p]
+    pt = [four(x.T) for x in p]
+    o = [[None] * 4 for _ in n]
+    for w in range(4):
+        for g in pairs:
+            o[g][w], o[g + 1][w] = two_dots(
+                [x[w] for x in pt[g : g + 2]], [spread(x[w], w, lm) for x in v4[g : g + 2]]
+            )
+    return p, [jnp.concatenate(x, axis=0) for x in o]
+
+
+def attend_groups_back(q, k, v, p, da, lm, lane):
+    n = range(len(q))
+    pairs = range(0, len(q), 2)
+    dat = [x.T for x in da]
+    v4, k4, p4 = [four(x) for x in v], [four(x) for x in k], [four(x) for x in p]
+    ds, dv, dk, dp, dq = ([[None] * 4 for _ in n] for _ in range(5))
+    for j in range(4):
+        for g in pairs:
+            dp[g][j], dp[g + 1][j] = two_dots(
+                [weave(x, j, lane) for x in v4[g : g + 2]], [masked(x, j, lm) for x in dat[g : g + 2]]
+            )
+            dv[g][j], dv[g + 1][j] = two_dots(
+                [x[j] for x in p4[g : g + 2]], [masked(x, j, lm) for x in da[g : g + 2]]
+            )
+    for g in n:
+        for j in range(4):
+            pr = p4[g][j].astype(F32)
+            t = pr * dp[g][j]
+            ds[g][j] = (t - pr * jnp.sum(t, axis=0, keepdims=True)).astype(BF)
+    dst = [four(jnp.concatenate(x, axis=0).T) for x in ds]
+    for j in range(4):
+        for g in pairs:
+            dk[g][j], dk[g + 1][j] = two_dots(
+                [x[j] for x in ds[g : g + 2]], [masked(x, j, lm) for x in q[g : g + 2]]
+            )
+    for w in range(4):
+        for g in pairs:
+            dq[g][w], dq[g + 1][w] = two_dots(
+                [x[w] for x in dst[g : g + 2]], [spread(x[w], w, lm) for x in k4[g : g + 2]]
+            )
+    whole = lambda parts: jnp.concatenate([weave(parts, w, lane) for w in range(4)], axis=0)
+    return [(jnp.concatenate(dq[g], axis=0), whole(dk[g]), whole(dv[g])) for g in n]
 
 
 def shifts(a):
@@ -131,12 +158,10 @@
 def attend_half(s, lm, taps, shift):
     tokens = s["q"].shape[0]
     lane = lax.broadcasted_iota(jnp.int32, (32, 128), 1)
-    out = []
-    for g in range(tokens // 128):
-        rows = slice(128 * g, 128 * g + 128)
-        p, o = attend_group(s["q"][rows], s["k"][rows], s["v"][rows], lm, lane)
-        s["p"][rows] = p
-        out.append(o)
+    rows = [slice(128 * n, 128 * n + 128) for n in range(tokens // 128)]
+    p, out = attend_groups(*([s[name][r] for r in rows] for name in "qkv"), lm, lane)
+    for r, x in zip(rows, p):
+        s["p"][r] = x
     tap = lambda i, j: taps[3 * (i + 1) + j + 1][None]
     near = {j: lines(z) for j, z in shifts(s["v"][...].astype(F32)).items()}
     line = lambda i, n: sum(near[j][n] * tap(i, j) for j in (-1, 0, 1))
@@ -147,10 +172,8 @@
 def attend_half_back(s, lm, taps, small, cols):
     tokens = s["q"].shape[0]
     lane = lax.broadcasted_iota(jnp.int32, (32, 128), 1)
-    parts = []
-    for g in range(tokens // 128):
-        rows = slice(128 * g, 128 * g + 128)
-        parts.append(attend_group_back(s["q"][rows], s["k"][rows], s["v"][rows], s["p"][rows], s["da"][rows], lm, lane))
+    rows = [slice(128 * n, 128 * n + 128) for n in range(tokens // 128)]
+    parts = attend_groups_back(*([s[name][r] for r in rows] for name in ("q", "k", "v", "p", "da")), lm, lane)
     dq, dk, dv = (jnp.concatenate(z, axis=0) for z in zip(*parts))
     tap = lambda i, j: taps[3 * (i + 1) + j + 1][None]
     da = s["da"][...].astype(F32)
@@ -286,14 +309,61 @@
             self.peers(lambda d, to, far: self.gather(d, to, mb).wait_send())
 
 
+class Tiny:
+    def __init__(self, me, mb, own, row, col, send_sem, recv_sem):
+        self.me, self.mb, self.own, self.row, self.col = me, mb, own, row, col
+        self.send_sem, self.recv_sem = send_sem, recv_sem
+        self.axes = (("row", me, own, row, 0), ("batch", mb, own, col, row.shape[0]))
+
+    def each(self, n, body):
+        axis, here, src, dst, base = self.axes[n]
+        size = dst.shape[0]
+
+        def one(d, _):
+            def copy(arriving):
+                at = lax.rem(here + size - d, size) if arriving else here
+                return pltpu.make_async_remote_copy(
+                    src_ref=src.at[n],
+                    dst_ref=dst.at[at],
+                    send_sem=self.send_sem.at[base + d],
+                    recv_sem=self.recv_sem.at[base + d],
+                    device_id={axis: lax.rem(here + d, size)},
+                    device_id_type=pl.DeviceIdType.MESH,
+                )
+
+            body(copy)
+            return 0
+
+        lax.fori_loop(1, size, one, 0)
+
+    def start(self, n, value):
+        _, here, src, dst, _ = self.axes[n]
+        src[n] = value
+        dst[here] = value
+        self.each(n, lambda copy: copy(False).start())
+
+    def total(self, n):
+        dst = self.axes[n][3]
+        self.each(n, lambda copy: copy(True).wait_recv())
+        return lax.fori_loop(0, dst.shape[0], lambda i, t: t + dst[i], jnp.zeros(dst.shape[1:], F32))
+
+    def sent(self):
+        for n in range(2):
+            self.each(n, lambda copy: copy(False).wait_send())
+
+
 def block_kernel(
     shares,
     ahead,
+    early,
     boxes_ref,
     drops_ref,
-    index_ref,
+    partners_ref,
+    inverse_ref,
+    cot_hbm,
+    w1_hbm,
+    w2_hbm,
     x_ref,
-    cot_ref,
     norm1_gain,
     norm1_bias,
     norm2_gain,
@@ -305,17 +375,27 @@
     fc1_bias,
     wq,
     wp,
-    w1,
-    w2,
     out,
     ig,
     whole1,
     whole2,
+    last,
+    tiny,
+    tiny_own,
+    tiny_row,
+    tiny_col,
+    tiny_send,
+    tiny_recv,
+    cot_ref,
+    w1,
+    w2,
+    out_s,
     stage1,
     stage2,
     boxes,
     drops,
-    index,
+    partners,
+    inverse,
     vec,
     gw1,
     gb1,
@@ -374,11 +454,17 @@
     red1 = Reduce(0, me, mb, shares, stage1, whole1, r11, r12, r13, z1, sum_send, sum_recv)
     red2 = Reduce(1, me, mb, shares, stage2, whole2, r21, r22, r23, z2, sum_send, sum_recv)
 
+    few = Tiny(me, mb, tiny_own, tiny_row, tiny_col, tiny_send, tiny_recv)
+
     loads = [
         pltpu.make_async_copy(src, dst, load_sem.at[n])
-        for n, (src, dst) in enumerate(((boxes_ref, boxes), (drops_ref, drops), (index_ref, index)))
+        for n, (src, dst) in enumerate(((boxes_ref, boxes), (drops_ref, drops), (partners_ref, partners), (inverse_ref, inverse)))
     ]
-    for load in loads:
+    late = [
+        pltpu.make_async_copy(src, dst, load_sem.at[4 + n])
+        for n, (src, dst) in enumerate(((cot_hbm, cot_ref), (w1_hbm, w1), (w2_hbm, w2)))
+    ]
+    for load in loads + late:
         load.start()
     barrier = pltpu.get_barrier_semaphore()
     for d in range(1, shares):
@@ -414,7 +500,7 @@
     to_row = lax.broadcasted_iota(jnp.int32, (256, 256), 0)
     to_col = lax.broadcasted_iota(jnp.int32, (256, 256), 1)
     perm_ref[...] = jnp.where((to_row % 16) * 16 + to_row // 16 == to_col, 1.0, 0.0).astype(BF)
-    for ref in (gw1, gb1, gw2t, gq, gp, small):
+    for ref in (gw1, gb1, gw2t, gq, gp, small, tiny):
         ref[...] = jnp.zeros_like(ref)
     for part in range(3):
         cols = slice(128 * part, 128 * part + 128)
@@ -430,10 +516,10 @@
 
     def shares_of(image):
         inside = (
-            (grid_row >= boxes[image, 0])
-            & (grid_row < boxes[image, 1])
-            & (grid_col >= boxes[image, 2])
-            & (grid_col < boxes[image, 3])
+            (grid_row >= boxes[0, image])
+            & (grid_row < boxes[1, image])
+            & (grid_col >= boxes[2, image])
+            & (grid_col < boxes[3, image])
         )
         return jnp.where(inside, 0.0, 0.7), jnp.where(inside, 1.0, 0.3)
 
@@ -448,21 +534,30 @@
 
     def keep(c, j):
         return jnp.concatenate(
-            [jnp.full((strip, 1), drops[image, j].astype(F32) * 1.25) for _, _, image in home(c)], axis=0
+            [jnp.full((strip, 1), drops[j, image].astype(F32) * 1.25) for _, _, image in home(c)], axis=0
         )
 
     def half(c, tall):
         refs = (qt, kt, vt, pt) if tall else (qf, kf, vf, pf)
         return dict(zip("qkvp", [r.at[c] for r in refs]))
 
+    def stores(c, src, dst, which):
+        return [
+            pltpu.make_async_copy(src.at[c, q], dst.at[pl.ds(mine * q + pair * c, pair)], store_sem.at[which, c, q])
+            for q in range(shares)
+        ]
+
     def mix(c, _):
         for q, i, image in home(c):
             own, other = shares_of(image)
-            m = own * x_ref[image].astype(F32) + other * x_ref[index[0, image]].astype(F32)
+            m = own * x_ref[image].astype(F32) + other * x_ref[lax.rem(partners[image], images)].astype(F32)
             mixed[image] = m
             u, _ = normalise(m)
             n1h[c, q, i] = (u * v(G1) + v(B1)).astype(BF)
-        ex.send(N1, c, n1h, n1t)
+        @pl.when(c < early)
+        def _():
+            ex.send(N1, c, n1h, n1t)
+
         return 0
 
     def flat(c, _):
@@ -499,7 +594,7 @@
         dn2 = jnp.zeros((tokens, 256), F32)
         for f in range(w1.shape[1] // 256):
             fs = slice(256 * f, 256 * f + 256)
-            act, slope = gelu_parts(dot(n2, w1[:, fs]) + v(FB1 + f))
+            act, slope = gelu_twice(dot(n2, w1[:, fs]) + v(FB1 + f))
             act = act.astype(BF)
             dpre = (slope * dot(db2, w2[fs, :], 1, 1)).astype(BF)
             branch2 = branch2 + dot(act, w2[fs, :])
@@ -508,12 +603,13 @@
             gw1[:, fs] += grad[:256]
             gb1[:, fs] += grad[256:]
             gw2t[:, fs] += dot(db2t, act)
-        done = (h1 + keep2 * (branch2 + v(FB2))).astype(BF)
-        for n, (_, _, image) in enumerate(home(c)):
-            out[image] = done[strip * n : strip * n + strip]
+        done = (h1 + (0.5 * keep2) * (branch2 + 2.0 * v(FB2))).astype(BF)
+        out_s[c] = done.reshape(out_s.shape[1:])
+        for store in stores(c, out_s, out, 0):
+            store.start()
         small[G2] += sum8(dn2 * u2)
         small[B2] += sum8(dn2)
-        d = cot + normalise_back(dn2, u2, rstd2, v(G2))
+        d = cot + normalise_back(dn2, u2, rstd2, 0.5 * v(G2))
         dh1[c] = d
         db1 = (keep1 * d).astype(BF)
         small[PB] += sum8(db1.astype(F32))
@@ -547,19 +643,19 @@
 
     def pack1():
         quarters = [slice(256 * f, 256 * f + 256) for f in range(w1.shape[1] // 256)]
-        blocks = [gw1[:, fs].astype(BF) for fs in quarters]
-        blocks += [gw2t[:, fs].astype(BF).T for fs in quarters]
+        blocks = [(0.5 * gw1[:, fs]).astype(BF) for fs in quarters]
+        blocks += [(0.5 * gw2t[:, fs]).astype(BF).T for fs in quarters]
         put(stage1, blocks + [gp[...].astype(BF)])
 
     def pack2():
         blocks = [gq[:, 256 * n : 256 * n + 256].astype(BF) for n in range(3)]
         row = lambda i: jnp.sum(small[i], axis=0, keepdims=True)
-        rows = [row(i) for i in range(CONV)]
+        rows = [row(i) * (0.5 if i in (G2, B2) else 1.0) for i in range(CONV)]
         conv = [row(CONV + i) for i in range(9)]
         for i in range(3):
             for j in range(3):
                 rows.append(jnp.concatenate([conv[3 * i + j][:, :128], conv[3 * j + i][:, 128:]], axis=1))
-        rows += [gb1[0:1, 256 * f : 256 * f + 256] for f in range(w1.shape[1] // 256)]
+        rows += [0.5 * gb1[0:1, 256 * f : 256 * f + 256] for f in range(w1.shape[1] // 256)]
         rows.append(jnp.zeros((32 - len(rows), 256), F32))
         put(stage2, blocks + [jnp.concatenate(rows, axis=0).astype(BF)])
 
@@ -576,31 +672,34 @@
     def flat_back(c, _):
         s = dict(half(c, False), da=da_f.at[c])
         dqkv = attend_half_back(s, lm, taps_f, small, slice(0, 128))
+        ex.sent(N1, c, n1h, n1t)
         add_qkv(dot(n1h[c].reshape(tokens, 256), dqkv, 0, 0), 0)
-        dn1 = dot(dqkv, wf_ref[...], 1, 1)
+        n1h[c] = dot(dqkv, wf_ref[...], 1, 1).astype(BF).reshape(n1h.shape[1:])
+        return 0
+
+    def norm_back(c, _):
         ex.receive(DN, c, dn_ts, dn_th)
-        dn1 = dn1 + dn_th[c].reshape(tokens, 256).astype(F32)
+        dn1 = n1h[c].reshape(tokens, 256).astype(F32) + dn_th[c].reshape(tokens, 256).astype(F32)
         m = jnp.concatenate([mixed[image] for _, _, image in home(c)], axis=0)
         u1, rstd1 = normalise(m)
-        small[G1] += sum8(dn1 * u1)
-        small[B1] += sum8(dn1)
+        tiny[0] += sum8(dn1 * u1)
+        tiny[1] += sum8(dn1)
         d = dh1[c] + normalise_back(dn1, u1, rstd1, v(G1))
         for n, (_, _, image) in enumerate(home(c)):
             mixed[image] = d[strip * n : strip * n + strip]
-        return 0
-
-    def stores(c):
-        return [
-            pltpu.make_async_copy(n1h.at[c, q], ig.at[pl.ds(mine * q + pair * c, pair)], store_sem.at[c, q])
-            for q in range(shares)
-        ]
+        for n, at in ((1, 0), (2, chunks // 3), (3, chunks // 2), (4, chunks - 1)):
+
+            @pl.when(c == at)
+            def _():
+                red2.step(n)
+
+        return 0
 
     def unmix(c, _):
-        ex.sent(N1, c, n1h, n1t)
         for q, i, image in home(c):
-            other = index[1, image]
+            other = inverse[image]
             n1h[c, q, i] = (shares_of(image)[0] * mixed[image] + shares_of(other)[1] * mixed[other]).astype(BF)
-        for store in stores(c):
+        for store in stores(c, n1h, ig, 1):
             store.start()
         return 0
 
@@ -609,6 +708,10 @@
     lax.fori_loop(0, ahead, tall, 0)
 
     def forward(c, _):
+        @pl.when(c < chunks - early)
+        def _():
+            ex.send(N1, c + early, n1h, n1t)
+
         @pl.when(c < chunks - ahead)
         def _():
             tall(c + ahead, 0)
@@ -616,6 +719,8 @@
         mlp(c, 0)
         return 0
 
+    for load in late:
+        load.wait()
     lax.fori_loop(0, chunks, forward, 0)
     pack1()
     red1.step(0)
@@ -640,18 +745,22 @@
     pack2()
     red2.step(0)
     red1.step(4)
-    red2.step(1)
-    lax.fori_loop(0, chunks, unmix, 0)
-    red2.step(2)
+    lax.fori_loop(0, chunks, norm_back, 0)
+    rows = [jnp.sum(tiny[n], axis=0, keepdims=True) for n in range(2)] + [jnp.zeros((6, 256), F32)]
+    few.start(0, jnp.concatenate(rows, axis=0))
     red1.step(5)
-    red2.step(3)
-    red2.step(4)
+    half_way = chunks // 2
+    lax.fori_loop(0, half_way, unmix, 0)
+    few.start(1, few.total(0))
+    lax.fori_loop(half_way, chunks, unmix, 0)
+    last[...] = few.total(1)
+    few.sent()
     red2.step(5)
 
     def drain(c, _):
         for kind, src, dst in ((AT, att_ts, att_th), (DA, da_ts, da_tt), (DN, dn_ts, dn_th)):
             ex.sent(kind, c, src, dst)
-        for store in stores(c):
+        for store in stores(c, out_s, out, 0) + stores(c, n1h, ig, 1):
             store.wait()
         return 0
 
@@ -662,7 +771,7 @@
     return -(-rows // (2 * batch * 16)) * 16
 
 
-def block(inputs, cotangent, boxes, drops, index, vectors, weights, pair=2, ahead=2):
+def block(inputs, cotangent, boxes, drops, partners, inverse, vectors, weights, pair=2, ahead=2, early=4):
     images, grid_rows, side, width = inputs.shape
     shares, batch = lax.axis_size("row"), lax.axis_size("batch")
     strip = grid_rows * side
@@ -681,21 +790,33 @@
     at_tall = lambda ch: pltpu.VMEM((chunks, pair, shares, strip, ch), BF)
     part = lambda n, *lead: pltpu.VMEM((*lead, n, width), BF)
     return pl.pallas_call(
-        functools.partial(block_kernel, shares, ahead),
-        in_specs=[hbm] * 3 + [vmem] * (2 + len(vectors) + len(weights)),
-        out_specs=[vmem, hbm, vmem, vmem],
+        functools.partial(block_kernel, shares, ahead, early),
+        in_specs=[hbm] * 7 + [vmem] * (1 + len(vectors) + 2),
+        out_specs=[hbm, hbm, vmem, vmem, vmem],
         out_shape=[
             sds(x.shape, BF),
             sds(x.shape, BF),
             sds((2, batch, n1, width), BF),
             sds((2, batch, n2, width), BF),
+            sds((8, width), F32),
         ],
         scratch_shapes=[
+            pltpu.VMEM((2, 8, width), F32),
+            pltpu.VMEM((2, 8, width), F32),
+            pltpu.VMEM((shares, 8, width), F32),
+            pltpu.VMEM((batch, 8, width), F32),
+            pltpu.SemaphoreType.DMA((shares + batch,)),
+            pltpu.SemaphoreType.DMA((shares + batch,)),
+            pltpu.VMEM(x.shape, BF),
+            pltpu.VMEM(weights[2].shape, BF),
+            pltpu.VMEM(weights[3].shape, BF),
+            at_home(width),
             pltpu.VMEM((2, batch, n1, width), BF),
             pltpu.VMEM((2, batch, n2, width), BF),
             pltpu.SMEM(boxes.shape, jnp.int32),
             pltpu.SMEM(drops.shape, jnp.int32),
-            pltpu.SMEM(index.shape, jnp.int32),
+            pltpu.SMEM(partners.shape, jnp.int32),
+            pltpu.SMEM(inverse.shape, jnp.int32),
             pltpu.VMEM((24, width), F32),
             pltpu.VMEM((width, hidden), F32),
             pltpu.VMEM((16, hidden), F32),
@@ -717,19 +838,25 @@
         + [part(n2, batch), part(n2, batch), part(n2), part(n2)]
         + [pltpu.SemaphoreType.DMA((4, chunks, shares - 1))] * 2
         + [pltpu.SemaphoreType.DMA((2, 2 * batch + 1))] * 2
-        + [pltpu.SemaphoreType.DMA((3,)), pltpu.SemaphoreType.DMA((chunks, shares))],
+        + [pltpu.SemaphoreType.DMA((7,)), pltpu.SemaphoreType.DMA((2, chunks, shares))],
         compiler_params=pltpu.CompilerParams(
             collective_id=0, has_side_effects=True, vmem_limit_bytes=63 * 2**20
         ),
-    )(boxes, drops, index, x, cot, *vectors, *weights)
+    )(boxes, drops, partners, inverse, cot, *weights[2:], x, *vectors, *weights[:2])
 
 
 def finish_kernel(
-    out_ref, ig_ref, sum1, sum2, out, ig, g1, b1, gq, conv, cb, gp, pb, g2, b2, gw1, fb1, gw2, fb2, sems
+    out_ref, ig_ref, sum1, sum2, last, out, ig, g1, b1, gq, conv, cb, gp, pb, g2, b2, gw1, fb1, gw2, fb2, held, sems
 ):
-    copies = [pltpu.make_async_copy(out_ref, out, sems.at[0]), pltpu.make_async_copy(ig_ref, ig, sems.at[1])]
-    for copy in copies:
-        copy.start()
+    third = out.shape[0] // 3
+    parts = [(n, pl.ds(third * i, third), 3 * n + i) for i in range(3) for n in range(2)]
+    loads = [pltpu.make_async_copy((out_ref, ig_ref)[n].at[rows], held.at[n, rows], sems.at[0, m]) for n, rows, m in parts]
+    stores = [pltpu.make_async_copy(held.at[n, rows], (out, ig)[n].at[rows], sems.at[1, m]) for n, rows, m in parts]
+    for load in loads:
+        load.start()
+    for load, store in zip(loads, stores):
+        load.wait()
+        store.start()
     hidden = gw1.shape[1]
     for f in range(hidden // 256):
         gw1[:, 256 * f : 256 * f + 256] = sum1[256 * f : 256 * f + 256].astype(F32)
@@ -738,18 +865,19 @@
     for f in range(3):
         gq[:, 256 * f : 256 * f + 256] = sum2[256 * f : 256 * f + 256].astype(F32)
     rows = sum2[768:800].astype(F32)
-    for n, ref in ((G1, g1), (B1, b1), (G2, g2), (B2, b2), (PB, pb), (FB2, fb2), (CB, cb)):
+    for n, ref in ((G2, g2), (B2, b2), (PB, pb), (FB2, fb2), (CB, cb)):
         ref[...] = rows[n]
+    g1[...], b1[...] = last[0], last[1]
     for i in range(3):
         for j in range(3):
             conv[i, j] = rows[CONV + 3 * i + j]
     for f in range(hidden // 256):
         fb1[256 * f : 256 * f + 256] = rows[FB1 + f]
-    for copy in copies:
-        copy.wait()
-
-
-def finish(out, ig, sum1, sum2, hidden):
+    for store in stores:
+        store.wait()
+
+
+def finish(out, ig, sum1, sum2, last, hidden):
     width = out.shape[-1]
     sds = jax.ShapeDtypeStruct
     vmem = pl.BlockSpec(memory_space=pltpu.VMEM)
@@ -773,12 +901,12 @@
     ]
     return pl.pallas_call(
         finish_kernel,
-        in_specs=[hbm, hbm, vmem, vmem],
+        in_specs=[hbm, hbm, vmem, vmem, vmem],
         out_specs=[hbm, hbm] + [vmem] * len(shapes),
         out_shape=[sds(out.shape, BF), sds(ig.shape, BF)] + shapes,
-        scratch_shapes=[pltpu.SemaphoreType.DMA((2,))],
-        compiler_params=pltpu.CompilerParams(vmem_limit_bytes=32 * 2**20),
-    )(out, ig, sum1.reshape(-1, width), sum2.reshape(-1, width))
+        scratch_shapes=[pltpu.VMEM((2,) + out.shape, BF), pltpu.SemaphoreType.DMA((2, 6))],
+        compiler_params=pltpu.CompilerParams(vmem_limit_bytes=62 * 2**20),
+    )(out, ig, sum1.reshape(-1, width), sum2.reshape(-1, width), last)
 
 
 def per_device(
@@ -803,13 +931,11 @@
 ):
     images = inputs.shape[0]
     ids = jnp.arange(images)
-    local = partners - lax.axis_index("batch") * images
-    inverse = jnp.sum(jnp.where(local[:, None] == ids[None, :], ids[:, None], 0), axis=0)
-    index = jnp.stack([local, inverse])
+    inverse = jnp.sum(jnp.where(partners[:, None] % images == ids[None, :], ids[:, None], 0), axis=0)
     vectors = (norm1_gain, norm1_bias, norm2_gain, norm2_bias, proj_bias, fc2_bias, lepe_bias, lepe_weight, fc1_bias)
     weights = (qkv_weight, proj_weight, fc1_weight, fc2_weight)
-    out, ig, sum1, sum2 = block(inputs, cotangent, boxes, drops, index, vectors, weights)
-    out, ig, *grads = finish(out, ig, sum1, sum2, fc1_weight.shape[1])
+    out, ig, sum1, sum2, last = block(inputs, cotangent, boxes.T, drops.T, partners, inverse, vectors, weights)
+    out, ig, *grads = finish(out, ig, sum1, sum2, last, fc1_weight.shape[1])
     return (out.reshape(inputs.shape), ig.reshape(inputs.shape), *grads)
 
 

time: 170 us -> 140 us (0.82)
  Pallas kernels: 158 us -> 138 us
  local copies, waits for them, and re-layouts: 8.41 us -> 0 us
    pallas_call x2, Pallas kernels: 158 us -> 138 us  [the longest x1 131 us: block(): pl.pallas_call(functools.partial(block_kernel, shares, ahead, early), in_...]
    unnamed x10 -> x0, local copies, waits for them, and re-layouts: 8.41 us -> none
where the time goes in v4:
time: 140 us
  Pallas kernels  138 us (99%)
    pallas_call x1, Pallas kernels, block(): pl.pallas_call(functools.partial(block_kernel, shares, ahead, early), in_...  131 us
    pallas_call x1, Pallas kernels, finish(): pl.pallas_call(finish_kernel, in_specs=[hbm, hbm, vmem, vmem, vmem], out_...  7.1 us

profile of v4, /device:TPU:0, one launch (start us, length us, event | category | flops | bytes accessed | tf_op | source)
XLA Modules:
  0.0 140.0 jit_solution(5671899195197308697)
XLA Ops:
  0.6 0.7 and_select_fusion
  1.3 0.6 select_reduce_fusion.inverse_ref
  1.9 131.0 %shard_map.289 = (bf16[72,64,256]{2,1,0:T(8,128)(2,1)}, bf16[72,64,256]{2,1,0:T(8,128)(2,1)}, bf16[2,8,144,256]{3,2,1,0:T(8,128)(2,1)}, bf16[2,8,64,256]{3,2,1,0:T(8,128)(2,1)}, f32[8,256]{1,0:T(8,128)}) custom-call(s32[4,72]{1,0:T(4,128)} %bitcast.12, s32[2,72]{1,0:T(2,128)} %bitcast.13, s32[72]{0:T(128)} %partners_ref.1, s32[72]{0:T(128)} %select_reduce_fusion.inverse_ref, ...), custom_call_target="tpu_custom_call" | custom-call | tf_op jit(solution)/shard_map/pallas_call | solution.py:792
  132.9 7.1 %shard_map.290 = (bf16[72,64,256]{2,1,0:T(8,128)(2,1)}, bf16[72,64,256]{2,1,0:T(8,128)(2,1)}, f32[256]{0:T(256)}, f32[256]{0:T(256)}, f32[256,768]{1,0:T(8,128)}...) custom-call(bf16[72,64,256]{2,1,0:T(8,128)(2,1)} %get-tuple-element., ...), custom_call_target="tpu_custom_call" | custom-call | tf_op jit(solution)/shard_map/pallas_call | solution.py:902

commit v5 on v4

--- a/solution.py
+++ b/solution.py
@@ -134,25 +134,33 @@
     return [(jnp.concatenate(dq[g], axis=0), whole(dk[g]), whole(dv[g])) for g in n]
 
 
-def shifts(a):
-    n = a.shape[0]
-    pos = lax.broadcasted_iota(jnp.int32, a.shape, 0) % 16
-    return {
-        -1: jnp.where(pos == 0, 0.0, pltpu.roll(a, 1, 0)),
-        0: a,
-        1: jnp.where(pos == 15, 0.0, pltpu.roll(a, n - 1, 0)),
-    }
-
-
-def lines(a):
+def tiles(a):
     n, c = a.shape
-    b = a.reshape(n // 32, 2, 16, c)
-    return b[:, 0].reshape(n // 2, c), b[:, 1].reshape(n // 2, c)
-
-
-def woven(a0, a1):
-    n, c = a0.shape
-    return jnp.stack([a0.reshape(n // 16, 16, c), a1.reshape(n // 16, 16, c)], axis=1).reshape(2 * n, c)
+    z = a.reshape(n // 32, 4, 8, c)
+    return [z[:, i] for i in range(4)]
+
+
+def untiled(parts):
+    n, _, c = parts[0].shape
+    return jnp.stack(parts, axis=1).reshape(32 * n, c)
+
+
+def shifts(parts):
+    row = lax.broadcasted_iota(jnp.int32, parts[0].shape, 1)
+    up = [pltpu.roll(p, 1, 1) for p in parts]
+    down = [pltpu.roll(p, 7, 1) for p in parts]
+    early, late = [], []
+    for lo in (0, 2):
+        early += [jnp.where(row == 0, 0.0, up[lo]), jnp.where(row == 0, up[lo], up[lo + 1])]
+        late += [jnp.where(row == 7, down[lo + 1], down[lo]), jnp.where(row == 7, 0.0, down[lo + 1])]
+    return {-1: early, 0: parts, 1: late}
+
+
+def taps_sum(near, taps, pairs):
+    return [
+        sum(near[j][2 * line + h] * taps[3 * (i + 1) + j + 1][None, None] for i, line in pairs for j in (-1, 0, 1))
+        for h in range(2)
+    ]
 
 
 def attend_half(s, lm, taps, shift):
@@ -162,10 +170,8 @@
     p, out = attend_groups(*([s[name][r] for r in rows] for name in "qkv"), lm, lane)
     for r, x in zip(rows, p):
         s["p"][r] = x
-    tap = lambda i, j: taps[3 * (i + 1) + j + 1][None]
-    near = {j: lines(z) for j, z in shifts(s["v"][...].astype(F32)).items()}
-    line = lambda i, n: sum(near[j][n] * tap(i, j) for j in (-1, 0, 1))
-    lepe = woven(line(0, 0) + line(1, 1), line(0, 1) + line(-1, 0))
+    near = shifts(tiles(s["v"][...].astype(F32)))
+    lepe = untiled(taps_sum(near, taps, ((0, 0), (1, 1))) + taps_sum(near, taps, ((0, 1), (-1, 0))))
     return (jnp.concatenate(out, axis=0) + (lepe + shift)).astype(BF)
 
 
@@ -175,18 +181,17 @@
     rows = [slice(128 * n, 128 * n + 128) for n in range(tokens // 128)]
     parts = attend_groups_back(*([s[name][r] for r in rows] for name in ("q", "k", "v", "p", "da")), lm, lane)
     dq, dk, dv = (jnp.concatenate(z, axis=0) for z in zip(*parts))
-    tap = lambda i, j: taps[3 * (i + 1) + j + 1][None]
     da = s["da"][...].astype(F32)
     small[CB, :, cols] += sum8(da)
-    moved = {-j: lines(z) for j, z in shifts(da).items()}
-    v0, v1 = lines(s["v"][...].astype(F32))
-    line = lambda i, n: sum(moved[j][n] * tap(i, j) for j in (-1, 0, 1))
-    dv = dv + woven(line(0, 0) + line(-1, 1), line(1, 0) + line(0, 1))
+    moved = {-j: parts for j, parts in shifts(tiles(da)).items()}
+    vt = tiles(s["v"][...].astype(F32))
+    dv = dv + untiled(taps_sum(moved, taps, ((0, 0), (-1, 1))) + taps_sum(moved, taps, ((1, 0), (0, 1))))
+    over = lambda z: jnp.sum(z, axis=0)
     for j in (-1, 0, 1):
-        m0, m1 = moved[j]
-        small[CONV + 3 + j + 1, :, cols] += sum8(m0 * v0 + m1 * v1)
-        small[CONV + 6 + j + 1, :, cols] += sum8(m0 * v1)
-        small[CONV + 0 + j + 1, :, cols] += sum8(m1 * v0)
+        m = moved[j]
+        small[CONV + 3 + j + 1, :, cols] += over(m[0] * vt[0] + m[1] * vt[1] + m[2] * vt[2] + m[3] * vt[3])
+        small[CONV + 6 + j + 1, :, cols] += over(m[0] * vt[2] + m[1] * vt[3])
+        small[CONV + 0 + j + 1, :, cols] += over(m[2] * vt[0] + m[3] * vt[1])
     return jnp.concatenate([(dq * SCALE).astype(BF), (dk * SCALE).astype(BF), dv.astype(BF)], axis=1)
 
 
@@ -377,8 +382,11 @@
     wp,
     out,
     ig,
-    whole1,
-    whole2,
+    *refs,
+):
+    n_sums = 4
+    wholes = refs[:n_sums]
+    (
     last,
     tiny,
     tiny_own,
@@ -389,9 +397,6 @@
     cot_ref,
     w1,
     w2,
-    out_s,
-    stage1,
-    stage2,
     boxes,
     drops,
     partners,
@@ -427,21 +432,14 @@
     da_tt,
     dn_ts,
     dn_th,
-    r11,
-    r12,
-    r13,
-    z1,
-    r21,
-    r22,
-    r23,
-    z2,
     send_sem,
     recv_sem,
     sum_send,
     sum_recv,
     load_sem,
     store_sem,
-):
+    *spare,
+    ) = refs[n_sums:]
     chunks, _, pair, strip = n1h.shape[:4]
     images = x_ref.shape[0]
     mine = images // shares
@@ -450,9 +448,12 @@
     ex = Exchange(me, shares, send_sem, recv_sem)
 
     mb = lax.axis_index("batch")
-    batch = stage1.shape[1]
-    red1 = Reduce(0, me, mb, shares, stage1, whole1, r11, r12, r13, z1, sum_send, sum_recv)
-    red2 = Reduce(1, me, mb, shares, stage2, whole2, r21, r22, r23, z2, sum_send, sum_recv)
+    batch = tiny_col.shape[0]
+    sums = [
+        Reduce(n, me, mb, shares, spare[5 * n], wholes[n], *spare[5 * n + 1 : 5 * n + 5], sum_send, sum_recv)
+        for n in range(n_sums)
+    ]
+    sum_a, sum_b, sum_c, sum_d = sums
 
     few = Tiny(me, mb, tiny_own, tiny_row, tiny_col, tiny_send, tiny_recv)
 
@@ -541,11 +542,13 @@
         refs = (qt, kt, vt, pt) if tall else (qf, kf, vf, pf)
         return dict(zip("qkvp", [r.at[c] for r in refs]))
 
-    def stores(c, src, dst, which):
-        return [
-            pltpu.make_async_copy(src.at[c, q], dst.at[pl.ds(mine * q + pair * c, pair)], store_sem.at[which, c, q])
-            for q in range(shares)
-        ]
+    def stores(c, which):
+        copies = []
+        for q in range(shares):
+            rows = pl.ds(mine * q + pair * c, pair)
+            src, dst = ((cot_ref.at[rows], out), (n1h.at[c, q], ig))[which]
+            copies.append(pltpu.make_async_copy(src, dst.at[rows], store_sem.at[which, c, q]))
+        return copies
 
     def mix(c, _):
         for q, i, image in home(c):
@@ -604,8 +607,9 @@
             gb1[:, fs] += grad[256:]
             gw2t[:, fs] += dot(db2t, act)
         done = (h1 + (0.5 * keep2) * (branch2 + 2.0 * v(FB2))).astype(BF)
-        out_s[c] = done.reshape(out_s.shape[1:])
-        for store in stores(c, out_s, out, 0):
+        for n, (_, _, image) in enumerate(home(c)):
+            cot_ref[image] = done[strip * n : strip * n + strip]
+        for store in stores(c, 0):
             store.start()
         small[G2] += sum8(dn2 * u2)
         small[B2] += sum8(dn2)
@@ -641,23 +645,28 @@
             stage[piece // batch, piece % batch, at:] = jnp.zeros((rows - at, 256), BF)
             spot += rows - at
 
-    def pack1():
-        quarters = [slice(256 * f, 256 * f + 256) for f in range(w1.shape[1] // 256)]
-        blocks = [(0.5 * gw1[:, fs]).astype(BF) for fs in quarters]
-        blocks += [(0.5 * gw2t[:, fs]).astype(BF).T for fs in quarters]
-        put(stage1, blocks + [gp[...].astype(BF)])
-
-    def pack2():
-        blocks = [gq[:, 256 * n : 256 * n + 256].astype(BF) for n in range(3)]
+    quarters = [slice(256 * f, 256 * f + 256) for f in range(w1.shape[1] // 256)]
+
+    def pack_fc1():
+        put(sum_a.stage, [(0.5 * gw1[:, fs]).astype(BF) for fs in quarters])
+
+    def pack_fc2():
+        put(sum_b.stage, [(0.5 * gw2t[:, fs]).astype(BF).T for fs in quarters] + [gp[...].astype(BF)])
+
+    def qkv_blocks(start):
+        one, two, three = (gq[:, 256 * n + start : 256 * n + start + 128].astype(BF) for n in range(3))
+        return [jnp.concatenate([one, two], axis=1), jnp.concatenate([three[:128], three[128:]], axis=1)]
+
+    def pack_flat():
         row = lambda i: jnp.sum(small[i], axis=0, keepdims=True)
         rows = [row(i) * (0.5 if i in (G2, B2) else 1.0) for i in range(CONV)]
         conv = [row(CONV + i) for i in range(9)]
         for i in range(3):
             for j in range(3):
                 rows.append(jnp.concatenate([conv[3 * i + j][:, :128], conv[3 * j + i][:, 128:]], axis=1))
-        rows += [0.5 * gb1[0:1, 256 * f : 256 * f + 256] for f in range(w1.shape[1] // 256)]
+        rows += [0.5 * gb1[0:1, fs] for fs in quarters]
         rows.append(jnp.zeros((32 - len(rows), 256), F32))
-        put(stage2, blocks + [jnp.concatenate(rows, axis=0).astype(BF)])
+        put(sum_d.stage, qkv_blocks(0) + [jnp.concatenate(rows, axis=0).astype(BF)])
 
     def tall_back(c, _):
         ex.receive(DA, c, da_ts, da_tt)
@@ -666,20 +675,40 @@
         dqkv = attend_half_back(s, lm, taps_t, small, slice(128, 256))
         add_qkv(dot(n1p[c], dqkv, 0, 0), 128)
         dn_ts[c] = permute(dot(dqkv, wt_ref[...], 1, 1).astype(BF)).reshape(dn_ts.shape[1:])
-        ex.send(DN, c, dn_ts, dn_th)
+        return 0
+
+    def at(c, steps):
+        for spot, total, n in steps:
+
+            @pl.when(c == min(spot, chunks - 1))
+            def _():
+                total.step(n)
+
+    def pace(c, first, last):
+        @pl.when((c % 2 == 0) & (first + c // 2 < last))
+        def _():
+            ex.send(DN, first + c // 2, dn_ts, dn_th)
+
+    def tall_loop(c, _):
+        tall_back(c, 0)
+        pace(c, 0, chunks)
+        at(c, TALL_STEPS)
         return 0
 
     def flat_back(c, _):
         s = dict(half(c, False), da=da_f.at[c])
         dqkv = attend_half_back(s, lm, taps_f, small, slice(0, 128))
+        add_qkv(dot(n1h[c].reshape(tokens, 256), dqkv, 0, 0), 0)
+        qf[c], kf[c], vf[c] = dqkv[:, :128], dqkv[:, 128:256], dqkv[:, 256:]
+        pace(c, (chunks + 1) // 2, chunks)
+        at(c, FLAT_STEPS)
+        return 0
+
+    def norm_back(c, _):
         ex.sent(N1, c, n1h, n1t)
-        add_qkv(dot(n1h[c].reshape(tokens, 256), dqkv, 0, 0), 0)
-        n1h[c] = dot(dqkv, wf_ref[...], 1, 1).astype(BF).reshape(n1h.shape[1:])
-        return 0
-
-    def norm_back(c, _):
         ex.receive(DN, c, dn_ts, dn_th)
-        dn1 = n1h[c].reshape(tokens, 256).astype(F32) + dn_th[c].reshape(tokens, 256).astype(F32)
+        dqkv = jnp.concatenate([qf[c], kf[c], vf[c]], axis=1)
+        dn1 = dot(dqkv, wf_ref[...], 1, 1) + dn_th[c].reshape(tokens, 256).astype(F32)
         m = jnp.concatenate([mixed[image] for _, _, image in home(c)], axis=0)
         u1, rstd1 = normalise(m)
         tiny[0] += sum8(dn1 * u1)
@@ -687,20 +716,22 @@
         d = dh1[c] + normalise_back(dn1, u1, rstd1, v(G1))
         for n, (_, _, image) in enumerate(home(c)):
             mixed[image] = d[strip * n : strip * n + strip]
-        for n, at in ((1, 0), (2, chunks // 3), (3, chunks // 2), (4, chunks - 1)):
-
-            @pl.when(c == at)
-            def _():
-                red2.step(n)
-
+        at(c, NORM_STEPS)
         return 0
 
     def unmix(c, _):
         for q, i, image in home(c):
             other = inverse[image]
             n1h[c, q, i] = (shares_of(image)[0] * mixed[image] + shares_of(other)[1] * mixed[other]).astype(BF)
-        for store in stores(c, n1h, ig, 1):
+        for store in stores(c, 1):
             store.start()
+        return 0
+
+    def drain(c, _):
+        for kind, src, dst in ((AT, att_ts, att_th), (DA, da_ts, da_tt), (DN, dn_ts, dn_th)):
+            ex.sent(kind, c, src, dst)
+        for store in stores(c, 0) + stores(c, 1):
+            store.wait()
         return 0
 
     lax.fori_loop(0, chunks, mix, 0)
@@ -722,49 +753,42 @@
     for load in late:
         load.wait()
     lax.fori_loop(0, chunks, forward, 0)
-    pack1()
-    red1.step(0)
-    lax.fori_loop(0, ahead, tall_back, 0)
-    red1.step(1)
-
-    def backward(c, _):
-        @pl.when(c < chunks - ahead)
-        def _():
-            tall_back(c + ahead, 0)
-
-        flat_back(c, 0)
-        for n, at in ((2, chunks // 2), (3, chunks // 2 + 1)):
-
-            @pl.when(c == at)
-            def _():
-                red1.step(n)
-
-        return 0
-
-    lax.fori_loop(0, chunks, backward, 0)
-    pack2()
-    red2.step(0)
-    red1.step(4)
+    TALL_STEPS = ((0, sum_a, 1), (4, sum_b, 1), (5, sum_a, 2), (7, sum_a, 3))
+    FLAT_STEPS = (
+        (1, sum_c, 1),
+        (1, sum_b, 2),
+        (3, sum_b, 3),
+        (4, sum_a, 4),
+        (5, sum_c, 2),
+        (6, sum_a, 5),
+        (7, sum_c, 3),
+    )
+    NORM_STEPS = ((1, sum_d, 1), (6, sum_b, 4), (7, sum_c, 4), (8, sum_d, 2))
+    pack_fc1()
+    sum_a.step(0)
+    pack_fc2()
+    sum_b.step(0)
+    lax.fori_loop(0, chunks, tall_loop, 0)
+    put(sum_c.stage, qkv_blocks(128))
+    sum_c.step(0)
+    lax.fori_loop(0, chunks, flat_back, 0)
+    pack_flat()
+    sum_d.step(0)
     lax.fori_loop(0, chunks, norm_back, 0)
     rows = [jnp.sum(tiny[n], axis=0, keepdims=True) for n in range(2)] + [jnp.zeros((6, 256), F32)]
     few.start(0, jnp.concatenate(rows, axis=0))
-    red1.step(5)
-    half_way = chunks // 2
+    sum_b.step(5)
+    sum_c.step(5)
+    half_way = 2 * chunks // 3
     lax.fori_loop(0, half_way, unmix, 0)
+    sum_d.step(3)
     few.start(1, few.total(0))
     lax.fori_loop(half_way, chunks, unmix, 0)
+    sum_d.step(4)
     last[...] = few.total(1)
     few.sent()
-    red2.step(5)
-
-    def drain(c, _):
-        for kind, src, dst in ((AT, att_ts, att_th), (DA, da_ts, da_tt), (DN, dn_ts, dn_th)):
-            ex.sent(kind, c, src, dst)
-        for store in stores(c, out_s, out, 0) + stores(c, n1h, ig, 1):
-            store.wait()
-        return 0
-
     lax.fori_loop(0, chunks, drain, 0)
+    sum_d.step(5)
 
 
 def share_rows(rows, batch):
@@ -783,8 +807,8 @@
     hbm = pl.BlockSpec(memory_space=pl.ANY)
     x = inputs.reshape(images, strip, width)
     cot = cotangent.reshape(images, strip, width)
-    n1 = share_rows(2 * hidden + width, batch)
-    n2 = share_rows(3 * width + 32, batch)
+    sizes = [hidden, hidden + width, 3 * width // 2, 3 * width // 2 + 32]
+    sizes = [share_rows(n, batch) for n in sizes]
     rows = lambda ch, dt=BF: pltpu.VMEM((chunks, tokens, ch), dt)
     at_home = lambda ch: pltpu.VMEM((chunks, shares, pair, strip, ch), BF)
     at_tall = lambda ch: pltpu.VMEM((chunks, pair, shares, strip, ch), BF)
@@ -792,14 +816,13 @@
     return pl.pallas_call(
         functools.partial(block_kernel, shares, ahead, early),
         in_specs=[hbm] * 7 + [vmem] * (1 + len(vectors) + 2),
-        out_specs=[hbm, hbm, vmem, vmem, vmem],
+        out_specs=[hbm, hbm] + [vmem] * 5,
         out_shape=[
             sds(x.shape, BF),
             sds(x.shape, BF),
-            sds((2, batch, n1, width), BF),
-            sds((2, batch, n2, width), BF),
-            sds((8, width), F32),
-        ],
+        ]
+        + [sds((2, batch, n, width), BF) for n in sizes]
+        + [sds((8, width), F32)],
         scratch_shapes=[
             pltpu.VMEM((2, 8, width), F32),
             pltpu.VMEM((2, 8, width), F32),
@@ -810,9 +833,6 @@
             pltpu.VMEM(x.shape, BF),
             pltpu.VMEM(weights[2].shape, BF),
             pltpu.VMEM(weights[3].shape, BF),
-            at_home(width),
-            pltpu.VMEM((2, batch, n1, width), BF),
-            pltpu.VMEM((2, batch, n2, width), BF),
             pltpu.SMEM(boxes.shape, jnp.int32),
             pltpu.SMEM(drops.shape, jnp.int32),
             pltpu.SMEM(partners.shape, jnp.int32),
@@ -834,37 +854,55 @@
         ]
         + [rows(128)] * 9
         + [at_tall(128), at_home(128), rows(width, F32), rows(128), at_home(128), at_tall(128), at_tall(width), at_home(width)]
-        + [part(n1, batch), part(n1, batch), part(n1), part(n1)]
-        + [part(n2, batch), part(n2, batch), part(n2), part(n2)]
         + [pltpu.SemaphoreType.DMA((4, chunks, shares - 1))] * 2
-        + [pltpu.SemaphoreType.DMA((2, 2 * batch + 1))] * 2
-        + [pltpu.SemaphoreType.DMA((7,)), pltpu.SemaphoreType.DMA((2, chunks, shares))],
+        + [pltpu.SemaphoreType.DMA((len(sizes), 2 * batch + 1))] * 2
+        + [pltpu.SemaphoreType.DMA((7,)), pltpu.SemaphoreType.DMA((2, chunks, shares))]
+        + [z for n in sizes for z in (part(n, 2, batch), part(n, batch), part(n, batch), part(n), part(n))],
         compiler_params=pltpu.CompilerParams(
             collective_id=0, has_side_effects=True, vmem_limit_bytes=63 * 2**20
         ),
     )(boxes, drops, partners, inverse, cot, *weights[2:], x, *vectors, *weights[:2])
 
 
-def finish_kernel(
-    out_ref, ig_ref, sum1, sum2, last, out, ig, g1, b1, gq, conv, cb, gp, pb, g2, b2, gw1, fb1, gw2, fb2, held, sems
-):
-    third = out.shape[0] // 3
-    parts = [(n, pl.ds(third * i, third), 3 * n + i) for i in range(3) for n in range(2)]
-    loads = [pltpu.make_async_copy((out_ref, ig_ref)[n].at[rows], held.at[n, rows], sems.at[0, m]) for n, rows, m in parts]
-    stores = [pltpu.make_async_copy(held.at[n, rows], (out, ig)[n].at[rows], sems.at[1, m]) for n, rows, m in parts]
+def finish_kernel(out_ref, ig_ref, hbm_a, hbm_b, hbm_c, hbm_d, last, *refs):
+    out, ig, g1, b1, gq_hbm, conv, cb, gp_hbm, pb, g2, b2, gw1_hbm, fb1, gw2_hbm, fb2 = refs[:15]
+    held, sum_a, sum_b, sum_c, sum_d, gq, gp, gw1, gw2, load_sem, store_sem = refs[15:]
+    sixth = out.shape[0] // 6
+    loads = [
+        pltpu.make_async_copy(src, dst, load_sem.at[m])
+        for m, (src, dst) in enumerate(((hbm_a, sum_a), (hbm_b, sum_b), (hbm_c, sum_c), (hbm_d, sum_d)))
+    ]
+    stores = [
+        pltpu.make_async_copy(src, dst, store_sem.at[m])
+        for m, (src, dst) in enumerate(((gw1, gw1_hbm), (gw2, gw2_hbm), (gp, gp_hbm), (gq, gq_hbm)))
+    ]
+    parts = [(n, pl.ds(sixth * i, sixth), 6 * n + i + 4) for i in range(6) for n in range(2)]
+    loads += [pltpu.make_async_copy((out_ref, ig_ref)[n].at[r], held.at[n, r], load_sem.at[m]) for n, r, m in parts]
+    stores += [pltpu.make_async_copy(held.at[n, r], (out, ig)[n].at[r], store_sem.at[m]) for n, r, m in parts]
     for load in loads:
         load.start()
-    for load, store in zip(loads, stores):
+    hidden = gw1.shape[1]
+    loads[0].wait()
+    for f in range(hidden // 256):
+        gw1[:, 256 * f : 256 * f + 256] = sum_a[256 * f : 256 * f + 256].astype(F32)
+    stores[0].start()
+    loads[1].wait()
+    gw2[...] = sum_b[:hidden].astype(F32)
+    gp[...] = sum_b[hidden : hidden + 256].astype(F32)
+    stores[1].start()
+    stores[2].start()
+    loads[2].wait()
+    loads[3].wait()
+    for ref, start in ((sum_d, 0), (sum_c, 128)):
+        gq[:, start : start + 128] = ref[:256, :128].astype(F32)
+        gq[:, 256 + start : 384 + start] = ref[:256, 128:].astype(F32)
+        gq[:128, 512 + start : 640 + start] = ref[256:384, :128].astype(F32)
+        gq[128:, 512 + start : 640 + start] = ref[256:384, 128:].astype(F32)
+    stores[3].start()
+    for load, store in zip(loads[4:], stores[4:]):
         load.wait()
         store.start()
-    hidden = gw1.shape[1]
-    for f in range(hidden // 256):
-        gw1[:, 256 * f : 256 * f + 256] = sum1[256 * f : 256 * f + 256].astype(F32)
-    gw2[...] = sum1[hidden : 2 * hidden].astype(F32)
-    gp[...] = sum1[2 * hidden : 2 * hidden + 256].astype(F32)
-    for f in range(3):
-        gq[:, 256 * f : 256 * f + 256] = sum2[256 * f : 256 * f + 256].astype(F32)
-    rows = sum2[768:800].astype(F32)
+    rows = sum_d[384:416].astype(F32)
     for n, ref in ((G2, g2), (B2, b2), (PB, pb), (FB2, fb2), (CB, cb)):
         ref[...] = rows[n]
     g1[...], b1[...] = last[0], last[1]
@@ -877,36 +915,41 @@
         store.wait()
 
 
-def finish(out, ig, sum1, sum2, last, hidden):
+def finish(out, ig, sums, last, hidden):
     width = out.shape[-1]
     sds = jax.ShapeDtypeStruct
     vmem = pl.BlockSpec(memory_space=pltpu.VMEM)
     hbm = pl.BlockSpec(memory_space=pl.ANY)
     flat = lambda n: sds((n,), F32)
     square = lambda *n: sds(n, F32)
+    large = [square(width, 3 * width), square(width, width), square(width, hidden), square(hidden, width)]
     shapes = [
         flat(width),
         flat(width),
-        square(width, 3 * width),
+        large[0],
         square(3, 3, width),
         flat(width),
-        square(width, width),
+        large[1],
         flat(width),
         flat(width),
         flat(width),
-        square(width, hidden),
+        large[2],
         flat(hidden),
-        square(hidden, width),
+        large[3],
         flat(width),
     ]
+    sums = [z.reshape(-1, width) for z in sums]
     return pl.pallas_call(
         finish_kernel,
-        in_specs=[hbm, hbm, vmem, vmem, vmem],
-        out_specs=[hbm, hbm] + [vmem] * len(shapes),
+        in_specs=[hbm] * 6 + [vmem],
+        out_specs=[hbm, hbm] + [hbm if z in large else vmem for z in shapes],
         out_shape=[sds(out.shape, BF), sds(ig.shape, BF)] + shapes,
-        scratch_shapes=[pltpu.VMEM((2,) + out.shape, BF), pltpu.SemaphoreType.DMA((2, 6))],
+        scratch_shapes=[pltpu.VMEM((2,) + out.shape, BF)]
+        + [pltpu.VMEM(z.shape, BF) for z in sums]
+        + [pltpu.VMEM(z.shape, F32) for z in large]
+        + [pltpu.SemaphoreType.DMA((16,))] * 2,
         compiler_params=pltpu.CompilerParams(vmem_limit_bytes=62 * 2**20),
-    )(out, ig, sum1.reshape(-1, width), sum2.reshape(-1, width), last)
+    )(out, ig, *sums, last)
 
 
 def per_device(
@@ -934,8 +977,8 @@
     inverse = jnp.sum(jnp.where(partners[:, None] % images == ids[None, :], ids[:, None], 0), axis=0)
     vectors = (norm1_gain, norm1_bias, norm2_gain, norm2_bias, proj_bias, fc2_bias, lepe_bias, lepe_weight, fc1_bias)
     weights = (qkv_weight, proj_weight, fc1_weight, fc2_weight)
-    out, ig, sum1, sum2, last = block(inputs, cotangent, boxes.T, drops.T, partners, inverse, vectors, weights)
-    out, ig, *grads = finish(out, ig, sum1, sum2, last, fc1_weight.shape[1])
+    out, ig, *sums, last = block(inputs, cotangent, boxes.T, drops.T, partners, inverse, vectors, weights)
+    out, ig, *grads = finish(out, ig, sums, last, fc1_weight.shape[1])
     return (out.reshape(inputs.shape), ig.reshape(inputs.shape), *grads)
 
 

time: 140 us -> 124 us (0.89)
  Pallas kernels: 138 us -> 122 us
    pallas_call x1, Pallas kernels: 131 us -> 114 us  [block(): pl.pallas_call(functools.partial(block_kernel, shares, ahead, early), in_...]
where the time goes in v5:
time: 124 us; the launch traced here: 123 us
  Pallas kernels  122 us (98%)
  other arithmetic  1.28 us (1%)
    pallas_call x1, Pallas kernels, block(): pl.pallas_call(functools.partial(block_kernel, shares, ahead, early), in_...  114 us
    pallas_call x1, Pallas kernels, finish(): pl.pallas_call(finish_kernel, in_specs=[hbm] * 6 + [vmem], out_specs=[hbm...  7.1 us

profile of v5, /device:TPU:0, one launch (start us, length us, event | category | flops | bytes accessed | tf_op | source)
XLA Modules:
  0.0 123.5 jit_solution(4248075254374023258)
XLA Ops:
  0.6 0.7 and_select_fusion
  1.3 0.6 select_reduce_fusion.inverse_ref
  1.9 114.5 %shard_map.289 = (bf16[72,64,256]{2,1,0:T(8,128)(2,1)}, bf16[72,64,256]{2,1,0:T(8,128)(2,1)}, bf16[2,8,64,256]{3,2,1,0:T(8,128)(2,1)}, bf16[2,8,80,256]{3,2,1,0:...) custom-call(s32[4,72]{1,0:T(4,128)} %bitcast.16, ...), custom_call_target="tpu_custom_call" | custom-call | tf_op jit(solution)/shard_map/pallas_call | solution.py:816
  116.4 7.1 %shard_map.290 = (bf16[72,64,256]{2,1,0:T(8,128)(2,1)}, bf16[72,64,256]{2,1,0:T(8,128)(2,1)}, f32[256]{0:T(256)}, f32[256]{0:T(256)}, f32[256,768]{1,0:T(8,128)}...) custom-call(bf16[72,64,256]{2,1,0:T(8,128)(2,1)} %get-tuple-element., ...), custom_call_target="tpu_custom_call" | custom-call | tf_op jit(solution)/shard_map/pallas_call | solution.py:942

commit v6 on v5

--- a/solution.py
+++ b/solution.py
@@ -234,13 +234,18 @@
 
 
 class Reduce:
-    def __init__(self, group, me, mb, shares, stage, whole, r1, r2, r3, z, send_sem, recv_sem):
+    def __init__(self, group, paired, me, mb, shares, stage, whole, r1, r2, r3, z, send_sem, recv_sem):
         self.whole = whole
         self.group, self.me, self.mb, self.shares = group, me, mb, shares
         self.stage, self.r1, self.r2, self.r3, self.z = stage, r1, r2, r3, z
         self.send_sem, self.recv_sem = send_sem, recv_sem
         self.core = lax.rem(me, 2)
         self.batch = stage.shape[1]
+        self.paired = paired
+        self.side = lax.rem(mb, 2) if paired else 0
+        self.size = self.batch // 2 if paired else self.batch
+        self.spot = lax.div(mb, 2) if paired else mb
+        self.base = self.side * self.size
 
     def copy(self, slot, src, dst, device):
         return pltpu.make_async_remote_copy(
@@ -266,52 +271,104 @@
 
     def peers(self, body):
         def one(d, _):
-            body(d, lax.rem(self.mb + d, self.batch), lax.rem(self.mb + self.batch - d, self.batch))
+            body(d, lax.rem(self.spot + d, self.size), lax.rem(self.spot + self.size - d, self.size))
             return 0
 
-        lax.fori_loop(1, self.batch, one, 0)
+        lax.fori_loop(1, self.size, one, 0)
+
+    def device(self, spot):
+        return {"batch": 2 * spot + self.side if self.paired else spot}
 
     def scatter(self, d, to, far):
-        return self.copy(2 + d, self.stage.at[self.core, to], self.r2.at[far], {"batch": to})
+        return self.copy(2 + d, self.stage.at[self.core, self.base + to], self.r2.at[far], self.device(to))
 
     def gather(self, d, to, far):
-        return self.copy(1 + self.batch + d, self.whole.at[self.core, self.mb], self.whole.at[self.core, far], {"batch": to})
+        mine, theirs = self.base + self.spot, self.base + far
+        return self.copy(
+            1 + self.batch + d, self.whole.at[self.core, mine], self.whole.at[self.core, theirs], self.device(to)
+        )
+
+    def pair(self):
+        half, partner = self.size, {"batch": self.mb + 1 - 2 * self.side}
+        src = self.stage.at[self.core, pl.ds((1 - self.side) * half, half)]
+        return self.copy(1 + self.batch, src, self.r2.at[pl.ds(half, half)], partner)
+
+    def pair_back(self, arriving):
+        half, partner = self.size, {"batch": self.mb + 1 - 2 * self.side}
+        side = 1 - self.side if arriving else self.side
+        src = self.whole.at[self.core, pl.ds(self.base, half)]
+        return self.copy(2 * self.batch, src, self.whole.at[self.core, pl.ds(side * half, half)], partner)
+
+    def add(self, first, count, other, start):
+        def one(b, _):
+            total = self.stage[self.core, first + b].astype(F32) + other[start + b].astype(F32)
+            self.stage[self.core, first + b] = total.astype(BF)
+            return 0
+
+        lax.fori_loop(0, count, one, 0)
 
     def step(self, n):
-        core, mb = self.core, self.mb
-        if n == 0:
-            self.near().start()
-        if n == 1:
-            self.near().wait_recv()
-
-            def add(b, _):
-                self.stage[core, b] = (self.stage[core, b].astype(F32) + self.r1[b].astype(F32)).astype(BF)
-                return 0
-
-            lax.fori_loop(0, self.batch, add, 0)
-            self.peers(lambda d, to, far: self.scatter(d, to, mb).start())
-        if n == 2:
-            self.peers(lambda d, to, far: self.scatter(d, to, far).wait_recv())
-
-            def more(d, total):
-                return total + self.r2[lax.rem(mb + d, self.batch)].astype(F32)
-
-            self.z[...] = lax.fori_loop(1, self.batch, more, self.stage[core, mb].astype(F32)).astype(BF)
-            self.across().start()
-        if n == 3:
-            self.across().wait_recv()
-            self.whole[core, mb] = (self.z[...].astype(F32) + self.r3[...].astype(F32)).astype(BF)
-            self.peers(lambda d, to, far: self.gather(d, to, mb).start())
-        if n == 4:
-            self.peers(lambda d, to, far: self.gather(d, to, far).wait_recv())
+        steps = [self.begin, self.after_near]
+        if self.paired:
+            steps.append(self.after_pair)
+        steps += [self.after_scatter, self.after_across, self.after_gather]
+        if self.paired:
+            steps.append(self.after_pair_back)
+        steps.append(self.end)
+        steps[n]()
+
+    def begin(self):
+        self.near().start()
+
+    def after_near(self):
+        self.near().wait_recv()
+        self.add(0, self.batch, self.r1, 0)
+        if self.paired:
+            self.pair().start()
+        else:
+            self.peers(lambda d, to, far: self.scatter(d, to, self.spot).start())
+
+    def after_pair(self):
+        self.pair().wait_recv()
+        self.add(self.base, self.size, self.r2, self.size)
+        self.peers(lambda d, to, far: self.scatter(d, to, self.spot).start())
+
+    def after_scatter(self):
+        self.peers(lambda d, to, far: self.scatter(d, to, far).wait_recv())
+
+        def more(d, total):
+            return total + self.r2[lax.rem(self.spot + d, self.size)].astype(F32)
+
+        own = self.stage[self.core, self.base + self.spot].astype(F32)
+        self.z[...] = lax.fori_loop(1, self.size, more, own).astype(BF)
+        self.across().start()
+
+    def after_across(self):
+        self.across().wait_recv()
+        self.whole[self.core, self.base + self.spot] = (self.z[...].astype(F32) + self.r3[...].astype(F32)).astype(BF)
+        self.peers(lambda d, to, far: self.gather(d, to, self.spot).start())
+
+    def after_gather(self):
+        self.peers(lambda d, to, far: self.gather(d, to, far).wait_recv())
+        if self.paired:
+            self.pair_back(False).start()
+        else:
             self.back(False).start()
-        if n == 5:
-            self.back(True).wait_recv()
-            self.near().wait_send()
-            self.across().wait_send()
-            self.back(False).wait_send()
-            self.peers(lambda d, to, far: self.scatter(d, to, mb).wait_send())
-            self.peers(lambda d, to, far: self.gather(d, to, mb).wait_send())
+
+    def after_pair_back(self):
+        self.pair_back(True).wait_recv()
+        self.back(False).start()
+
+    def end(self):
+        self.back(True).wait_recv()
+        self.near().wait_send()
+        self.across().wait_send()
+        self.back(False).wait_send()
+        self.peers(lambda d, to, far: self.scatter(d, to, self.spot).wait_send())
+        self.peers(lambda d, to, far: self.gather(d, to, self.spot).wait_send())
+        if self.paired:
+            self.pair().wait_send()
+            self.pair_back(False).wait_send()
 
 
 class Tiny:
@@ -450,7 +507,7 @@
     mb = lax.axis_index("batch")
     batch = tiny_col.shape[0]
     sums = [
-        Reduce(n, me, mb, shares, spare[5 * n], wholes[n], *spare[5 * n + 1 : 5 * n + 5], sum_send, sum_recv)
+        Reduce(n, n < 2, me, mb, shares, spare[5 * n], wholes[n], *spare[5 * n + 1 : 5 * n + 5], sum_send, sum_recv)
         for n in range(n_sums)
     ]
     sum_a, sum_b, sum_c, sum_d = sums
@@ -753,17 +810,9 @@
     for load in late:
         load.wait()
     lax.fori_loop(0, chunks, forward, 0)
-    TALL_STEPS = ((0, sum_a, 1), (4, sum_b, 1), (5, sum_a, 2), (7, sum_a, 3))
-    FLAT_STEPS = (
-        (1, sum_c, 1),
-        (1, sum_b, 2),
-        (3, sum_b, 3),
-        (4, sum_a, 4),
-        (5, sum_c, 2),
-        (6, sum_a, 5),
-        (7, sum_c, 3),
-    )
-    NORM_STEPS = ((1, sum_d, 1), (6, sum_b, 4), (7, sum_c, 4), (8, sum_d, 2))
+    TALL_STEPS = ((0, sum_a, 1), (1, sum_b, 1), (3, sum_a, 2), (5, sum_b, 2), (7, sum_a, 3),)
+    FLAT_STEPS = ((0, sum_b, 3), (1, sum_c, 1), (1, sum_a, 4), (3, sum_b, 4), (4, sum_a, 5), (5, sum_c, 2), (6, sum_b, 5), (7, sum_c, 3), (7, sum_a, 6),)
+    NORM_STEPS = ((0, sum_a, 7), (1, sum_d, 1), (2, sum_b, 6), (5, sum_c, 4), (8, sum_d, 2),)
     pack_fc1()
     sum_a.step(0)
     pack_fc2()
@@ -777,7 +826,7 @@
     lax.fori_loop(0, chunks, norm_back, 0)
     rows = [jnp.sum(tiny[n], axis=0, keepdims=True) for n in range(2)] + [jnp.zeros((6, 256), F32)]
     few.start(0, jnp.concatenate(rows, axis=0))
-    sum_b.step(5)
+    sum_b.step(7)
     sum_c.step(5)
     half_way = 2 * chunks // 3
     lax.fori_loop(0, half_way, unmix, 0)

time: 124 us -> 123 us (level)
  no operation moved by 1% of the time
where the time goes in v6:
time: 123 us
  Pallas kernels  121 us (98%)
  other arithmetic  1.28 us (1%)
    pallas_call x1, Pallas kernels, block(): pl.pallas_call(functools.partial(block_kernel, shares, ahead, early), in_...  114 us
    pallas_call x1, Pallas kernels, finish(): pl.pallas_call(finish_kernel, in_specs=[hbm] * 6 + [vmem], out_specs=[hbm...  7.1 us

profile of v6, /device:TPU:0, one launch (start us, length us, event | category | flops | bytes accessed | tf_op | source)
XLA Modules:
  0.0 122.7 jit_solution(4502498435886925887)
XLA Ops:
  0.6 0.7 and_select_fusion
  1.3 0.6 select_reduce_fusion.inverse_ref
  1.9 113.7 %shard_map.289 = (bf16[72,64,256]{2,1,0:T(8,128)(2,1)}, bf16[72,64,256]{2,1,0:T(8,128)(2,1)}, bf16[2,8,64,256]{3,2,1,0:T(8,128)(2,1)}, bf16[2,8,80,256]{3,2,1,0:...) custom-call(s32[4,72]{1,0:T(4,128)} %bitcast.16, ...), custom_call_target="tpu_custom_call" | custom-call | tf_op jit(solution)/shard_map/pallas_call | solution.py:865
  115.6 7.1 %shard_map.290 = (bf16[72,64,256]{2,1,0:T(8,128)(2,1)}, bf16[72,64,256]{2,1,0:T(8,128)(2,1)}, f32[256]{0:T(256)}, f32[256]{0:T(256)}, f32[256,768]{1,0:T(8,128)}...) custom-call(bf16[72,64,256]{2,1,0:T(8,128)(2,1)} %get-tuple-element., ...), custom_call_target="tpu_custom_call" | custom-call | tf_op jit(solution)/shard_map/pallas_call | solution.py:991
